TPU v7x, 128 devices: a whole 4x4x4 slice. The times are simulated.
128 devices in a mesh: cand: 16 (over x, y), dom: 8 (over z, core).
Axes of the slice: x: 4, y: 4, z: 4, core: 2. Of those that a mesh axis runs over, the one named last changes fastest.
Arguments:
- strain_ops: bfloat16 [4, 6, 30, 131072], P(None, None, None, ('cand', 'dom')), may hold values from -0.109375 to 0.109375
- elem_scale: float32 [4, 131072], P(None, ('cand', 'dom')), may hold values from 0.5 to 2
- moduli: float32 [2, 131072], P(None, ('cand', 'dom')), may hold values from 0.5 to 2
- elem_block: int32 [131072, 1], P(('cand', 'dom')), may hold values from 0 to 127, as said below
- elem_slot: int32 [131072], P(('cand', 'dom')), may hold values from 0 to 11
- mass: float32 [8, 6144], P('dom', 'cand'), may hold values from 0.5 to 2
- updates: bfloat16 [8, 6144, 256], P('dom', 'cand'), may hold values from -6 to 6
Outputs:
- factor: float32 [8, 6144, 6144], P('dom', 'cand')
Inputs may be any that keep to these rules, and one draw needn't show every extreme that they name: `elem_block`: the elements of the device at index c of cand and d of dom, with i = c * 8 + d, go to the blocks i - o modulo 128 for o in 0, 1, 2, 3, 8, 9, 64 and 65. Of the 1024 elements of one device, at most 256 go to one block, and every device sends exactly 256 to one of its blocks.
All inputs are finite; a program needn't handle non-finite values.
Results may differ from a plain program's by a relative error of at most 0.0003.
Values may be sent and summed in bfloat16 or wider, within the bound.
No kernel may reach another device: no remote copies, remote signals or barrier semaphores. Data moves between devices by JAX's collectives and lax.ppermute only.
A program may use at most 192 MiB of HBM per device.

v0:
```python
import jax
import jax.numpy as jnp
from jax import lax
from jax.sharding import PartitionSpec as P

KSTEPS = 2


HIGHEST_PREC = lax.Precision.HIGHEST


def element_blocks(strain, scale, moduli):
    as_float = strain.astype(jnp.float32)
    weighted = as_float * (scale * moduli[0][None, :])[:, None, None, :]
    stiffness = jnp.einsum("qsie,qsje->ije", weighted, as_float, precision=HIGHEST_PREC)
    diverge = as_float[:, 0] + as_float[:, 1] + as_float[:, 2]
    stiffness = stiffness + jnp.einsum(
        "qie,qje->ije",
        diverge * (scale * moduli[1][None, :])[:, None, :],
        diverge,
        precision=HIGHEST_PREC,
    )
    padded = jnp.pad(stiffness, ((0, 2), (0, 2), (0, 0)))
    return padded.reshape(1024, stiffness.shape[2])


def solve_right(pivot_block, right_side):
    return lax.linalg.triangular_solve(
        pivot_block, right_side, left_side=False, lower=True, transpose_a=True
    )


def local(strain_ops, elem_scale, moduli, elem_block, elem_slot, mass, updates):
    block_width = mass.shape[1]
    slot_count = block_width // 32
    rank_cols = updates.shape[2]
    n_cand = lax.axis_size("cand")
    order_total = block_width * n_cand
    stiff_flat = element_blocks(strain_ops, elem_scale, moduli)
    flat_target = elem_block[:, 0] * slot_count + elem_slot
    wanted = jnp.arange(slot_count * lax.axis_size(("cand", "dom")), dtype=jnp.int32)
    chosen = (flat_target[:, None] == wanted[None, :]).astype(jnp.float32)
    tile_sums = lax.psum_scatter(
        lax.dot_general(chosen, stiff_flat, (((0,), (1,)), ((), ())), precision=HIGHEST_PREC),
        ("cand", "dom"),
        scatter_dimension=0,
        tiled=True,
    )
    tile_mats = tile_sums.reshape(slot_count, 32, 32)
    identity = jnp.eye(slot_count, dtype=jnp.float32)
    blockdiag = (identity[:, None, :, None] * tile_mats[:, :, None, :]).reshape(
        block_width, block_width
    )
    own_updates = updates[0]
    block_row = (
        lax.dot_general(
            own_updates,
            lax.all_gather(own_updates, "cand", axis=0, tiled=True),
            (((1,), (1,)), ((), ())),
            preferred_element_type=jnp.float32,
        )
        / rank_cols
    )
    cand_index = lax.axis_index("cand")
    zero_index = jnp.zeros((), jnp.int32)
    start_col = cand_index * block_width
    diag_now = lax.dynamic_slice(block_row, (zero_index, start_col), (block_width, block_width))
    diag_now = diag_now + blockdiag + jnp.diag(mass[0])
    block_row = lax.dynamic_update_slice(block_row, diag_now, (zero_index, start_col))
    block_of = jnp.arange(order_total, dtype=jnp.int32) // block_width
    for column_step in range(KSTEPS):
        col_start = column_step * block_width
        col_end = col_start + block_width
        current = block_row[:, col_start:col_end]
        col_panel = lax.all_gather(current, "cand", axis=0, tiled=True)
        pivot_block = jnp.linalg.cholesky(col_panel[col_start:col_end])
        solved = solve_right(pivot_block, col_panel)
        own_solved = lax.dynamic_slice_in_dim(solved, start_col, block_width, 0)
        change = lax.dot_general(
            own_solved, solved, (((1,), (1,)), ((), ())), precision=HIGHEST_PREC
        )
        later_cols = (block_of > column_step)[None, :]
        beyond = jnp.where(
            cand_index > column_step,
            block_row - change,
            jnp.where(cand_index == column_step, jnp.zeros_like(block_row), block_row),
        )
        block_row = jnp.where(later_cols, beyond, block_row)
        newcol = jnp.where(
            cand_index > column_step,
            own_solved,
            jnp.where(cand_index == column_step, pivot_block, current),
        )
        block_row = block_row.at[:, col_start:col_end].set(newcol)
    return block_row[None]


def solution(mesh):
    placed = (
        P(None, None, None, ("cand", "dom")),
        P(None, ("cand", "dom")),
        P(None, ("cand", "dom")),
        P(("cand", "dom"), None),
        P(("cand", "dom")),
        P("dom", "cand"),
        P("dom", "cand", None),
    )
    return jax.shard_map(
        local, mesh=mesh, in_specs=placed, out_specs=P("dom", "cand", None), check_vma=False
    )
```

profile of v0, /device:TPU:96, one launch (start us, length us, event | category | flops | bytes accessed | tf_op | source)
XLA Modules:
  0.0 1104.1 jit_solution(6346671628978281984)
XLA Ops:
  11.1 12.8 %copy.59 = bf16[4,6,30,1024]{2,1,0,3:T(8,128)(2,1)} copy(bf16[4,6,30,1024]{3,0,2,1:T(4,128)(2,1)S(1)} %copy-done.4) | data formatting | bytes 2949120 | tf_op args[0]
  31.1 14.7 %copy.58 = f32[4,6,30,1024]{2,1,0,3:T(8,128)} copy(f32[4,6,30,1024]{3,0,2,1:T(4,128)} %bitcast.117) | data formatting | bytes 5898240 | tf_op jit(solution)/shard_map/mul | solution.py:14
  45.9 30.4 %fusion.62 = f32[1024,30,30]{1,2,0:T(8,128)} fusion(f32[4,30,1024]{1,0,2:T(4,128)S(1)} %copy-done.5, f32[4,30,1024]{1,0,2:T(4,128)} %copy.61), kind=kOutput, calls=%fused_computation.138 | convolution fusion | flops 44236800 | bytes 4669440 | tf_op jit(solution)/shard_map/qie,qje->ije/dot_general | solution.py:17
  76.3 26.7 %bitcast_add_fusion = f32[30,30,1024]{1,0,2:T(8,128)} fusion(f32[1024,30,30]{1,2,0:T(8,128)} %fusion.62, f32[4,6,30,1024]{2,1,0,3:T(8,128)} %copy.58, bf16[4,6,30,1024]{2,1,0,3:T(8,128)(2,1)} %copy.59), kind=kOutput, calls=%fused_computation.4 | convolution fusion | flops 266342400 | bytes 11796480 | tf_op jit(solution)/shard_map/qsie,qsje->ije/dot_general | solution.py:15
  103.0 13.3 %copy.99 = f32[30,30,1024]{2,1,0:T(8,128)} copy(f32[30,30,1024]{1,0,2:T(8,128)} %bitcast_add_fusion) | data formatting | bytes 7372800
  118.9 14.1 %fusion.8 = f32[1536,1024]{1,0:T(8,128)} fusion(f32[1024,1024]{1,0:T(8,128)S(1)} %bitcast.118, s32[1024]{0:T(1024)S(1)} %add.69), kind=kOutput, calls=%fused_computation.22 | convolution fusion | flops 19330498560 | bytes 10489856 | tf_op jit(solution)/shard_map/dot_general | solution.py:44
  133.1 343.1 %fusion = f32[16,1024]{1,0:T(8,128)S(1)} fusion(f32[1536,1024]{1,0:T(8,128)} %fusion.8), kind=kCustom, calls=%all-reduce-scatter | all-reduce-scatter fusion | flops 2097153 | bytes 6356992
  485.3 20.9 %collective-permute-start.13 = (f32[16,1024]{1,0:T(8,128)S(1)}, f32[16,1024]{1,0:T(8,128)S(1)}, u32[]{:S(2)}, u32[]{:S(2)}) collective-permute-start(f32[16,1024]{1,0:T(8,128)S(1)} %fusion), channel_id=1, source_target_pairs={{0,14},{1,15},{2,16},{3,17},{4,18},{5,19},{6,20},{7,21},{8,22},{9,... | collective-permute-start | bytes 196616
  508.8 19.5 %collective-permute-start.16 = (f32[16,1024]{1,0:T(8,128)S(1)}, f32[16,1024]{1,0:T(8,128)S(1)}, u32[]{:S(2)}, u32[]{:S(2)}) collective-permute-start(f32[16,1024]{1,0:T(8,128)S(1)} %fusion), channel_id=1, source_target_pairs={{0,17},{1,18},{2,19},{3,20},{4,21},{5,22},{6,23},{7,24},{8,25},{9,... | collective-permute-start | bytes 196616
  587.0 13.7 %concatenate.18 = f32[524,1024]{1,0:T(8,128)S(1)} concatenate(f32[12,1024]{1,0:T(8,128)S(1)} %collective-permute-done.31, f32[16,1024]{1,0:T(8,128)} %copy-done.18, f32[16,1024]{1,0:T(8,128)} %copy-done.16, f32[16,1024]{1,0:T(8,128)} %copy-done.15, f32[16,1024]{1,0:T(8,128)} %copy-done.14, f32[16,1024]{1,0:T(8,128)} %copy-done.13, f32[16,1024]{1,0:T(8,128)S(1)} %collective-permute-done.25, ...), dimensions={0} | concatenate | bytes 4292608
  613.6 74.4 %all-gather.5.cloned.1.call-done = f32[6144,384]{0,1:T(8,128)} async-done(((f32[384,384]{0,1:T(8,128)}), f32[6144,384]{0,1:T(8,128)}) %all-gather.5.cloned.1.call-update) | async-done | bytes 9437200 | tf_op jit(solution)/shard_map/all_gather | solution.py:75
  690.5 11.7 %cholesky.208 = f32[128,128]{1,0:T(8,128)S(1)} custom-call(f32[128,128]{1,0:T(8,128)S(1)} %cholesky.310), custom_call_target="Cholesky" | custom-call | tf_op jit(solution)/shard_map/jit(cholesky)/cholesky | solution.py:76
  702.2 9.8 custom-call.20
  712.6 11.7 %cholesky.227 = f32[128,128]{1,0:T(8,128)S(1)} custom-call(f32[128,128]{1,0:T(8,128)S(1)} %cholesky.314), custom_call_target="Cholesky" | custom-call | tf_op jit(solution)/shard_map/jit(cholesky)/cholesky | solution.py:76
  724.7 10.0 custom-call.21
  735.5 11.7 %cholesky.246 = f32[128,128]{1,0:T(8,128)S(1)} custom-call(f32[128,128]{1,0:T(8,128)S(1)} %convolution_subtract_fusion.7), custom_call_target="Cholesky" | custom-call | tf_op jit(solution)/shard_map/jit(cholesky)/cholesky | solution.py:76
  757.9 29.9 %custom-call.22 = f32[3,128,128]{1,2,0:T(8,128)S(1)} custom-call(f32[3,128,128]{2,1,0:T(8,128)S(1)} %get-tuple-element.45), custom_call_target="InvertDiagBlocksLowerTriangular" | custom-call | tf_op jit(solution)/shard_map/triangular_solve/custom-call.2 | solution.py:28
  800.7 7.4 convolution_subtract_fusion.3
  812.7 7.5 pad_maximum_fusion
  820.2 21.9 %select_select_fusion.1 = f32[384,6144]{0,1:T(8,128)S(1)} fusion(f32[384,6144]{0,1:T(8,128)} %copy-done.1, f32[6144,384]{0,1:T(8,128)} %pad_maximum_fusion, pred[6144]{0:T(1024)(128)(4,1)S(1)} %broadcast_compare_fusion, pred[]{:T(512)S(6)} %eq.37, pred[]{:T(512)S(6)} %gt.27, s32[]{:T(128)S(6)} %select_n.90), kind=kOutput, calls=%fused_computation.8 | convolution fusion | flops 10881073152 | bytes 28907526 | tf_op jit(solution)/shard_map/dot_general | solution.py:79
  849.9 74.6 %all-gather.7.cloned.1.call-done = f32[6144,384]{0,1:T(8,128)} async-done(((f32[384,384]{0,1:T(8,128)}), f32[6144,384]{0,1:T(8,128)}) %all-gather.7.cloned.1.call-update) | async-done | bytes 9437200 | tf_op jit(solution)/shard_map/all_gather | solution.py:75
  926.9 11.7 %cholesky.261 = f32[128,128]{1,0:T(8,128)S(1)} custom-call(f32[128,128]{1,0:T(8,128)S(1)} %cholesky.318), custom_call_target="Cholesky" | custom-call | tf_op jit(solution)/shard_map/jit(cholesky)/cholesky | solution.py:76
  938.7 9.8 custom-call.23
  949.1 11.7 %cholesky.280 = f32[128,128]{1,0:T(8,128)S(1)} custom-call(f32[128,128]{1,0:T(8,128)S(1)} %cholesky.322), custom_call_target="Cholesky" | custom-call | tf_op jit(solution)/shard_map/jit(cholesky)/cholesky | solution.py:76
  961.1 10.2 custom-call.24
  972.1 11.7 %cholesky.299 = f32[128,128]{1,0:T(8,128)S(1)} custom-call(f32[128,128]{1,0:T(8,128)S(1)} %convolution_subtract_fusion.6), custom_call_target="Cholesky" | custom-call | tf_op jit(solution)/shard_map/jit(cholesky)/cholesky | solution.py:76
  987.8 6.4 while.7
  995.1 29.6 %custom-call.25 = f32[3,128,128]{1,2,0:T(8,128)S(1)} custom-call(f32[3,128,128]{2,1,0:T(8,128)S(1)} %get-tuple-element.46), custom_call_target="InvertDiagBlocksLowerTriangular" | custom-call | tf_op jit(solution)/shard_map/triangular_solve/custom-call.2 | solution.py:28
  1037.7 7.4 convolution_subtract_fusion.2
  1049.7 7.5 pad_maximum_fusion.1
  1057.2 24.1 %select_select_fusion = f32[384,6144]{0,1:T(8,128)S(1)} fusion(f32[384,6144]{0,1:T(8,128)} %copy-done, f32[6144,384]{0,1:T(8,128)} %pad_maximum_fusion.1, pred[6144]{0:T(1024)(128)(4,1)S(1)} %broadcast_compare_fusion.1, pred[]{:T(512)S(6)} %eq.38, pred[]{:T(512)S(6)} %gt.25, s32[]{:T(128)S(6)} %select_n.90), kind=kOutput, calls=%fused_computation.7 | convolution fusion | flops 10881073152 | bytes 28907526 | tf_op jit(solution)/shard_map/dot_general | solution.py:79
  1087.8 9.6 copy.85
  (247 shorter events, 178.8 us)
Async XLA Ops:
  6.5 597.6 %all-gather.9.cloned.1.call-start = ((), (), s32[]{:S(2)}) async-start(), calls=%async_computation.2 | async-start | bytes 3342336 | tf_op jit(solution)/shard_map/all_gather | solution.py:58
  7.3 680.8 %all-gather.5.cloned.1.call-start = ((), (), s32[]{:S(2)}) async-start(), calls=%async_computation | async-start | bytes 10027008 | tf_op jit(solution)/shard_map/all_gather | solution.py:75
  476.2 9.1 collective-permute-start
  479.4 26.8 %collective-permute-start.1 = (f32[16,1024]{1,0:T(8,128)S(1)}, f32[16,1024]{1,0:T(8,128)S(1)}, u32[]{:S(2)}, u32[]{:S(2)}) collective-permute-start(f32[16,1024]{1,0:T(8,128)S(1)} %fusion), channel_id=1, source_target_pairs={{0,2},{1,3},{2,4},{3,5},{4,6},{5,7},{6,8},{7,9},{8,10},{9,11},{10,... | collective-permute-start | bytes 196616
  481.3 26.2 %collective-permute-start.10 = (f32[16,1024]{1,0:T(8,128)S(1)}, f32[16,1024]{1,0:T(8,128)S(1)}, u32[]{:S(2)}, u32[]{:S(2)}) collective-permute-start(f32[16,1024]{1,0:T(8,128)S(1)} %fusion), channel_id=1, source_target_pairs={{0,11},{1,12},{2,13},{3,14},{4,15},{5,16},{6,17},{7,18},{8,19},{9,... | collective-permute-start | bytes 196616
  482.6 26.2 %collective-permute-start.11 = (f32[16,1024]{1,0:T(8,128)S(1)}, f32[16,1024]{1,0:T(8,128)S(1)}, u32[]{:S(2)}, u32[]{:S(2)}) collective-permute-start(f32[16,1024]{1,0:T(8,128)S(1)} %fusion), channel_id=1, source_target_pairs={{0,12},{1,13},{2,14},{3,15},{4,16},{5,17},{6,18},{7,19},{8,20},{9,... | collective-permute-start | bytes 196616
  484.0 44.4 %collective-permute-start.12 = (f32[16,1024]{1,0:T(8,128)S(1)}, f32[16,1024]{1,0:T(8,128)S(1)}, u32[]{:S(2)}, u32[]{:S(2)}) collective-permute-start(f32[16,1024]{1,0:T(8,128)S(1)} %fusion), channel_id=1, source_target_pairs={{0,13},{1,14},{2,15},{3,16},{4,17},{5,18},{6,19},{7,20},{8,21},{9,... | collective-permute-start | bytes 196616
  485.3 46.8 %collective-permute-start.13 = (f32[16,1024]{1,0:T(8,128)S(1)}, f32[16,1024]{1,0:T(8,128)S(1)}, u32[]{:S(2)}, u32[]{:S(2)}) collective-permute-start(f32[16,1024]{1,0:T(8,128)S(1)} %fusion), channel_id=1, source_target_pairs={{0,14},{1,15},{2,16},{3,17},{4,18},{5,19},{6,20},{7,21},{8,22},{9,... | collective-permute-start | bytes 196616
  506.2 30.5 %collective-permute-start.14 = (f32[16,1024]{1,0:T(8,128)S(1)}, f32[16,1024]{1,0:T(8,128)S(1)}, u32[]{:S(2)}, u32[]{:S(2)}) collective-permute-start(f32[16,1024]{1,0:T(8,128)S(1)} %fusion), channel_id=1, source_target_pairs={{0,15},{1,16},{2,17},{3,18},{4,19},{5,20},{6,21},{7,22},{8,23},{9,... | collective-permute-start | bytes 196616
  507.5 31.4 %collective-permute-start.15 = (f32[16,1024]{1,0:T(8,128)S(1)}, f32[16,1024]{1,0:T(8,128)S(1)}, u32[]{:S(2)}, u32[]{:S(2)}) collective-permute-start(f32[16,1024]{1,0:T(8,128)S(1)} %fusion), channel_id=1, source_target_pairs={{0,16},{1,17},{2,18},{3,19},{4,20},{5,21},{6,22},{7,23},{8,24},{9,... | collective-permute-start | bytes 196616
  508.8 32.0 %collective-permute-start.16 = (f32[16,1024]{1,0:T(8,128)S(1)}, f32[16,1024]{1,0:T(8,128)S(1)}, u32[]{:S(2)}, u32[]{:S(2)}) collective-permute-start(f32[16,1024]{1,0:T(8,128)S(1)} %fusion), channel_id=1, source_target_pairs={{0,17},{1,18},{2,19},{3,20},{4,21},{5,22},{6,23},{7,24},{8,25},{9,... | collective-permute-start | bytes 196616
  528.4 14.4 %collective-permute-start.17 = (f32[16,1024]{1,0:T(8,128)S(1)}, f32[16,1024]{1,0:T(8,128)S(1)}, u32[]{:S(2)}, u32[]{:S(2)}) collective-permute-start(f32[16,1024]{1,0:T(8,128)S(1)} %fusion), channel_id=1, source_target_pairs={{0,18},{1,19},{2,20},{3,21},{4,22},{5,23},{6,24},{7,25},{8,26},{9,... | collective-permute-start | bytes 196616
  532.1 12.6 %collective-permute-start.18 = (f32[16,1024]{1,0:T(8,128)S(1)}, f32[16,1024]{1,0:T(8,128)S(1)}, u32[]{:S(2)}, u32[]{:S(2)}) collective-permute-start(f32[16,1024]{1,0:T(8,128)S(1)} %fusion), channel_id=1, source_target_pairs={{0,19},{1,20},{2,21},{3,22},{4,23},{5,24},{6,25},{7,26},{8,27},{9,... | collective-permute-start | bytes 196616
  536.7 12.1 %collective-permute-start.19 = (f32[16,1024]{1,0:T(8,128)S(1)}, f32[16,1024]{1,0:T(8,128)S(1)}, u32[]{:S(2)}, u32[]{:S(2)}) collective-permute-start(f32[16,1024]{1,0:T(8,128)S(1)} %fusion), channel_id=1, source_target_pairs={{0,20},{1,21},{2,22},{3,23},{4,24},{5,25},{6,26},{7,27},{8,28},{9,... | collective-permute-start | bytes 196616
  538.9 11.2 %collective-permute-start.2 = (f32[16,1024]{1,0:T(8,128)S(1)}, f32[16,1024]{1,0:T(8,128)S(1)}, u32[]{:S(2)}, u32[]{:S(2)}) collective-permute-start(f32[16,1024]{1,0:T(8,128)S(1)} %fusion), channel_id=1, source_target_pairs={{0,3},{1,4},{2,5},{3,6},{4,7},{5,8},{6,9},{7,10},{8,11},{9,12},{10... | collective-permute-start | bytes 196616
  540.8 10.6 collective-permute-start.20
  542.7 10.9 collective-permute-start.21
  544.7 10.3 collective-permute-start.22
  548.8 8.8 collective-permute-start.23
  550.1 8.7 collective-permute-start.24
  551.5 8.7 collective-permute-start.25
  553.7 11.2 %collective-permute-start.26 = (f32[16,1024]{1,0:T(8,128)S(1)}, f32[16,1024]{1,0:T(8,128)S(1)}, u32[]{:S(2)}, u32[]{:S(2)}) collective-permute-start(f32[16,1024]{1,0:T(8,128)S(1)} %fusion), channel_id=1, source_target_pairs={{0,27},{1,28},{2,29},{3,30},{4,31},{5,32},{6,33},{7,34},{8,35},{9,... | collective-permute-start | bytes 196616
  555.0 11.1 %collective-permute-start.27 = (f32[16,1024]{1,0:T(8,128)S(1)}, f32[16,1024]{1,0:T(8,128)S(1)}, u32[]{:S(2)}, u32[]{:S(2)}) collective-permute-start(f32[16,1024]{1,0:T(8,128)S(1)} %fusion), channel_id=1, source_target_pairs={{0,28},{1,29},{2,30},{3,31},{4,32},{5,33},{6,34},{7,35},{8,36},{9,... | collective-permute-start | bytes 196616
  557.5 11.8 %collective-permute-start.28 = (f32[16,1024]{1,0:T(8,128)S(1)}, f32[16,1024]{1,0:T(8,128)S(1)}, u32[]{:S(2)}, u32[]{:S(2)}) collective-permute-start(f32[16,1024]{1,0:T(8,128)S(1)} %fusion), channel_id=1, source_target_pairs={{0,29},{1,30},{2,31},{3,32},{4,33},{5,34},{6,35},{7,36},{8,37},{9,... | collective-permute-start | bytes 196616
  558.8 13.0 %collective-permute-start.29 = (f32[16,1024]{1,0:T(8,128)S(1)}, f32[16,1024]{1,0:T(8,128)S(1)}, u32[]{:S(2)}, u32[]{:S(2)}) collective-permute-start(f32[16,1024]{1,0:T(8,128)S(1)} %fusion), channel_id=1, source_target_pairs={{0,30},{1,31},{2,32},{3,33},{4,34},{5,35},{6,36},{7,37},{8,38},{9,... | collective-permute-start | bytes 196616
  560.2 13.2 %collective-permute-start.3 = (f32[16,1024]{1,0:T(8,128)S(1)}, f32[16,1024]{1,0:T(8,128)S(1)}, u32[]{:S(2)}, u32[]{:S(2)}) collective-permute-start(f32[16,1024]{1,0:T(8,128)S(1)} %fusion), channel_id=1, source_target_pairs={{0,4},{1,5},{2,6},{3,7},{4,8},{5,9},{6,10},{7,11},{8,12},{9,13},{1... | collective-permute-start | bytes 196616
  564.8 13.2 %collective-permute-start.30 = (f32[16,1024]{1,0:T(8,128)S(1)}, f32[16,1024]{1,0:T(8,128)S(1)}, u32[]{:S(2)}, u32[]{:S(2)}) collective-permute-start(f32[16,1024]{1,0:T(8,128)S(1)} %fusion), channel_id=1, source_target_pairs={{0,31},{1,32},{2,33},{3,34},{4,35},{5,36},{6,37},{7,38},{8,39},{9,... | collective-permute-start | bytes 196616
  566.2 13.4 %collective-permute-start.4 = (f32[16,1024]{1,0:T(8,128)S(1)}, f32[16,1024]{1,0:T(8,128)S(1)}, u32[]{:S(2)}, u32[]{:S(2)}) collective-permute-start(f32[16,1024]{1,0:T(8,128)S(1)} %fusion), channel_id=1, source_target_pairs={{0,5},{1,6},{2,7},{3,8},{4,9},{5,10},{6,11},{7,12},{8,13},{9,14},{... | collective-permute-start | bytes 196616
  569.4 16.3 %collective-permute-start.5 = (f32[16,1024]{1,0:T(8,128)S(1)}, f32[16,1024]{1,0:T(8,128)S(1)}, u32[]{:S(2)}, u32[]{:S(2)}) collective-permute-start(f32[16,1024]{1,0:T(8,128)S(1)} %fusion), channel_id=1, source_target_pairs={{0,6},{1,7},{2,8},{3,9},{4,10},{5,11},{6,12},{7,13},{8,14},{9,15},... | collective-permute-start | bytes 196616
  571.9 13.8 %collective-permute-start.6 = (f32[16,1024]{1,0:T(8,128)S(1)}, f32[16,1024]{1,0:T(8,128)S(1)}, u32[]{:S(2)}, u32[]{:S(2)}) collective-permute-start(f32[16,1024]{1,0:T(8,128)S(1)} %fusion), channel_id=1, source_target_pairs={{0,7},{1,8},{2,9},{3,10},{4,11},{5,12},{6,13},{7,14},{8,15},{9,16}... | collective-permute-start | bytes 196616
  573.4 12.3 %collective-permute-start.7 = (f32[16,1024]{1,0:T(8,128)S(1)}, f32[16,1024]{1,0:T(8,128)S(1)}, u32[]{:S(2)}, u32[]{:S(2)}) collective-permute-start(f32[16,1024]{1,0:T(8,128)S(1)} %fusion), channel_id=1, source_target_pairs={{0,8},{1,9},{2,10},{3,11},{4,12},{5,13},{6,14},{7,15},{8,16},{9,17... | collective-permute-start | bytes 196616
  612.7 311.8 %all-gather.7.cloned.1.call-start = ((), (), s32[]{:S(2)}) async-start(), calls=%async_computation.1 | async-start | bytes 10027008 | tf_op jit(solution)/shard_map/all_gather | solution.py:75
  (32 other events, 628.3 us)
Sparse Core Ops, SparseCore 0:
  9.5 49.0 all-gather.8
  612.8 75.1 all-gather.4
  849.0 75.3 all-gather.6
where the time goes:
time: 1110 us; the launch traced here: 1100 us
  blocking collectives  343 us (31%)
  other arithmetic  205 us (18%)
  matrix products  173 us (16%)
  waiting for transfers between devices  150 us (14%)
  starting transfers between devices  109 us (10%)
  local copies, waits for them, and re-layouts  105 us (9%)
  between operations  18.4 us (2%)
    unnamed x1, blocking collectives  343 us
    all_gather x2, waiting for transfers between devices, local(): col_panel = lax.all_gather(current, 'cand', axis=0, tiled=True)  149 us
    another operation x21, other arithmetic, local(): pivot_block = jnp.linalg.cholesky(col_panel[col_start:col_end])  114 us
    unnamed x32, starting transfers between devices  109 us
    another operation x7, other arithmetic, solve_right(): lax.linalg.triangular_solve(pivot_block, right_side, left_side=False, low...  74.6 us
    unnamed x65, local copies, waits for them, and re-layouts  53.9 us
    another operation x10, matrix products, solve_right(): lax.linalg.triangular_solve(pivot_block, right_side, left_side=False, low...  49.7 us
    dot_general x2, matrix products, local(): lax.dot_general(own_solved, solved, (((1,), (1,)), ((), ())), precision=H...  46 us
  transfers between devices with their start and end apart: 35, of which 2 were waited for; matrix products, arithmetic and copies ran while one was open for 44% of the time, Pallas kernels for 0%

commit v1 on v0

v1 whole, which is shorter than its diff:
```python
import jax
import jax.numpy as jnp
from jax import lax
from jax.experimental import pallas as pl
from jax.experimental.pallas import tpu as pltpu
from jax.sharding import PartitionSpec as P

F32 = jnp.float32
BF16 = jnp.bfloat16
W = 384
WINDOW = 768
RANK = 256
SLOTS = 12
TILE = 1024
CHUNK = 256
SHIFTS = (0, 1, 3, 2)
BINS = {0: 0, 8: 12, 64: 24, 1: 40, 9: 52, 65: 64, 2: 80, 3: 96}
BIN_ROWS = 112


def split3(x):
    a = x.astype(BF16); r = x - a.astype(F32)
    b = r.astype(BF16); c = (r - b.astype(F32)).astype(BF16)
    return a, b, c


def dot_nn(a, b): return lax.dot_general(a, b, (((1,), (0,)), ((), ())), preferred_element_type=F32)
def dot_nt(a, b): return lax.dot_general(a, b, (((1,), (1,)), ((), ())), preferred_element_type=F32)


def product_tn(x, y):
    xt = x.T
    x1, x2, x3 = split3(xt)
    y1, y2, y3 = split3(y)
    left = jnp.concatenate([x1, x1, x2, x1, x2, x3], axis=1)
    right = jnp.concatenate([y1, y2, y1, y3, y2, y1], axis=0)
    return dot_nn(left, right)


def eliminate(rows, first):
    sub = lax.broadcasted_iota(jnp.int32, (8, 128), 0)
    n = len(rows)
    for t in range(n):
        c0 = first + 8 * t
        cols = {q: [jnp.broadcast_to(rows[q][0][:, c0 + k:c0 + k + 1], (8, 128)) for k in range(8)] for q in range(t, n)}
        for k in range(8):
            pivot = jnp.broadcast_to(cols[t][k][k:k + 1, :], (8, 128))
            rs = lax.rsqrt(pivot)
            f = {q: cols[q][k] * rs for q in range(t, n)}
            for m in range(k + 1, 8):
                sm = jnp.broadcast_to(f[t][m:m + 1, :], (8, 128))
                for q in range(t, n):
                    cols[q][m] = cols[q][m] - f[q] * sm
            fm = jnp.where(sub > k, f[t], 0.0)
            for h in range(len(rows[t])):
                r = jnp.broadcast_to(rows[t][h][k:k + 1, :], (8, 128)) * rs
                rows[t][h] = jnp.where(sub == k, r, rows[t][h] - fm * r)
                for q in range(t + 1, n):
                    rows[q][h] = rows[q][h] - f[q] * r
    return rows


def unpack_tiles(packed, out_ref):
    n = packed.shape[0]
    lane = lax.broadcasted_iota(jnp.int32, (n, 128), 1) // 32
    tile = lax.broadcasted_iota(jnp.int32, (n, 128), 0) % 4
    for g in range(8):
        x = packed[:, 128 * g:128 * g + 128]
        turned = [x] + [pltpu.roll(x, 32 * r, 1) for r in range(1, 4)]
        for u in range(4):
            row = jnp.zeros((n, 128), F32)
            for v in range(4):
                row = jnp.where((lane == v) & (tile == v), turned[(v - u) % 4], row)
            out_ref[pl.ds(4 * g + u, n, stride=32), :] = row


def stiffness_kernel(strain, scale, moduli, bins, mass, keep, far, two, three, plain, weighted, high, low, total):
    step = pl.program_id(0)

    @pl.when(step == 0)
    def _():
        plain[...] = jnp.zeros_like(plain)
        weighted[...] = jnp.zeros_like(weighted)
        high[...] = jnp.zeros_like(high)
        low[...] = jnp.zeros_like(low)
        total[...] = jnp.zeros_like(total)
        lane = lax.broadcasted_iota(jnp.int32, (SLOTS, TILE), 1)
        spread = jnp.concatenate([mass[...]] * 32, axis=1)
        total[:SLOTS, :] = jnp.where(lane // 32 == lane % 32, spread, 0.0)

    for part in range(CHUNK // 128):
        at = slice(128 * part, 128 * part + 128)
        for q in range(4):
            weight = scale[q:q + 1, at]
            shear = weight * moduli[0:1, at]
            bulk = weight * moduli[1:2, at]
            diverge = None
            for s in range(6):
                b = strain[q, s, :, at].astype(F32)
                plain[7 * q + s, :30, :] = b
                weighted[7 * q + s, :30, :] = b * shear
                if s < 3:
                    diverge = b if s == 0 else diverge + b
            plain[7 * q + 6, :30, :] = diverge
            weighted[7 * q + 6, :30, :] = diverge * bulk
        for a in range(4):
            rows = range(8 * a, min(8 * a + 8, 30))
            sums = {}
            for n in range(28):
                right = weighted[n, 8 * a:, :]
                for i in rows:
                    term = plain[n, i:i + 1, :] * right
                    sums[i] = term if n == 0 else sums[i] + term
            for i in rows:
                k = sums[i]
                if a:
                    k = jnp.concatenate([jnp.zeros((8 * a, 128), F32), k], axis=0)
                top = k.astype(BF16)
                high[32 * i:32 * i + 32, at] = top
                low[32 * i:32 * i + 32, at] = (k - top.astype(F32)).astype(BF16)
    chosen = lax.broadcasted_iota(jnp.int32, (BIN_ROWS, CHUNK), 0) == bins[...]
    chosen = chosen.astype(F32).astype(BF16)
    total[...] += dot_nt(chosen, high[...]) + dot_nt(chosen, low[...])

    @pl.when(step == pl.num_programs(0) - 1)
    def _():
        keep[...] = total[0:40, :]
        far[...] = total[40:80, :]
        two[...] = total[80:96, :]
        three[...] = total[96:112, :]


def stiffness_tiles(strain, scale, moduli, bins, mass):
    steps = strain.shape[3] // CHUNK
    whole = lambda rows: pl.BlockSpec((rows, TILE), lambda i: (0, 0))
    return pl.pallas_call(
        stiffness_kernel,
        grid=(steps,),
        in_specs=[
            pl.BlockSpec((4, 6, 30, CHUNK), lambda i: (0, 0, 0, i)),
            pl.BlockSpec((4, CHUNK), lambda i: (0, i)),
            pl.BlockSpec((2, CHUNK), lambda i: (0, i)),
            pl.BlockSpec((1, CHUNK), lambda i: (0, i)),
            pl.BlockSpec((SLOTS, 32), lambda i: (0, 0)),
        ],
        out_specs=[whole(40), whole(40), whole(16), whole(16)],
        out_shape=[jax.ShapeDtypeStruct((r, TILE), F32) for r in (40, 40, 16, 16)],
        scratch_shapes=[
            pltpu.VMEM((28, 32, 128), F32),
            pltpu.VMEM((28, 32, 128), F32),
            pltpu.VMEM((TILE, CHUNK), BF16),
            pltpu.VMEM((TILE, CHUNK), BF16),
            pltpu.VMEM((BIN_ROWS, TILE), F32),
        ],
        compiler_params=pltpu.CompilerParams(vmem_limit_bytes=32 * 2**20),
        name="stiffness_tiles",
    )(strain, scale, moduli, bins, mass)


def mirror(block):
    row = lax.broadcasted_iota(jnp.int32, block.shape, 0) // 8
    col = lax.broadcasted_iota(jnp.int32, block.shape, 1) // 8
    return jnp.where(row <= col, block, block.T)


def factor_window(diag, v_ref, h_ref, m_ref, work):
    square = lambda n, dim: lax.broadcasted_iota(jnp.int32, (n, n), dim)
    m_ref[...] = (square(256, 0) == square(256, 1)).astype(F32)
    upper = square(128, 0) <= square(128, 1)

    def block(j, carry):
        at = pl.ds(pl.multiple_of(j * 128, 128), 128)
        v = v_ref[at, :]
        m1, m2, m3 = split3(m_ref[...])
        p = dot_nn(v, m1) + (dot_nn(v, m2) + dot_nn(v, m3))
        p1, p2, p3 = split3(p)
        work[:, :128] = mirror(diag[at, :]) + (dot_nt(p1, v) + (dot_nt(p2, v) + dot_nt(p3, v)))
        work[:, 128:] = p
        for s in range(4):
            at_row = lambda q: slice(32 * s + 8 * q, 32 * s + 8 * q + 8)
            rows = [[work[at_row(q), 128 * h:128 * h + 128] for h in range(3)] for q in range(4)]
            rows = eliminate(rows, 32 * s)
            for q in range(4):
                for h in range(3):
                    work[at_row(q), 128 * h:128 * h + 128] = rows[q][h]
            if s < 3:
                done = work[32 * s:32 * s + 32, :]
                change = product_tn(done[:, :128], done)
                work[32 * s + 32:, :] = work[32 * s + 32:, :] - change[32 * s + 32:, :]
        h = work[:, 128:]
        h_ref[at, :] = h
        diag[at, :] = jnp.where(upper, work[:, :128], 0.0).T
        m_ref[...] = m_ref[...] - product_tn(h, h)
        return carry

    lax.fori_loop(0, WINDOW // 128, block, 0)


def kept_at(shift):
    return jnp.where(shift == 3, 2, jnp.where(shift == 2, 3, shift))


def factor_kernel(place, lead, own_tiles, own, *refs):
    left, right = refs[0:4], refs[4:8]
    out = refs[8]
    diag, own_diag, v_ref, h_ref, m_ref, work, panel, blocks, sems = refs[9:]
    x, y = place[0], place[1]
    cand = 4 * x + y

    unpack_tiles(lead[...], diag)
    unpack_tiles(own_tiles[...], own_diag)
    kept_x = kept_at(x)
    for b in range(2):
        shift_y = lax.rem(y - b + 4, 4)
        kept_y = kept_at(shift_y)
        for n, shift in enumerate(SHIFTS):
            @pl.when(shift_y == shift)
            def _():
                v_ref[W * b:W * b + W, :128] = left[n][kept_x] * 0.0625

            @pl.when(x == shift)
            def _():
                v_ref[W * b:W * b + W, 128:] = right[n][kept_y] * 0.0625
    factor_window(diag, v_ref, h_ref, m_ref, work)

    v_own = own[...] * 0.0625
    m1, m2, m3 = split3(m_ref[...])
    q = (dot_nn(v_own, m1) + (dot_nn(v_own, m2) + dot_nn(v_own, m3))) * 0.0625
    q1 = q.astype(BF16)
    q2 = (q - q1.astype(F32)).astype(BF16)
    h = h_ref[...]
    h1 = h.astype(BF16)
    h2 = (h - h1.astype(F32)).astype(BF16)
    panel[...] = dot_nt(v_own, h1) + dot_nt(v_own, h2)

    @pl.when(cand < 2)
    def _():
        row = lax.broadcasted_iota(jnp.int32, (W, WINDOW), 0) // 128 + 3 * cand
        col = lax.broadcasted_iota(jnp.int32, (W, WINDOW), 1) // 128
        panel[...] = jnp.where(row > col, panel[...], 0.0)
        for a in range(3):
            rows = pl.ds(pl.multiple_of(W * cand + 128 * a, 128), 128)
            panel[128 * a:128 * a + 128, rows] = diag[rows, :]

    lead_copy = pltpu.make_async_copy(panel, out.at[0, :, pl.ds(0, WINDOW)], sems.at[16])
    lead_copy.start()

    copies = []
    for n, shift_y in enumerate(SHIFTS):
        for m, shift_x in enumerate(SHIFTS):
            column = 4 * lax.rem(x - shift_x + 4, 4) + lax.rem(y - shift_y + 4, 4)
            slot = 4 * n + m
            copy = pltpu.make_async_copy(
                blocks.at[slot],
                out.at[0, :, pl.ds(pl.multiple_of(column * W, 128), W)],
                sems.at[slot],
            )
            copies.append((column, copy))

            @pl.when(column >= 2)
            def _():
                @pl.when(cand < 2)
                def _():
                    blocks[slot] = jnp.zeros((W, W), F32)

                @pl.when(cand >= 2)
                def _():
                    v = jnp.concatenate([left[n][m], right[m][n]], axis=1)
                    blocks[slot] = dot_nt(q1, v) + dot_nt(q2, v)
                    if slot == 0:
                        for a in range(3):
                            at = slice(128 * a, 128 * a + 128)
                            blocks[slot, at, at] += mirror(own_diag[at, :])

                copy.start()
    lead_copy.wait()
    for column, copy in copies:
        @pl.when(column >= 2)
        def _():
            copy.wait()


def factor_rows(place, lead, own_tiles, own, left, right):
    vmem = pl.BlockSpec(memory_space=pltpu.VMEM)
    return pl.pallas_call(
        factor_kernel,
        in_specs=[pl.BlockSpec(memory_space=pltpu.SMEM)] + [vmem] * 11,
        out_specs=pl.BlockSpec(memory_space=pl.ANY),
        out_shape=jax.ShapeDtypeStruct((1, W, 16 * W), F32),
        scratch_shapes=[
            pltpu.VMEM((WINDOW, 128), F32),
            pltpu.VMEM((W, 128), F32),
            pltpu.VMEM((WINDOW, RANK), BF16),
            pltpu.VMEM((WINDOW, RANK), F32),
            pltpu.VMEM((RANK, RANK), F32),
            pltpu.VMEM((128, 128 + RANK), F32),
            pltpu.VMEM((W, WINDOW), F32),
            pltpu.VMEM((16, W, W), F32),
            pltpu.SemaphoreType.DMA((17,)),
        ],
        compiler_params=pltpu.CompilerParams(vmem_limit_bytes=40 * 2**20),
        name="factor_rows",
    )(place, lead, own_tiles, own, *left, *right)


def move_x(value, shift):
    return lax.ppermute(value, "cand", [(4 * x + y, (x + shift) % 4 * 4 + y) for x in range(4) for y in range(4)])


def move_y(value, shift):
    return lax.ppermute(value, "cand", [(4 * x + y, 4 * x + (y + shift) % 4) for x in range(4) for y in range(4)])


def move_back(value, offset):
    return lax.ppermute(value, ("cand", "dom"), [(i, (i - offset) % 128) for i in range(128)])


def local(strain_ops, elem_scale, moduli, elem_block, elem_slot, mass, updates):
    cand = lax.axis_index("cand")
    device = cand * lax.axis_size("dom") + lax.axis_index("dom")
    own = updates[0]

    left = jnp.stack([own[:, :128]] + [move_x(own[:, :128], s) for s in SHIFTS[1:]])
    right = jnp.stack([own[:, 128:]] + [move_y(own[:, 128:], s) for s in SHIFTS[1:]])
    left = [left] + [move_y(left, s) for s in SHIFTS[1:]]
    right = [right] + [move_x(right, s) for s in SHIFTS[1:]]

    offset = (device - elem_block[:, 0]) & 127
    first = jnp.zeros_like(offset)
    for o, start in BINS.items():
        first = jnp.where(offset == o, start, first)
    bins = (first + elem_slot)[None, :]
    keep, far, two, three = stiffness_tiles(strain_ops, elem_scale, moduli, bins, mass.reshape(SLOTS, 32))

    far = move_back(far, 1)
    two = move_back(two, 2)
    three = move_back(three, 3)
    here = keep[:12] + far[:12] + two[:12] + three[:12]
    near = keep[12:24] + far[12:24]
    half = keep[24:36] + far[24:36]
    zero = jnp.zeros_like(here)
    pick = lambda c: jnp.where(cand == c, here, jnp.where(cand == c + 1, near, jnp.where(cand == c + 8, half, zero)))
    lead = jnp.concatenate([pick(0), pick(1)], axis=0)
    for bit in (1, 2, 4, 8):
        lead = lead + lax.ppermute(lead, "cand", [(i, i ^ bit) for i in range(16)])
    own_tiles = here + move_back(near, 8) + move_back(half, 64)
    place = jnp.stack([cand // 4, cand % 4]).astype(jnp.int32)
    return factor_rows(place, lead, own_tiles, own, left, right)


def solution(mesh):
    placed = (
        P(None, None, None, ("cand", "dom")),
        P(None, ("cand", "dom")),
        P(None, ("cand", "dom")),
        P(("cand", "dom"), None),
        P(("cand", "dom")),
        P("dom", "cand"),
        P("dom", "cand", None),
    )
    return jax.shard_map(
        local, mesh=mesh, in_specs=placed, out_specs=P("dom", "cand", None), check_vma=False
    )
```

time: 1110 us -> 120 us (0.11)
  blocking collectives: 343 us -> 0 us
  other arithmetic: 205 us -> 1.96 us
  matrix products: 173 us -> 0 us
  waiting for transfers between devices: 150 us -> 33.2 us
  local copies, waits for them, and re-layouts: 105 us -> 1.97 us
  starting transfers between devices: 109 us -> 35.3 us
  Pallas kernels: 0 us -> 45 us
  between operations: 18.4 us -> 0.36 us
    unnamed x1 -> x0, blocking collectives: 343 us -> none
    another operation x30 -> x3, other arithmetic: 190 us -> 0.18 us  [the longest x1 0.07 us: local(): place = jnp.stack([cand // 4, cand % 4]).astype(jnp.int32)]
    all_gather x3 -> x0, waiting for transfers between devices: 149 us -> none  [the longest x2 149 us: local(): col_panel = lax.all_gather(current, 'cand', axis=0, tiled=True)]
    dot_general x6 -> x0, matrix products: 121 us -> none  [the longest x2 46 us: local(): lax.dot_general(own_solved, solved, (((1,), (1,)), ((), ())), precision=H...]
    unnamed x32 -> x0, starting transfers between devices: 109 us -> none
    another operation x18 -> x0, matrix products: 52.1 us -> none  [the longest x10 49.7 us: solve_right(): lax.linalg.triangular_solve(pivot_block, right_side, left_side=False, low...]
    unnamed x65 -> x11, local copies, waits for them, and re-layouts: 53.9 us -> 1.84 us
    pallas_call x0 -> x2, Pallas kernels: none -> 45 us  [the longest x1 34 us: factor_rows(): pl.pallas_call(factor_kernel, in_specs=[pl.BlockSpec(memory_space=pltpu.S...]
  transfers between devices with their start and end apart: 35 -> 21, of which waited for: 2 -> 10; matrix products, arithmetic and copies ran while one was open for 44% -> 1% of each run, Pallas kernels for 0% -> 0%
where the time goes in v1:
time: 120 us; the launch traced here: 118 us
  Pallas kernels  45 us (38%)
  starting transfers between devices  35.3 us (29%)
  waiting for transfers between devices  33.2 us (28%)
  local copies, waits for them, and re-layouts  1.97 us (2%)
  other arithmetic  1.96 us (2%)
    pallas_call x1, Pallas kernels, factor_rows(): pl.pallas_call(factor_kernel, in_specs=[pl.BlockSpec(memory_space=pltpu.S...  34 us
    ppermute x6, waiting for transfers between devices, move_x(): lax.ppermute(value, 'cand', [(4 * x + y, (x + shift) % 4 * 4 + y) for x i...  15.5 us
    ppermute x6, starting transfers between devices, move_y(): lax.ppermute(value, 'cand', [(4 * x + y, 4 * x + (y + shift) % 4) for x i...  14.2 us
    pallas_call x1, Pallas kernels, stiffness_tiles(): pl.pallas_call(stiffness_kernel, grid=(steps,), in_specs=[pl.BlockSpec((4...  11 us
    ppermute x4, waiting for transfers between devices, local(): lead = lead + lax.ppermute(lead, 'cand', [(i, i ^ bit) for i in range(16)])  10.1 us
    ppermute x6, starting transfers between devices, move_x(): lax.ppermute(value, 'cand', [(4 * x + y, (x + shift) % 4 * 4 + y) for x i...  7.83 us
    ppermute x5, starting transfers between devices, move_back(): lax.ppermute(value, ('cand', 'dom'), [(i, (i - offset) % 128) for i in ra...  6.81 us
    ppermute x4, starting transfers between devices, local(): lead = lead + lax.ppermute(lead, 'cand', [(i, i ^ bit) for i in range(16)])  6.44 us
  transfers between devices with their start and end apart: 21, of which 10 were waited for; matrix products, arithmetic and copies ran while one was open for 1% of the time, Pallas kernels for 0%

profile of v1, /device:TPU:96, one launch (start us, length us, event | category | flops | bytes accessed | tf_op | source)
XLA Modules:
  0.0 117.8 jit_solution(1827159780125293376)
XLA Ops:
  0.0 0.7 reduce
  0.8 1.8 %copy.8.strain = bf16[4,6,30,1024]{3,2,1,0:T(8,128)(2,1)S(1)} copy(bf16[4,6,30,1024]{3,0,2,1:T(4,128)(2,1)} %param.7) | data formatting | bytes 2949120 | tf_op args[0]
  2.8 11.0 %stiffness_tiles.1 = (f32[40,1024]{1,0:T(8,128)S(1)}, f32[40,1024]{1,0:T(8,128)S(1)}, f32[16,1024]{1,0:T(8,128)S(1)}, f32[16,1024]{1,0:T(8,128)S(1)}) custom-call(bf16[4,6,30,1024]{3,2,1,0:T(8,128)(2,1)S(1)} %copy.8.strain, f32[4,1024]{1,0:T(4,128)S(1)} %copy-done.1, f32[2,1024]{1,0:T(2,128)S(1)} %copy-done.2, s32[1,1024]{1,0:T(1,128)S(1)} %bitcast.17, ...), custom_call_target="tpu_custom_call" | custom-call | tf_op jit(solution)/shard_map/stiffness_tiles/pallas_call | solution.py:136
  13.8 0.5 collective-permute-start.1
  14.3 0.2 collective-permute-start.2
  14.5 3.5 %collective-permute-done = f32[40,1024]{1,0:T(8,128)S(1)} collective-permute-done((f32[40,1024]{1,0:T(8,128)S(1)}, f32[40,1024]{1,0:T(8,128)S(1)}, u32[]{:S(2)}, u32[]{:S(2)}) %collective-permute-start) | collective-permute-done | bytes 163872 | tf_op jit(solution)/shard_map/ppermute | solution.py:315
  18.0 5.3 %collective-permute-start.7 = (f32[12,1024]{1,0:T(8,128)S(1)}, f32[12,1024]{1,0:T(8,128)S(1)}, u32[]{:S(2)}, u32[]{:S(2)}) collective-permute-start(f32[12,1024]{1,0:T(8,128)S(1)} %get-tuple-element.15), channel_id=1, source_target_pairs={{0,120},{1,121},{2,122},{3,123},{4,124},{5,125},{6,126},{7,127},{8... | collective-permute-start | bytes 147464 | tf_op jit(solution)/shard_map/ppermute | solution.py:315
  23.3 0.8 collective-permute-start.8
  24.2 1.2 %collective-permute-start.10 = (bf16[384,128]{1,0:T(8,128)(2,1)S(1)}, bf16[384,128]{1,0:T(8,128)(2,1)S(1)}, u32[]{:S(2)}, u32[]{:S(2)}) collective-permute-start(bf16[384,128]{1,0:T(8,128)(2,1)S(1)} %get-tuple-element.20), channel_id=1, source_target_pairs={{0,96},{8,104},{16,112},{24,120},{32,0},{40,8},{48,16},{56,24},{64... | collective-permute-start | bytes 294920 | tf_op jit(solution)/shard_map/ppermute | solution.py:307
  25.4 0.9 collective-permute-start.9
  26.3 2.7 %collective-permute-start.11 = (bf16[384,128]{1,0:T(8,128)(2,1)S(1)}, bf16[384,128]{1,0:T(8,128)(2,1)S(1)}, u32[]{:S(2)}, u32[]{:S(2)}) collective-permute-start(bf16[384,128]{1,0:T(8,128)(2,1)S(1)} %get-tuple-element.20), channel_id=1, source_target_pairs={{0,64},{8,72},{16,80},{24,88},{32,96},{40,104},{48,112},{56,120},{... | collective-permute-start | bytes 294920 | tf_op jit(solution)/shard_map/ppermute | solution.py:307
  29.1 0.7 collective-permute-start.3
  29.8 1.4 %collective-permute-done.9 = bf16[384,128]{1,0:T(8,128)(2,1)S(1)} collective-permute-done((bf16[384,128]{1,0:T(8,128)(2,1)S(1)}, bf16[384,128]{1,0:T(8,128)(2,1)S(1)}, u32[]{:S(2)}, u32[]{:S(2)}) %collective-permute-start.9) | collective-permute-done | bytes 98336 | tf_op jit(solution)/shard_map/ppermute | solution.py:307
  31.2 1.4 %collective-permute-done.11 = bf16[384,128]{1,0:T(8,128)(2,1)S(1)} collective-permute-done((bf16[384,128]{1,0:T(8,128)(2,1)S(1)}, bf16[384,128]{1,0:T(8,128)(2,1)S(1)}, u32[]{:S(2)}, u32[]{:S(2)}) %collective-permute-start.11) | collective-permute-done | bytes 98336 | tf_op jit(solution)/shard_map/ppermute | solution.py:307
  32.7 4.1 %collective-permute-start.14 = (bf16[4,384,128]{2,1,0:T(8,128)(2,1)S(1)}, bf16[4,384,128]{2,1,0:T(8,128)(2,1)S(1)}, u32[]{:S(2)}, u32[]{:S(2)}) collective-permute-start(bf16[4,384,128]{2,1,0:T(8,128)(2,1)S(1)} %pad_maximum_fusion.refs_0_), channel_id=1, source_target_pairs={{0,16},{8,24},{16,0},{24,8},{32,48},{40,56},{48,32},{56,40},{64,80... | collective-permute-start | bytes 1179656 | tf_op jit(solution)/shard_map/ppermute | solution.py:311
  36.8 2.5 %collective-permute-start.4 = (f32[24,1024]{1,0:T(8,128)S(1)}, f32[24,1024]{1,0:T(8,128)S(1)}, u32[]{:S(2)}, u32[]{:S(2)}) collective-permute-start(f32[24,1024]{1,0:T(8,128)S(1)} %fusion), channel_id=1, source_target_pairs={{0,16},{8,24},{16,0},{24,8},{32,48},{40,56},{48,32},{56,40},{64,80... | collective-permute-start | bytes 294920 | tf_op jit(solution)/shard_map/ppermute | solution.py:345
  39.3 7.8 %collective-permute-done.4 = f32[24,1024]{1,0:T(8,128)S(1)} collective-permute-done((f32[24,1024]{1,0:T(8,128)S(1)}, f32[24,1024]{1,0:T(8,128)S(1)}, u32[]{:S(2)}, u32[]{:S(2)}) %collective-permute-start.4) | collective-permute-done | bytes 98336 | tf_op jit(solution)/shard_map/ppermute | solution.py:345
  47.1 0.7 collective-permute-start.5
  47.8 5.8 %collective-permute-start.16 = (bf16[384,128]{1,0:T(8,128)(2,1)S(1)}, bf16[384,128]{1,0:T(8,128)(2,1)S(1)}, u32[]{:S(2)}, u32[]{:S(2)}) collective-permute-start(bf16[384,128]{1,0:T(8,128)(2,1)S(1)} %get-tuple-element.19), channel_id=1, source_target_pairs={{0,24},{8,0},{16,8},{24,16},{32,56},{40,32},{48,40},{56,48},{64,88... | collective-permute-start | bytes 294920 | tf_op jit(solution)/shard_map/ppermute | solution.py:311
  53.7 1.5 %collective-permute-start.17 = (bf16[384,128]{1,0:T(8,128)(2,1)S(1)}, bf16[384,128]{1,0:T(8,128)(2,1)S(1)}, u32[]{:S(2)}, u32[]{:S(2)}) collective-permute-start(bf16[384,128]{1,0:T(8,128)(2,1)S(1)} %get-tuple-element.19), channel_id=1, source_target_pairs={{0,16},{8,24},{16,0},{24,8},{32,48},{40,56},{48,32},{56,40},{64,80... | collective-permute-start | bytes 294920 | tf_op jit(solution)/shard_map/ppermute | solution.py:311
  55.1 2.8 %collective-permute-start.13 = (bf16[4,384,128]{2,1,0:T(8,128)(2,1)S(1)}, bf16[4,384,128]{2,1,0:T(8,128)(2,1)S(1)}, u32[]{:S(2)}, u32[]{:S(2)}) collective-permute-start(bf16[4,384,128]{2,1,0:T(8,128)(2,1)S(1)} %pad_maximum_fusion.refs_0_), channel_id=1, source_target_pairs={{0,24},{8,0},{16,8},{24,16},{32,56},{40,32},{48,40},{56,48},{64,88... | collective-permute-start | bytes 1179656 | tf_op jit(solution)/shard_map/ppermute | solution.py:311
  58.0 4.0 %collective-permute-done.15 = bf16[384,128]{1,0:T(8,128)(2,1)S(1)} collective-permute-done((bf16[384,128]{1,0:T(8,128)(2,1)S(1)}, bf16[384,128]{1,0:T(8,128)(2,1)S(1)}, u32[]{:S(2)}, u32[]{:S(2)}) %collective-permute-start.15) | collective-permute-done | bytes 98336 | tf_op jit(solution)/shard_map/ppermute | solution.py:311
  62.0 2.5 %collective-permute-start.6 = (f32[24,1024]{1,0:T(8,128)S(1)}, f32[24,1024]{1,0:T(8,128)}, u32[]{:S(2)}, u32[]{:S(2)}) collective-permute-start(f32[24,1024]{1,0:T(8,128)S(1)} %add.54), channel_id=1, source_target_pairs={{0,64},{8,72},{16,80},{24,88},{32,96},{40,104},{48,112},{56,120},{... | collective-permute-start | bytes 294920 | tf_op jit(solution)/shard_map/ppermute | solution.py:345
  64.6 1.1 collective-permute-start.20
  65.7 1.3 %collective-permute-start.19 = (bf16[4,384,128]{2,1,0:T(8,128)(2,1)S(1)}, bf16[4,384,128]{2,1,0:T(8,128)(2,1)S(1)}, u32[]{:S(2)}, u32[]{:S(2)}) collective-permute-start(bf16[4,384,128]{2,1,0:T(8,128)(2,1)S(1)} %pad_maximum_fusion.1.refs_4_), channel_id=1, source_target_pairs={{0,96},{8,104},{16,112},{24,120},{32,0},{40,8},{48,16},{56,24},{64... | collective-permute-start | bytes 1179656 | tf_op jit(solution)/shard_map/ppermute | solution.py:307
  67.0 2.3 %collective-permute-done.6 = f32[24,1024]{1,0:T(8,128)} collective-permute-done((f32[24,1024]{1,0:T(8,128)S(1)}, f32[24,1024]{1,0:T(8,128)}, u32[]{:S(2)}, u32[]{:S(2)}) %collective-permute-start.6) | collective-permute-done | bytes 98336 | tf_op jit(solution)/shard_map/ppermute | solution.py:345
  69.4 0.6 collective-permute-start.18
  70.0 0.9 add.55.lead
  70.9 7.3 %collective-permute-done.20.refs_7_ = bf16[4,384,128]{2,1,0:T(8,128)(2,1)S(1)} collective-permute-done((bf16[4,384,128]{2,1,0:T(8,128)(2,1)S(1)}, bf16[4,384,128]{2,1,0:T(8,128)(2,1)S(1)}, u32[]{:S(2)}, u32[]{:S(2)}) %collective-permute-start.20) | collective-permute-done | bytes 393248 | tf_op jit(solution)/shard_map/ppermute | solution.py:307
  78.2 3.0 %collective-permute-done.19.refs_6_ = bf16[4,384,128]{2,1,0:T(8,128)(2,1)S(1)} collective-permute-done((bf16[4,384,128]{2,1,0:T(8,128)(2,1)S(1)}, bf16[4,384,128]{2,1,0:T(8,128)(2,1)S(1)}, u32[]{:S(2)}, u32[]{:S(2)}) %collective-permute-start.19) | collective-permute-done | bytes 393248 | tf_op jit(solution)/shard_map/ppermute | solution.py:307
  81.2 2.4 %collective-permute-done.18.refs_5_ = bf16[4,384,128]{2,1,0:T(8,128)(2,1)S(1)} collective-permute-done((bf16[4,384,128]{2,1,0:T(8,128)(2,1)S(1)}, bf16[4,384,128]{2,1,0:T(8,128)(2,1)S(1)}, u32[]{:S(2)}, u32[]{:S(2)}) %collective-permute-start.18) | collective-permute-done | bytes 393248 | tf_op jit(solution)/shard_map/ppermute | solution.py:307
  83.6 34.0 %factor_rows.1 = f32[1,384,6144]{2,1,0:T(8,128)} custom-call(s32[2]{0:T(128)S(1)} %pad_add_fusion.place, f32[24,1024]{1,0:T(8,128)S(1)} %add.55.lead, f32[12,1024]{1,0:T(8,128)S(1)} %get-tuple-element.13.own_tiles, bf16[384,256]{1,0:T(8,128)(2,1)S(1)} %bitcast.16, bf16[4,384,128]{2,1,0:T(8,128)(2,1)S(1)} %pad_maximum_fusion.refs_0_, ...), custom_call_target="tpu_custom_call" | custom-call | tf_op jit(solution)/shard_map/factor_rows/pallas_call | solution.py:285
  (39 shorter events, 0.7 us)
Async XLA Ops:
  0.0 2.7 %copy-start.4 = (s32[1024,1]{0,1:T(1,128)S(1)}, s32[1024,1]{0,1:T(1,128)}, u32[]{:S(2)}) copy-start(s32[1024,1]{0,1:T(1,128)} %param.10) | copy-start | bytes 12292
  0.0 2.7 %copy-start.3 = (s32[1024]{0:T(1024)S(1)}, s32[1024]{0:T(1024)}, u32[]{:S(2)}) copy-start(s32[1024]{0:T(1024)} %param.11) | copy-start | bytes 12292
  0.0 2.7 %copy-start.2 = (f32[2,1024]{1,0:T(2,128)S(1)}, f32[2,1024]{1,0:T(2,128)}, u32[]{:S(2)}) copy-start(f32[2,1024]{1,0:T(2,128)} %moduli.1) | copy-start | bytes 24580
  0.0 2.7 %copy-start.1 = (f32[4,1024]{1,0:T(4,128)S(1)}, f32[4,1024]{1,0:T(4,128)}, u32[]{:S(2)}) copy-start(f32[4,1024]{1,0:T(4,128)} %scale.1) | copy-start | bytes 49156
  2.7 21.4 %copy-start = (bf16[1,384,256]{2,1,0:T(8,128)(2,1)S(1)}, bf16[1,384,256]{2,1,0:T(8,128)(2,1)}, u32[]{:S(2)}) copy-start(bf16[1,384,256]{2,1,0:T(8,128)(2,1)} %param.13) | copy-start | bytes 589828
  13.7 4.3 %collective-permute-start = (f32[40,1024]{1,0:T(8,128)S(1)}, f32[40,1024]{1,0:T(8,128)S(1)}, u32[]{:S(2)}, u32[]{:S(2)}) collective-permute-start(f32[40,1024]{1,0:T(8,128)S(1)} %get-tuple-element.10), channel_id=1, source_target_pairs={{0,127},{1,0},{2,1},{3,2},{4,3},{5,4},{6,5},{7,6},{8,7},{9,8},{10,... | collective-permute-start | bytes 491528 | tf_op jit(solution)/shard_map/ppermute | solution.py:315
  13.8 11.6 %collective-permute-start.1 = (f32[16,1024]{1,0:T(8,128)S(1)}, f32[16,1024]{1,0:T(8,128)S(1)}, u32[]{:S(2)}, u32[]{:S(2)}) collective-permute-start(f32[16,1024]{1,0:T(8,128)S(1)} %get-tuple-element.11), channel_id=1, source_target_pairs={{0,126},{1,127},{2,0},{3,1},{4,2},{5,3},{6,4},{7,5},{8,6},{9,7},{1... | collective-permute-start | bytes 196616 | tf_op jit(solution)/shard_map/ppermute | solution.py:315
  14.3 12.0 %collective-permute-start.2 = (f32[16,1024]{1,0:T(8,128)S(1)}, f32[16,1024]{1,0:T(8,128)S(1)}, u32[]{:S(2)}, u32[]{:S(2)}) collective-permute-start(f32[16,1024]{1,0:T(8,128)S(1)} %get-tuple-element.12), channel_id=1, source_target_pairs={{0,125},{1,126},{2,127},{3,0},{4,1},{5,2},{6,3},{7,4},{8,5},{9,6},... | collective-permute-start | bytes 196616 | tf_op jit(solution)/shard_map/ppermute | solution.py:315
  18.0 11.0 %collective-permute-start.7 = (f32[12,1024]{1,0:T(8,128)S(1)}, f32[12,1024]{1,0:T(8,128)S(1)}, u32[]{:S(2)}, u32[]{:S(2)}) collective-permute-start(f32[12,1024]{1,0:T(8,128)S(1)} %get-tuple-element.15), channel_id=1, source_target_pairs={{0,120},{1,121},{2,122},{3,123},{4,124},{5,125},{6,126},{7,127},{8... | collective-permute-start | bytes 147464 | tf_op jit(solution)/shard_map/ppermute | solution.py:315
  23.3 5.8 %collective-permute-start.8 = (f32[12,1024]{1,0:T(8,128)S(1)}, f32[12,1024]{1,0:T(8,128)S(1)}, u32[]{:S(2)}, u32[]{:S(2)}) collective-permute-start(f32[12,1024]{1,0:T(8,128)S(1)} %get-tuple-element.16), channel_id=1, source_target_pairs={{0,64},{1,65},{2,66},{3,67},{4,68},{5,69},{6,70},{7,71},{8,72},{9,... | collective-permute-start | bytes 147464 | tf_op jit(solution)/shard_map/ppermute | solution.py:315
  24.2 5.7 %collective-permute-start.10 = (bf16[384,128]{1,0:T(8,128)(2,1)S(1)}, bf16[384,128]{1,0:T(8,128)(2,1)S(1)}, u32[]{:S(2)}, u32[]{:S(2)}) collective-permute-start(bf16[384,128]{1,0:T(8,128)(2,1)S(1)} %get-tuple-element.20), channel_id=1, source_target_pairs={{0,96},{8,104},{16,112},{24,120},{32,0},{40,8},{48,16},{56,24},{64... | collective-permute-start | bytes 294920 | tf_op jit(solution)/shard_map/ppermute | solution.py:307
  25.4 5.8 %collective-permute-start.9 = (bf16[384,128]{1,0:T(8,128)(2,1)S(1)}, bf16[384,128]{1,0:T(8,128)(2,1)S(1)}, u32[]{:S(2)}, u32[]{:S(2)}) collective-permute-start(bf16[384,128]{1,0:T(8,128)(2,1)S(1)} %get-tuple-element.20), channel_id=1, source_target_pairs={{0,32},{8,40},{16,48},{24,56},{32,64},{40,72},{48,80},{56,88},{64,... | collective-permute-start | bytes 294920 | tf_op jit(solution)/shard_map/ppermute | solution.py:307
  26.3 6.4 %collective-permute-start.11 = (bf16[384,128]{1,0:T(8,128)(2,1)S(1)}, bf16[384,128]{1,0:T(8,128)(2,1)S(1)}, u32[]{:S(2)}, u32[]{:S(2)}) collective-permute-start(bf16[384,128]{1,0:T(8,128)(2,1)S(1)} %get-tuple-element.20), channel_id=1, source_target_pairs={{0,64},{8,72},{16,80},{24,88},{32,96},{40,104},{48,112},{56,120},{... | collective-permute-start | bytes 294920 | tf_op jit(solution)/shard_map/ppermute | solution.py:307
  29.1 7.6 %collective-permute-start.3 = (f32[24,1024]{1,0:T(8,128)S(1)}, f32[24,1024]{1,0:T(8,128)S(1)}, u32[]{:S(2)}, u32[]{:S(2)}) collective-permute-start(f32[24,1024]{1,0:T(8,128)S(1)} %pad_maximum_fusion.2), channel_id=1, source_target_pairs={{0,8},{8,0},{16,24},{24,16},{32,40},{40,32},{48,56},{56,48},{64,72... | collective-permute-start | bytes 294920 | tf_op jit(solution)/shard_map/ppermute | solution.py:345
  32.7 33.0 %collective-permute-start.14 = (bf16[4,384,128]{2,1,0:T(8,128)(2,1)S(1)}, bf16[4,384,128]{2,1,0:T(8,128)(2,1)S(1)}, u32[]{:S(2)}, u32[]{:S(2)}) collective-permute-start(bf16[4,384,128]{2,1,0:T(8,128)(2,1)S(1)} %pad_maximum_fusion.refs_0_), channel_id=1, source_target_pairs={{0,16},{8,24},{16,0},{24,8},{32,48},{40,56},{48,32},{56,40},{64,80... | collective-permute-start | bytes 1179656 | tf_op jit(solution)/shard_map/ppermute | solution.py:311
  36.8 10.3 %collective-permute-start.4 = (f32[24,1024]{1,0:T(8,128)S(1)}, f32[24,1024]{1,0:T(8,128)S(1)}, u32[]{:S(2)}, u32[]{:S(2)}) collective-permute-start(f32[24,1024]{1,0:T(8,128)S(1)} %fusion), channel_id=1, source_target_pairs={{0,16},{8,24},{16,0},{24,8},{32,48},{40,56},{48,32},{56,40},{64,80... | collective-permute-start | bytes 294920 | tf_op jit(solution)/shard_map/ppermute | solution.py:345
  47.1 8.0 %collective-permute-start.5 = (f32[24,1024]{1,0:T(8,128)S(1)}, f32[24,1024]{1,0:T(8,128)S(1)}, u32[]{:S(2)}, u32[]{:S(2)}) collective-permute-start(f32[24,1024]{1,0:T(8,128)S(1)} %add.53), channel_id=1, source_target_pairs={{0,32},{8,40},{16,48},{24,56},{32,0},{40,8},{48,16},{56,24},{64,96... | collective-permute-start | bytes 294920 | tf_op jit(solution)/shard_map/ppermute | solution.py:345
  47.8 10.1 %collective-permute-start.16 = (bf16[384,128]{1,0:T(8,128)(2,1)S(1)}, bf16[384,128]{1,0:T(8,128)(2,1)S(1)}, u32[]{:S(2)}, u32[]{:S(2)}) collective-permute-start(bf16[384,128]{1,0:T(8,128)(2,1)S(1)} %get-tuple-element.19), channel_id=1, source_target_pairs={{0,24},{8,0},{16,8},{24,16},{32,56},{40,32},{48,40},{56,48},{64,88... | collective-permute-start | bytes 294920 | tf_op jit(solution)/shard_map/ppermute | solution.py:311
  53.7 8.3 %collective-permute-start.15 = (bf16[384,128]{1,0:T(8,128)(2,1)S(1)}, bf16[384,128]{1,0:T(8,128)(2,1)S(1)}, u32[]{:S(2)}, u32[]{:S(2)}) collective-permute-start(bf16[384,128]{1,0:T(8,128)(2,1)S(1)} %get-tuple-element.19), channel_id=1, source_target_pairs={{0,8},{8,16},{16,24},{24,0},{32,40},{40,48},{48,56},{56,32},{64,72... | collective-permute-start | bytes 294920 | tf_op jit(solution)/shard_map/ppermute | solution.py:311
  53.7 10.8 %collective-permute-start.17 = (bf16[384,128]{1,0:T(8,128)(2,1)S(1)}, bf16[384,128]{1,0:T(8,128)(2,1)S(1)}, u32[]{:S(2)}, u32[]{:S(2)}) collective-permute-start(bf16[384,128]{1,0:T(8,128)(2,1)S(1)} %get-tuple-element.19), channel_id=1, source_target_pairs={{0,16},{8,24},{16,0},{24,8},{32,48},{40,56},{48,32},{56,40},{64,80... | collective-permute-start | bytes 294920 | tf_op jit(solution)/shard_map/ppermute | solution.py:311
  55.1 15.8 %collective-permute-start.13 = (bf16[4,384,128]{2,1,0:T(8,128)(2,1)S(1)}, bf16[4,384,128]{2,1,0:T(8,128)(2,1)S(1)}, u32[]{:S(2)}, u32[]{:S(2)}) collective-permute-start(bf16[4,384,128]{2,1,0:T(8,128)(2,1)S(1)} %pad_maximum_fusion.refs_0_), channel_id=1, source_target_pairs={{0,24},{8,0},{16,8},{24,16},{32,56},{40,32},{48,40},{56,48},{64,88... | collective-permute-start | bytes 1179656 | tf_op jit(solution)/shard_map/ppermute | solution.py:311
  57.9 13.0 %collective-permute-start.12 = (bf16[4,384,128]{2,1,0:T(8,128)(2,1)S(1)}, bf16[4,384,128]{2,1,0:T(8,128)(2,1)S(1)}, u32[]{:S(2)}, u32[]{:S(2)}) collective-permute-start(bf16[4,384,128]{2,1,0:T(8,128)(2,1)S(1)} %pad_maximum_fusion.refs_0_), channel_id=1, source_target_pairs={{0,8},{8,16},{16,24},{24,0},{32,40},{40,48},{48,56},{56,32},{64,72... | collective-permute-start | bytes 1179656 | tf_op jit(solution)/shard_map/ppermute | solution.py:311
  62.0 7.3 %collective-permute-start.6 = (f32[24,1024]{1,0:T(8,128)S(1)}, f32[24,1024]{1,0:T(8,128)}, u32[]{:S(2)}, u32[]{:S(2)}) collective-permute-start(f32[24,1024]{1,0:T(8,128)S(1)} %add.54), channel_id=1, source_target_pairs={{0,64},{8,72},{16,80},{24,88},{32,96},{40,104},{48,112},{56,120},{... | collective-permute-start | bytes 294920 | tf_op jit(solution)/shard_map/ppermute | solution.py:345
  64.6 13.7 %collective-permute-start.20 = (bf16[4,384,128]{2,1,0:T(8,128)(2,1)S(1)}, bf16[4,384,128]{2,1,0:T(8,128)(2,1)S(1)}, u32[]{:S(2)}, u32[]{:S(2)}) collective-permute-start(bf16[4,384,128]{2,1,0:T(8,128)(2,1)S(1)} %pad_maximum_fusion.1.refs_4_), channel_id=1, source_target_pairs={{0,64},{8,72},{16,80},{24,88},{32,96},{40,104},{48,112},{56,120},{... | collective-permute-start | bytes 1179656 | tf_op jit(solution)/shard_map/ppermute | solution.py:307
  65.7 15.5 %collective-permute-start.19 = (bf16[4,384,128]{2,1,0:T(8,128)(2,1)S(1)}, bf16[4,384,128]{2,1,0:T(8,128)(2,1)S(1)}, u32[]{:S(2)}, u32[]{:S(2)}) collective-permute-start(bf16[4,384,128]{2,1,0:T(8,128)(2,1)S(1)} %pad_maximum_fusion.1.refs_4_), channel_id=1, source_target_pairs={{0,96},{8,104},{16,112},{24,120},{32,0},{40,8},{48,16},{56,24},{64... | collective-permute-start | bytes 1179656 | tf_op jit(solution)/shard_map/ppermute | solution.py:307
  69.4 14.3 %collective-permute-start.18 = (bf16[4,384,128]{2,1,0:T(8,128)(2,1)S(1)}, bf16[4,384,128]{2,1,0:T(8,128)(2,1)S(1)}, u32[]{:S(2)}, u32[]{:S(2)}) collective-permute-start(bf16[4,384,128]{2,1,0:T(8,128)(2,1)S(1)} %pad_maximum_fusion.1.refs_4_), channel_id=1, source_target_pairs={{0,32},{8,40},{16,48},{24,56},{32,64},{40,72},{48,80},{56,88},{64,... | collective-permute-start | bytes 1179656 | tf_op jit(solution)/shard_map/ppermute | solution.py:307

commit v2 on v1

v2 whole, which is shorter than its diff:
```python
import functools

import jax
import jax.numpy as jnp
from jax import lax
from jax.experimental import pallas as pl
from jax.experimental.pallas import tpu as pltpu
from jax.sharding import PartitionSpec as P

F32 = jnp.float32
BF16 = jnp.bfloat16
W = 384
WINDOW = 768
PARTS = ((0, 512), (512, 256))
RANK = 256
SLOTS = 12
TILE = 1024
CHUNK = 256
ACROSS = (0, 1, 3, 2)
BINS = {0: 0, 8: 12, 64: 24, 1: 40, 9: 52, 65: 64, 2: 80, 3: 96}
BIN_ROWS = 112


def split3(x):
    a = x.astype(BF16); r = x - a.astype(F32)
    b = r.astype(BF16); c = (r - b.astype(F32)).astype(BF16)
    return a, b, c


def dot_nn(a, b): return lax.dot_general(a, b, (((1,), (0,)), ((), ())), preferred_element_type=F32)
def dot_nt(a, b): return lax.dot_general(a, b, (((1,), (1,)), ((), ())), preferred_element_type=F32)


def product_tn(x, y):
    x1, x2, x3 = split3(x)
    y1, y2, y3 = split3(y)
    left = jnp.concatenate([x1, x1, x2, x1, x2, x3], axis=0)
    right = jnp.concatenate([y1, y2, y1, y3, y2, y1], axis=0)
    return lax.dot_general(left, right, (((0,), (0,)), ((), ())), preferred_element_type=F32)


def eliminate(rows, first):
    sub = lax.broadcasted_iota(jnp.int32, (8, 128), 0)
    n = len(rows)
    spread = lambda x, at: jnp.broadcast_to(x[at:at + 1, :], (8, 128))
    cols = {}
    for k in range(8 * n):
        for q in range(k // 8, n):
            cols[q, k] = jnp.broadcast_to(rows[q][0][:, first + k:first + k + 1], (8, 128))
    for k in range(8 * n):
        t, u = k // 8, k % 8
        rs = lax.rsqrt(spread(cols[t, k], u))
        f = {q: cols[q, k] * rs for q in range(t, n)}
        for m in range(k + 1, 8 * n):
            sm = spread(f[m // 8], m % 8)
            for q in range(m // 8, n):
                cols[q, m] = cols[q, m] - f[q] * sm
        fm = jnp.where(sub > u, f[t], 0.0)
        for h in range(len(rows[t])):
            r = spread(rows[t][h], u) * rs
            rows[t][h] = jnp.where(sub == u, r, rows[t][h] - fm * r)
            for q in range(t + 1, n):
                rows[q][h] = rows[q][h] - f[q] * r
    return rows


def unpack_tiles(packed, out_ref):
    n = packed.shape[0]
    lane = lax.broadcasted_iota(jnp.int32, (n, 128), 1) // 32
    tile = lax.broadcasted_iota(jnp.int32, (n, 128), 0) % 4
    for g in range(8):
        x = packed[:, 128 * g:128 * g + 128]
        turned = [x] + [pltpu.roll(x, 32 * r, 1) for r in range(1, 4)]
        for u in range(4):
            row = jnp.zeros((n, 128), F32)
            for v in range(4):
                row = jnp.where((lane == v) & (tile == v), turned[(v - u) % 4], row)
            out_ref[pl.ds(4 * g + u, n, stride=32), :] = row


def stiffness_kernel(first, strain, scale, moduli, bins, begin, *refs):
    outs, (plain, weighted, high, low, total, data, sems) = refs[:-7], refs[-7:]
    steps = data.shape[0]
    copies = []
    for n in range(steps):
        at = pl.ds((first + n) * CHUNK, CHUNK)
        copies.append(pltpu.make_async_copy(strain.at[:, :, :, at], data.at[n], sems.at[n]))
        copies[n].start()
    plain[...] = jnp.zeros_like(plain)
    weighted[...] = jnp.zeros_like(weighted)
    high[...] = jnp.zeros_like(high)
    low[...] = jnp.zeros_like(low)
    if first:
        total[...] = begin[...]
    else:
        total[...] = jnp.zeros_like(total)
        lane = lax.broadcasted_iota(jnp.int32, (SLOTS, TILE), 1)
        spread = jnp.concatenate([begin[...]] * 32, axis=1)
        total[:SLOTS, :] = jnp.where(lane // 32 == lane % 32, spread, 0.0)

    for step in range(steps):
        copies[step].wait()

        def one_part(part, carry):
            here = pl.multiple_of(128 * part, 128)
            at = pl.ds(here, 128)
            there = pl.ds(pl.multiple_of((first + step) * CHUNK + here, 128), 128)
            for q in range(4):
                weight = scale[q:q + 1, there]
                shear = weight * moduli[0:1, there]
                bulk = weight * moduli[1:2, there]
                diverge = None
                for s in range(6):
                    b = data[step, q, s, :, at].astype(F32)
                    plain[7 * q + s, :30, :] = b
                    weighted[7 * q + s, :30, :] = b * shear
                    if s < 3:
                        diverge = b if s == 0 else diverge + b
                plain[7 * q + 6, :30, :] = diverge
                weighted[7 * q + 6, :30, :] = diverge * bulk
            for a in range(4):
                rows = range(8 * a, min(8 * a + 8, 30))
                sums = {}
                for n in range(28):
                    right = weighted[n, 8 * a:, :]
                    for i in rows:
                        term = plain[n, i:i + 1, :] * right
                        sums[i] = term if n == 0 else sums[i] + term
                for i in rows:
                    k = sums[i]
                    if a:
                        k = jnp.concatenate([jnp.zeros((8 * a, 128), F32), k], axis=0)
                    top = k.astype(BF16)
                    high[32 * i:32 * i + 32, at] = top
                    low[32 * i:32 * i + 32, at] = (k - top.astype(F32)).astype(BF16)
            return carry

        lax.fori_loop(0, CHUNK // 128, one_part, 0)
        chosen = lax.broadcasted_iota(jnp.int32, (BIN_ROWS, CHUNK), 0) == bins[:, (first + step) * CHUNK:(first + step + 1) * CHUNK]
        chosen = chosen.astype(F32).astype(BF16)
        total[...] += dot_nt(chosen, high[...]) + dot_nt(chosen, low[...])

    at = 0
    for out in outs:
        out[...] = total[at:at + out.shape[0], :]
        at += out.shape[0]


def stiffness_tiles(first, steps, strain, scale, moduli, bins, begin, outs):
    vmem = pl.BlockSpec(memory_space=pltpu.VMEM)
    return pl.pallas_call(
        functools.partial(stiffness_kernel, first),
        in_specs=[pl.BlockSpec(memory_space=pltpu.HBM)] + [vmem] * 4,
        out_specs=[vmem] * len(outs),
        out_shape=[jax.ShapeDtypeStruct((r, TILE), F32) for r in outs],
        scratch_shapes=[
            pltpu.VMEM((28, 32, 128), F32),
            pltpu.VMEM((28, 32, 128), F32),
            pltpu.VMEM((TILE, CHUNK), BF16),
            pltpu.VMEM((TILE, CHUNK), BF16),
            pltpu.VMEM((BIN_ROWS, TILE), F32),
            pltpu.VMEM((steps, 4, 6, 30, CHUNK), BF16),
            pltpu.SemaphoreType.DMA((steps,)),
        ],
        cost_estimate=pl.CostEstimate(flops=5 * 10**9, bytes_accessed=15 * 10**6, transcendentals=0),
        compiler_params=pltpu.CompilerParams(vmem_limit_bytes=32 * 2**20),
        name="stiffness_tiles",
    )(strain, scale, moduli, bins, begin)


def mirror(block):
    row = lax.broadcasted_iota(jnp.int32, block.shape, 0) // 8
    col = lax.broadcasted_iota(jnp.int32, block.shape, 1) // 8
    return jnp.where(row <= col, block, block.T)


def factor_window(diag, v_ref, h_ref, m_ref, work):
    square = lambda n, dim: lax.broadcasted_iota(jnp.int32, (n, n), dim)
    upper = square(128, 0) <= square(128, 1)

    def block(j, carry):
        at = pl.ds(pl.multiple_of(j * 128, 128), 128)
        v = v_ref[at, :]
        m1, m2, m3 = split3(m_ref[...])
        p = dot_nn(v, m1) + (dot_nn(v, m2) + dot_nn(v, m3))
        p1, p2, p3 = split3(p)
        work[:, :128] = mirror(diag[at, :]) + (dot_nt(p1, v) + (dot_nt(p2, v) + dot_nt(p3, v)))
        work[:, 128:] = p
        for s in range(4):
            at_row = lambda q: slice(32 * s + 8 * q, 32 * s + 8 * q + 8)
            rows = [[work[at_row(q), 128 * h:128 * h + 128] for h in range(3)] for q in range(4)]
            rows = eliminate(rows, 32 * s)
            for q in range(4):
                for h in range(3):
                    work[at_row(q), 128 * h:128 * h + 128] = rows[q][h]
            if s < 3:
                done = work[32 * s:32 * s + 32, :]
                change = product_tn(done[:, :128], done)
                work[32 * s + 32:, :] = work[32 * s + 32:, :] - change[32 * s + 32:, :]
        h = work[:, 128:]
        h_ref[at, :] = h
        diag[at, :] = jnp.where(upper, work[:, :128], 0.0).T
        m_ref[...] = m_ref[...] - product_tn(h, h)
        return carry

    lax.fori_loop(0, diag.shape[0] // 128, block, 0)


def window_kernel(part, place, lead, v0, v1, v2, *refs):
    high_ref, low_ref, m_ref, diag, v_ref, h_ref, work = refs[-7:]
    first, size = PARTS[part]
    x = place[0] // 4
    for n, v in enumerate((v0, v1, v2)):
        @pl.when((x == n) | ((x == 3) & (n == 2)))
        def _():
            v_ref[...] = v[first:first + size, :] * 0.0625

    if part:
        m_ref[...] = refs[0][...]
    else:
        square = lambda dim: lax.broadcasted_iota(jnp.int32, (RANK, RANK), dim)
        m_ref[...] = (square(0) == square(1)).astype(F32)
    unpack_tiles(lead[first // 32:(first + size) // 32, :], diag)
    factor_window(diag, v_ref, h_ref, m_ref, work)
    h = h_ref[...]
    high = h.astype(BF16)
    high_ref[...] = high
    low_ref[...] = (h - high.astype(F32)).astype(BF16)


def window_factor(part, place, lead, v, m):
    vmem = pl.BlockSpec(memory_space=pltpu.VMEM)
    size = PARTS[part][1]
    return pl.pallas_call(
        functools.partial(window_kernel, part),
        in_specs=[pl.BlockSpec(memory_space=pltpu.SMEM)] + [vmem] * (4 + len(m)),
        out_specs=[vmem] * 4,
        out_shape=[
            jax.ShapeDtypeStruct((size, RANK), BF16),
            jax.ShapeDtypeStruct((size, RANK), BF16),
            jax.ShapeDtypeStruct((RANK, RANK), F32),
            jax.ShapeDtypeStruct((size, 128), F32),
        ],
        scratch_shapes=[
            pltpu.VMEM((size, RANK), BF16),
            pltpu.VMEM((size, RANK), F32),
            pltpu.VMEM((128, 128 + RANK), F32),
        ],
        cost_estimate=pl.CostEstimate(flops=size * 10**7, bytes_accessed=size * 10**5, transcendentals=0),
        compiler_params=pltpu.CompilerParams(vmem_limit_bytes=32 * 2**20),
        name="window_factor",
    )(place, lead, *v, *m)


def rows_kernel(place, high0, low0, diag0, high1, low1, m_ref, diag1, own_tiles, own, here, before, after, low, high, out, *scratch):
    own_diag, panel, blocks, sems = scratch
    cand = place[0]
    x, y = cand // 4, lax.rem(cand, 4)
    v_own = own[...] * 0.0625
    split = PARTS[1][0]
    panel[:, :split] = dot_nt(v_own, high0[...]) + dot_nt(v_own, low0[...])
    panel[:, split:] = dot_nt(v_own, high1[...]) + dot_nt(v_own, low1[...])
    for n in range(2):
        @pl.when(cand == n)
        def _():
            row = lax.broadcasted_iota(jnp.int32, (W, WINDOW), 0) // 128 + 3 * n
            col = lax.broadcasted_iota(jnp.int32, (W, WINDOW), 1) // 128
            panel[...] = jnp.where(row > col, panel[...], 0.0)
            for a in range(3):
                at = W * n + 128 * a
                diag = diag0[at:at + 128, :] if at < split else diag1[at - split:at - split + 128, :]
                panel[128 * a:128 * a + 128, at:at + 128] = diag

    panel_copy = pltpu.make_async_copy(panel, out.at[0, :, pl.ds(0, WINDOW)], sems.at[16])
    panel_copy.start()
    unpack_tiles(own_tiles[...], own_diag)
    m1, m2, m3 = split3(m_ref[...])
    q = (dot_nn(v_own, m1) + (dot_nn(v_own, m2) + dot_nn(v_own, m3))) * 0.0625
    q = jnp.where(cand < 2, 0.0, q)
    q1 = q.astype(BF16)
    q2 = (q - q1.astype(F32)).astype(BF16)
    stores = []
    for n, pieces in enumerate((here, before, after, (low, high))):
        column_x = lax.rem(x + (0, 3, 1, 2)[n], 4)
        for pair in range(2):
            v = pieces[pair][...] if n == 3 else pieces[2 * pair:2 * pair + 2]
            v = v.reshape(2 * W, RANK)
            slot = 2 * n + pair
            blocks[slot] = dot_nt(q1, v) + dot_nt(q2, v)
            if slot == 0:
                @pl.when(cand >= 2)
                def _():
                    for a in range(3):
                        at = slice(128 * a, 128 * a + 128)
                        blocks[0, at, at] += mirror(own_diag[at, :])

            for m in range(2):
                column = 4 * column_x + (y ^ ACROSS[2 * pair + m])
                copy = pltpu.make_async_copy(
                    blocks.at[slot, :, pl.ds(W * m, W)],
                    out.at[0, :, pl.ds(pl.multiple_of(column * W, 128), W)],
                    sems.at[2 * slot + m],
                )
                stores.append((column, copy))

                @pl.when(column >= 2)
                def _():
                    copy.start()
    panel_copy.wait()
    for column, copy in stores:
        @pl.when(column >= 2)
        def _():
            copy.wait()


def factor_rows(place, *operands):
    vmem = pl.BlockSpec(memory_space=pltpu.VMEM)
    return pl.pallas_call(
        rows_kernel,
        in_specs=[pl.BlockSpec(memory_space=pltpu.SMEM)] + [vmem] * len(operands),
        out_specs=pl.BlockSpec(memory_space=pltpu.HBM),
        out_shape=jax.ShapeDtypeStruct((1, W, 16 * W), F32),
        scratch_shapes=[
            pltpu.VMEM((W, 128), F32),
            pltpu.VMEM((W, WINDOW), F32),
            pltpu.VMEM((8, W, 2 * W), F32),
            pltpu.SemaphoreType.DMA((17,)),
        ],
        compiler_params=pltpu.CompilerParams(vmem_limit_bytes=40 * 2**20),
        name="factor_rows",
    )(place, *operands)


def move_x(value, shift, sources=range(4)):
    pairs = [(4 * x + y, 4 * ((x + shift) % 4) + y) for x in sources for y in range(4)]
    return lax.ppermute(value, "cand", pairs)


def swap(value, bits):
    return lax.ppermute(value, "cand", [(i, i ^ bits) for i in range(16)])


def move_back(value, offset):
    return lax.ppermute(value, ("cand", "dom"), [(i, (i - offset) % 128) for i in range(128)])


def local(strain_ops, elem_scale, moduli, elem_block, elem_slot, mass, updates):
    cand = lax.axis_index("cand")
    device = cand * lax.axis_size("dom") + lax.axis_index("dom")
    x, y = cand // 4, cand % 4
    own = updates[0]
    place = cand.astype(jnp.int32)[None]

    offset = (device - elem_block[:, 0]) & 127
    start = jnp.zeros_like(offset)
    for o, at in BINS.items():
        start = jnp.where(offset == o, at, start)
    bins = (start + elem_slot)[None, :]

    here = jnp.stack([own, swap(own, 1)])
    here, bins = lax.optimization_barrier((here, bins))
    here_far = swap(here, 3)
    tiles = stiffness_tiles(0, 4, strain_ops, elem_scale, moduli, bins, mass.reshape(SLOTS, 32), (40, 40, 16, 16))
    here = jnp.concatenate([here, here_far])
    (keep, far, two, three), here = lax.optimization_barrier((tiles, here))

    piece = lambda r: functools.reduce(lambda u, n: jnp.where(r == ACROSS[n], here[n], u), range(1, 4), here[0])
    window = jnp.concatenate([piece(y), piece(y ^ 1)])
    window_1 = move_x(window, 1, (0,))

    far = move_back(far, 1)
    two = move_back(two, 2)
    three = move_back(three, 3)
    kept = keep[:12] + far[:12] + two[:12] + three[:12]
    near = keep[12:24] + far[12:24]
    half = keep[24:36] + far[24:36]
    zero = jnp.zeros_like(kept)
    pick = lambda c: jnp.where(cand == c, kept, jnp.where(cand == c + 1, near, jnp.where(cand == c + 8, half, zero)))
    lead = jnp.concatenate([pick(0), pick(1)], axis=0)
    lead = lead + swap(lead, 1)
    lead, window_1 = lax.optimization_barrier((lead, window_1))
    window_2 = jnp.where(x == 0, window, window_1)
    window_2 = lax.ppermute(window_2, "cand", [(y, 12 + y) for y in range(4)] + [(4 + y, 8 + y) for y in range(4)])
    lead = lead + swap(lead, 3)
    lead = lead + swap(lead, 4)
    lead = lead + swap(lead, 12)
    lead, window_2, here, near, half = lax.optimization_barrier((lead, window_2, here, near, half))

    before, after = move_x(here, 1), move_x(here, 3)
    own_tiles = kept + move_back(near, 8) + move_back(half, 64)
    high0, low0, m, diag0 = window_factor(0, place, lead, (window, window_1, window_2), ())
    m, before, after = lax.optimization_barrier((m, before, after))
    low, high = move_x(before[:2], 1), move_x(after[2:], 3)
    high1, low1, m, diag1 = window_factor(1, place, lead, (window, window_1, window_2), (m,))
    return factor_rows(place, high0, low0, diag0, high1, low1, m, diag1, own_tiles, own, here, before, after, low, high)


def solution(mesh):
    placed = (
        P(None, None, None, ("cand", "dom")),
        P(None, ("cand", "dom")),
        P(None, ("cand", "dom")),
        P(("cand", "dom"), None),
        P(("cand", "dom")),
        P("dom", "cand"),
        P("dom", "cand", None),
    )
    return jax.shard_map(
        local, mesh=mesh, in_specs=placed, out_specs=P("dom", "cand", None), check_vma=False
    )
```

time: 120 us -> 96.1 us (0.80); the launches traced: 118 us -> 95.9 us
  Pallas kernels: 45 us -> 37 us
  starting transfers between devices: 35.3 us -> 28.4 us
  waiting for transfers between devices: 33.2 us -> 27 us
    pallas_call x2 -> x4, Pallas kernels: 45 us -> 37 us  [the longest x2 24 us: window_factor(): pl.pallas_call(functools.partial(window_kernel, part), in_specs=[pl.Block...]
    ppermute x16 -> x12, waiting for transfers between devices: 29.6 us -> 24 us  [the longest x6 21.8 us: swap(): return lax.ppermute(value, 'cand', [(i, i ^ bits) for i in range(16)])]
    ppermute x16 -> x12, starting transfers between devices: 28.5 us -> 23.3 us  [the longest x6 11.6 us: swap(): return lax.ppermute(value, 'cand', [(i, i ^ bits) for i in range(16)])]
    ppermute x5, starting transfers between devices: 6.81 us -> 5.11 us  [move_back(): lax.ppermute(value, ('cand', 'dom'), [(i, (i - offset) % 128) for i in ra...]
  transfers between devices with their start and end apart: 21 -> 17, of which waited for: 10 -> 9; matrix products, arithmetic and copies ran while one was open for 1% -> 3% of each run, Pallas kernels for 0% -> 33%
where the time goes in v2:
time: 96.1 us; the launch traced here: 95.9 us
  Pallas kernels  37 us (39%)
  starting transfers between devices  28.4 us (30%)
  waiting for transfers between devices  27 us (28%)
  local copies, waits for them, and re-layouts  1.99 us (2%)
  other arithmetic  1.17 us (1%)
    pallas_call x2, Pallas kernels, window_factor(): pl.pallas_call(functools.partial(window_kernel, part), in_specs=[pl.Block...  24 us
    ppermute x6, waiting for transfers between devices, swap(): return lax.ppermute(value, 'cand', [(i, i ^ bits) for i in range(16)])  21.8 us
    ppermute x6, starting transfers between devices, swap(): return lax.ppermute(value, 'cand', [(i, i ^ bits) for i in range(16)])  11.6 us
    ppermute x5, starting transfers between devices, move_x(): return lax.ppermute(value, 'cand', pairs)  8.19 us
    pallas_call x1, Pallas kernels, stiffness_tiles(): pl.pallas_call(functools.partial(stiffness_kernel, first), in_specs=[pl.B...  7.36 us
    pallas_call x1, Pallas kernels, factor_rows(): pl.pallas_call(rows_kernel, in_specs=[pl.BlockSpec(memory_space=pltpu.SME...  5.64 us
    ppermute x5, starting transfers between devices, move_back(): lax.ppermute(value, ('cand', 'dom'), [(i, (i - offset) % 128) for i in ra...  5.11 us
    ppermute x1, starting transfers between devices, local(): lax.ppermute(window_2, 'cand', [(y, 12 + y) for y in range(4)] + [(4 + y,...  3.49 us
  transfers between devices with their start and end apart: 17, of which 9 were waited for; matrix products, arithmetic and copies ran while one was open for 3% of the time, Pallas kernels for 33%

profile of v2, /device:TPU:96, one launch (start us, length us, event | category | flops | bytes accessed | tf_op | source)
XLA Modules:
  0.0 95.9 jit_solution(11194619539966572100)
XLA Ops:
  0.0 1.6 %collective-permute-start = (bf16[384,256]{1,0:T(8,128)(2,1)}, bf16[384,256]{1,0:T(8,128)(2,1)S(1)}, u32[]{:S(2)}, u32[]{:S(2)}) collective-permute-start(bf16[384,256]{1,0:T(8,128)(2,1)} %bitcast.9), channel_id=1, source_target_pairs={{0,8},{8,0},{16,24},{24,16},{32,40},{40,32},{48,56},{56,48},{64,72... | collective-permute-start | bytes 589832 | tf_op jit(solution)/shard_map/ppermute | solution.py:340
  1.6 0.7 reduce
  2.3 0.1 reshape.36.begin
  2.4 1.8 %copy.8.strain = bf16[4,6,30,1024]{3,2,1,0:T(8,128)(2,1)S(1)} copy(bf16[4,6,30,1024]{3,0,2,1:T(4,128)(2,1)} %param.7) | data formatting | bytes 2949120 | tf_op args[0]
  4.3 2.5 %collective-permute-done = bf16[384,256]{1,0:T(8,128)(2,1)S(1)} collective-permute-done((bf16[384,256]{1,0:T(8,128)(2,1)}, bf16[384,256]{1,0:T(8,128)(2,1)S(1)}, u32[]{:S(2)}, u32[]{:S(2)}) %collective-permute-start) | collective-permute-done | bytes 196640 | tf_op jit(solution)/shard_map/ppermute | solution.py:340
  6.9 3.1 %collective-permute-start.1 = (bf16[2,384,256]{2,1,0:T(8,128)(2,1)S(1)}, bf16[2,384,256]{2,1,0:T(8,128)(2,1)S(1)}, u32[]{:S(2)}, u32[]{:S(2)}) collective-permute-start(bf16[2,384,256]{2,1,0:T(8,128)(2,1)S(1)} %pad_maximum_fusion.1), channel_id=1, source_target_pairs={{0,24},{8,16},{16,8},{24,0},{32,56},{40,48},{48,40},{56,32},{64,88... | collective-permute-start | bytes 1179656 | tf_op jit(solution)/shard_map/ppermute | solution.py:340
  10.0 7.4 %stiffness_tiles.1 = (f32[40,1024]{1,0:T(8,128)S(1)}, f32[40,1024]{1,0:T(8,128)S(1)}, f32[16,1024]{1,0:T(8,128)S(1)}, f32[16,1024]{1,0:T(8,128)S(1)}) custom-call(bf16[4,6,30,1024]{3,2,1,0:T(8,128)(2,1)S(1)} %copy.8.strain, f32[4,1024]{1,0:T(4,128)S(1)} %copy-done.1, f32[2,1024]{1,0:T(2,128)S(1)} %copy-done.2, s32[1,1024]{1,0:T(1,128)S(1)} %bitcast.11, ...), custom_call_target="tpu_custom_call" | custom-call | flops 5000000000 | bytes 15000000 | tf_op jit(solution)/shard_map/stiffness_tiles/pallas_call | solution.py:151
  17.4 0.9 collective-permute-done.1
  18.2 0.1 pad_maximum_fusion.here
  18.3 0.5 collective-permute-start.3
  18.9 3.4 %collective-permute-start.6 = (bf16[768,256]{1,0:T(8,128)(2,1)S(1)}, bf16[768,256]{1,0:T(8,128)(2,1)S(1)}, u32[]{:S(2)}, u32[]{:S(2)}) collective-permute-start(bf16[768,256]{1,0:T(8,128)(2,1)S(1)} %pad_maximum_fusion.2.v0), channel_id=1, source_target_pairs={{0,32},{8,40},{16,48},{24,56},{1,33},{9,41},{17,49},{25,57},{2,34}... | collective-permute-start | bytes 1179656 | tf_op jit(solution)/shard_map/ppermute | solution.py:336
  22.3 3.0 %collective-permute-done.3 = f32[16,1024]{1,0:T(8,128)S(1)} collective-permute-done((f32[16,1024]{1,0:T(8,128)S(1)}, f32[16,1024]{1,0:T(8,128)S(1)}, u32[]{:S(2)}, u32[]{:S(2)}) %collective-permute-start.3) | collective-permute-done | bytes 65568 | tf_op jit(solution)/shard_map/ppermute | solution.py:344
  25.4 0.4 collective-permute-start.5
  25.8 4.3 %collective-permute-done.5 = f32[24,1024]{1,0:T(8,128)S(1)} collective-permute-done((f32[24,1024]{1,0:T(8,128)S(1)}, f32[24,1024]{1,0:T(8,128)S(1)}, u32[]{:S(2)}, u32[]{:S(2)}) %collective-permute-start.5) | collective-permute-done | bytes 98336 | tf_op jit(solution)/shard_map/ppermute | solution.py:340
  30.1 1.2 %collective-permute-done.6.v1 = bf16[768,256]{1,0:T(8,128)(2,1)S(1)} collective-permute-done((bf16[768,256]{1,0:T(8,128)(2,1)S(1)}, bf16[768,256]{1,0:T(8,128)(2,1)S(1)}, u32[]{:S(2)}, u32[]{:S(2)}) %collective-permute-start.6) | collective-permute-done | bytes 393248 | tf_op jit(solution)/shard_map/ppermute | solution.py:336
  31.3 0.1 broadcast_select_fusion
  31.4 3.5 %collective-permute-start.10 = (bf16[768,256]{1,0:T(8,128)(2,1)S(1)}, bf16[768,256]{1,0:T(8,128)(2,1)S(1)}, u32[]{:S(2)}, u32[]{:S(2)}) collective-permute-start(bf16[768,256]{1,0:T(8,128)(2,1)S(1)} %broadcast_select_fusion), channel_id=1, source_target_pairs={{0,96},{8,104},{16,112},{24,120},{32,64},{40,72},{48,80},{56,88},{... | collective-permute-start | bytes 1179656 | tf_op jit(solution)/shard_map/ppermute | solution.py:383
  34.9 6.3 %collective-permute-start.7 = (f32[24,1024]{1,0:T(8,128)S(1)}, f32[24,1024]{1,0:T(8,128)S(1)}, u32[]{:S(2)}, u32[]{:S(2)}) collective-permute-start(f32[24,1024]{1,0:T(8,128)S(1)} %fusion), channel_id=1, source_target_pairs={{0,24},{8,16},{16,8},{24,0},{32,56},{40,48},{48,40},{56,32},{64,88... | collective-permute-start | bytes 294920 | tf_op jit(solution)/shard_map/ppermute | solution.py:340
  41.3 3.5 %collective-permute-done.7 = f32[24,1024]{1,0:T(8,128)S(1)} collective-permute-done((f32[24,1024]{1,0:T(8,128)S(1)}, f32[24,1024]{1,0:T(8,128)S(1)}, u32[]{:S(2)}, u32[]{:S(2)}) %collective-permute-start.7) | collective-permute-done | bytes 98336 | tf_op jit(solution)/shard_map/ppermute | solution.py:340
  44.8 0.1 collective-permute-start.8
  44.9 4.8 %collective-permute-done.8 = f32[24,1024]{1,0:T(8,128)S(1)} collective-permute-done((f32[24,1024]{1,0:T(8,128)S(1)}, f32[24,1024]{1,0:T(8,128)S(1)}, u32[]{:S(2)}, u32[]{:S(2)}) %collective-permute-start.8) | collective-permute-done | bytes 98336 | tf_op jit(solution)/shard_map/ppermute | solution.py:340
  49.7 0.1 collective-permute-start.9
  49.8 5.8 %collective-permute-done.9 = f32[24,1024]{1,0:T(8,128)S(1)} collective-permute-done((f32[24,1024]{1,0:T(8,128)S(1)}, f32[24,1024]{1,0:T(8,128)S(1)}, u32[]{:S(2)}, u32[]{:S(2)}) %collective-permute-start.9) | collective-permute-done | bytes 98336 | tf_op jit(solution)/shard_map/ppermute | solution.py:340
  55.6 0.1 collective-permute-start.12
  55.7 2.0 %collective-permute-start.11 = (bf16[4,384,256]{2,1,0:T(8,128)(2,1)S(1)}, bf16[4,384,256]{2,1,0:T(8,128)(2,1)S(1)}, u32[]{:S(2)}, u32[]{:S(2)}) collective-permute-start(bf16[4,384,256]{2,1,0:T(8,128)(2,1)S(1)} %pad_maximum_fusion.here), channel_id=1, source_target_pairs={{0,32},{8,40},{16,48},{24,56},{32,64},{40,72},{48,80},{56,88},{64,... | collective-permute-start | bytes 2359304 | tf_op jit(solution)/shard_map/ppermute | solution.py:336
  57.7 3.9 %collective-permute-start.13 = (f32[12,1024]{1,0:T(8,128)S(1)}, f32[12,1024]{1,0:T(8,128)S(1)}, u32[]{:S(2)}, u32[]{:S(2)}) collective-permute-start(f32[12,1024]{1,0:T(8,128)S(1)} %get-tuple-element.59), channel_id=1, source_target_pairs={{0,120},{1,121},{2,122},{3,123},{4,124},{5,125},{6,126},{7,127},{8... | collective-permute-start | bytes 147464 | tf_op jit(solution)/shard_map/ppermute | solution.py:344
  61.6 0.8 collective-permute-start.14
  62.3 16.0 %window_factor.2 = (bf16[512,256]{1,0:T(8,128)(2,1)S(1)}, bf16[512,256]{1,0:T(8,128)(2,1)S(1)}, f32[256,256]{1,0:T(8,128)S(1)}, f32[512,128]{1,0:T(8,128)S(1)}) custom-call(s32[1]{0:T(128)} %bitcast.place, f32[24,1024]{1,0:T(8,128)S(1)} %add.55.lead, bf16[768,256]{1,0:T(8,128)(2,1)S(1)} %pad_maximum_fusion.2.v0, ...), custom_call_target="tpu_custom_call" | custom-call | flops 5120000000 | bytes 51200000 | tf_op jit(solution)/shard_map/window_factor/pallas_call | solution.py:234
  78.5 2.7 %collective-permute-start.16 = (bf16[2,384,256]{2,1,0:T(8,128)(2,1)S(1)}, bf16[2,384,256]{2,1,0:T(8,128)(2,1)S(1)}, u32[]{:S(2)}, u32[]{:S(2)}) collective-permute-start(bf16[2,384,256]{2,1,0:T(8,128)(2,1)S(1)} %slice.59), channel_id=1, source_target_pairs={{0,96},{8,104},{16,112},{24,120},{32,0},{40,8},{48,16},{56,24},{64... | collective-permute-start | bytes 1179656 | tf_op jit(solution)/shard_map/ppermute | solution.py:336
  81.2 8.0 %window_factor.3 = (bf16[256,256]{1,0:T(8,128)(2,1)S(1)}, bf16[256,256]{1,0:T(8,128)(2,1)S(1)}, f32[256,256]{1,0:T(8,128)S(1)}, f32[256,128]{1,0:T(8,128)S(1)}) custom-call(s32[1]{0:T(128)} %bitcast.place, f32[24,1024]{1,0:T(8,128)S(1)} %add.55.lead, bf16[768,256]{1,0:T(8,128)(2,1)S(1)} %pad_maximum_fusion.2.v0, ...), custom_call_target="tpu_custom_call" | custom-call | flops 2560000000 | bytes 25600000 | tf_op jit(solution)/shard_map/window_factor/pallas_call | solution.py:234
  89.2 1.0 %collective-permute-done.15.low = bf16[2,384,256]{2,1,0:T(8,128)(2,1)S(1)} collective-permute-done((bf16[2,384,256]{2,1,0:T(8,128)(2,1)S(1)}, bf16[2,384,256]{2,1,0:T(8,128)(2,1)S(1)}, u32[]{:S(2)}, u32[]{:S(2)}) %collective-permute-start.15) | collective-permute-done | bytes 393248 | tf_op jit(solution)/shard_map/ppermute | solution.py:336
  90.1 5.6 %factor_rows.1 = f32[1,384,6144]{2,1,0:T(8,128)} custom-call(s32[1]{0:T(128)} %bitcast.place, bf16[512,256]{1,0:T(8,128)(2,1)S(1)} %get-tuple-element.49.high0, bf16[512,256]{1,0:T(8,128)(2,1)S(1)} %get-tuple-element.50.low0, f32[512,128]{1,0:T(8,128)S(1)} %get-tuple-element.51.diag0, bf16[256,256]{1,0:T(8,128)(2,1)S(1)} %get-tuple-element.55.high1, ...), custom_call_target="tpu_custom_call" | custom-call | tf_op jit(solution)/shard_map/factor_rows/pallas_call | solution.py:318
  (36 shorter events, 0.4 us)
Async XLA Ops:
  0.0 4.3 %copy-start.4 = (s32[1024,1]{0,1:T(1,128)S(1)}, s32[1024,1]{0,1:T(1,128)}, u32[]{:S(2)}) copy-start(s32[1024,1]{0,1:T(1,128)} %param.10) | copy-start | bytes 12292
  0.0 4.3 %copy-start.3 = (s32[1024]{0:T(1024)S(1)}, s32[1024]{0:T(1024)}, u32[]{:S(2)}) copy-start(s32[1024]{0:T(1024)} %param.11) | copy-start | bytes 12292
  0.0 6.9 %collective-permute-start = (bf16[384,256]{1,0:T(8,128)(2,1)}, bf16[384,256]{1,0:T(8,128)(2,1)S(1)}, u32[]{:S(2)}, u32[]{:S(2)}) collective-permute-start(bf16[384,256]{1,0:T(8,128)(2,1)} %bitcast.9), channel_id=1, source_target_pairs={{0,8},{8,0},{16,24},{24,16},{32,40},{40,32},{48,56},{56,48},{64,72... | collective-permute-start | bytes 589832 | tf_op jit(solution)/shard_map/ppermute | solution.py:340
  1.6 5.3 %copy-start = (bf16[1,384,256]{2,1,0:T(8,128)(2,1)S(1)}, bf16[1,384,256]{2,1,0:T(8,128)(2,1)}, u32[]{:S(2)}) copy-start(bf16[1,384,256]{2,1,0:T(8,128)(2,1)} %param.13) | copy-start | bytes 589828
  2.4 7.6 %copy-start.1 = (f32[4,1024]{1,0:T(4,128)S(1)}, f32[4,1024]{1,0:T(4,128)}, u32[]{:S(2)}) copy-start(f32[4,1024]{1,0:T(4,128)} %scale.1) | copy-start | bytes 49156
  2.4 7.6 %copy-start.2 = (f32[2,1024]{1,0:T(2,128)S(1)}, f32[2,1024]{1,0:T(2,128)}, u32[]{:S(2)}) copy-start(f32[2,1024]{1,0:T(2,128)} %moduli.1) | copy-start | bytes 24580
  6.9 11.3 %collective-permute-start.1 = (bf16[2,384,256]{2,1,0:T(8,128)(2,1)S(1)}, bf16[2,384,256]{2,1,0:T(8,128)(2,1)S(1)}, u32[]{:S(2)}, u32[]{:S(2)}) collective-permute-start(bf16[2,384,256]{2,1,0:T(8,128)(2,1)S(1)} %pad_maximum_fusion.1), channel_id=1, source_target_pairs={{0,24},{8,16},{16,8},{24,0},{32,56},{40,48},{48,40},{56,32},{64,88... | collective-permute-start | bytes 1179656 | tf_op jit(solution)/shard_map/ppermute | solution.py:340
  18.3 7.0 %collective-permute-start.3 = (f32[16,1024]{1,0:T(8,128)S(1)}, f32[16,1024]{1,0:T(8,128)S(1)}, u32[]{:S(2)}, u32[]{:S(2)}) collective-permute-start(f32[16,1024]{1,0:T(8,128)S(1)} %get-tuple-element.42), channel_id=1, source_target_pairs={{0,126},{1,127},{2,0},{3,1},{4,2},{5,3},{6,4},{7,5},{8,6},{9,7},{1... | collective-permute-start | bytes 196616 | tf_op jit(solution)/shard_map/ppermute | solution.py:344
  18.8 6.5 %collective-permute-start.4 = (f32[16,1024]{1,0:T(8,128)S(1)}, f32[16,1024]{1,0:T(8,128)S(1)}, u32[]{:S(2)}, u32[]{:S(2)}) collective-permute-start(f32[16,1024]{1,0:T(8,128)S(1)} %get-tuple-element.43), channel_id=1, source_target_pairs={{0,125},{1,126},{2,127},{3,0},{4,1},{5,2},{6,3},{7,4},{8,5},{9,6},... | collective-permute-start | bytes 196616 | tf_op jit(solution)/shard_map/ppermute | solution.py:344
  18.8 6.5 %collective-permute-start.2 = (f32[40,1024]{1,0:T(8,128)S(1)}, f32[40,1024]{1,0:T(8,128)S(1)}, u32[]{:S(2)}, u32[]{:S(2)}) collective-permute-start(f32[40,1024]{1,0:T(8,128)S(1)} %get-tuple-element.41), channel_id=1, source_target_pairs={{0,127},{1,0},{2,1},{3,2},{4,3},{5,4},{6,5},{7,6},{8,7},{9,8},{10,... | collective-permute-start | bytes 491528 | tf_op jit(solution)/shard_map/ppermute | solution.py:344
  18.9 12.4 %collective-permute-start.6 = (bf16[768,256]{1,0:T(8,128)(2,1)S(1)}, bf16[768,256]{1,0:T(8,128)(2,1)S(1)}, u32[]{:S(2)}, u32[]{:S(2)}) collective-permute-start(bf16[768,256]{1,0:T(8,128)(2,1)S(1)} %pad_maximum_fusion.2.v0), channel_id=1, source_target_pairs={{0,32},{8,40},{16,48},{24,56},{1,33},{9,41},{17,49},{25,57},{2,34}... | collective-permute-start | bytes 1179656 | tf_op jit(solution)/shard_map/ppermute | solution.py:336
  25.4 4.7 %collective-permute-start.5 = (f32[24,1024]{1,0:T(8,128)S(1)}, f32[24,1024]{1,0:T(8,128)S(1)}, u32[]{:S(2)}, u32[]{:S(2)}) collective-permute-start(f32[24,1024]{1,0:T(8,128)S(1)} %pad_maximum_fusion.3), channel_id=1, source_target_pairs={{0,8},{8,0},{16,24},{24,16},{32,40},{40,32},{48,56},{56,48},{64,72... | collective-permute-start | bytes 294920 | tf_op jit(solution)/shard_map/ppermute | solution.py:340
  31.4 24.2 %collective-permute-start.10 = (bf16[768,256]{1,0:T(8,128)(2,1)S(1)}, bf16[768,256]{1,0:T(8,128)(2,1)S(1)}, u32[]{:S(2)}, u32[]{:S(2)}) collective-permute-start(bf16[768,256]{1,0:T(8,128)(2,1)S(1)} %broadcast_select_fusion), channel_id=1, source_target_pairs={{0,96},{8,104},{16,112},{24,120},{32,64},{40,72},{48,80},{56,88},{... | collective-permute-start | bytes 1179656 | tf_op jit(solution)/shard_map/ppermute | solution.py:383
  34.9 9.8 %collective-permute-start.7 = (f32[24,1024]{1,0:T(8,128)S(1)}, f32[24,1024]{1,0:T(8,128)S(1)}, u32[]{:S(2)}, u32[]{:S(2)}) collective-permute-start(f32[24,1024]{1,0:T(8,128)S(1)} %fusion), channel_id=1, source_target_pairs={{0,24},{8,16},{16,8},{24,0},{32,56},{40,48},{48,40},{56,32},{64,88... | collective-permute-start | bytes 294920 | tf_op jit(solution)/shard_map/ppermute | solution.py:340
  44.8 4.9 %collective-permute-start.8 = (f32[24,1024]{1,0:T(8,128)S(1)}, f32[24,1024]{1,0:T(8,128)S(1)}, u32[]{:S(2)}, u32[]{:S(2)}) collective-permute-start(f32[24,1024]{1,0:T(8,128)S(1)} %add.53), channel_id=1, source_target_pairs={{0,32},{8,40},{16,48},{24,56},{32,0},{40,8},{48,16},{56,24},{64,96... | collective-permute-start | bytes 294920 | tf_op jit(solution)/shard_map/ppermute | solution.py:340
  49.7 5.9 %collective-permute-start.9 = (f32[24,1024]{1,0:T(8,128)S(1)}, f32[24,1024]{1,0:T(8,128)S(1)}, u32[]{:S(2)}, u32[]{:S(2)}) collective-permute-start(f32[24,1024]{1,0:T(8,128)S(1)} %add.54), channel_id=1, source_target_pairs={{0,96},{8,104},{16,112},{24,120},{32,64},{40,72},{48,80},{56,88},{... | collective-permute-start | bytes 294920 | tf_op jit(solution)/shard_map/ppermute | solution.py:340
  55.6 22.8 %collective-permute-start.12 = (bf16[4,384,256]{2,1,0:T(8,128)(2,1)S(1)}, bf16[4,384,256]{2,1,0:T(8,128)(2,1)S(1)}, u32[]{:S(2)}, u32[]{:S(2)}) collective-permute-start(bf16[4,384,256]{2,1,0:T(8,128)(2,1)S(1)} %pad_maximum_fusion.here), channel_id=1, source_target_pairs={{0,96},{8,104},{16,112},{24,120},{32,0},{40,8},{48,16},{56,24},{64... | collective-permute-start | bytes 2359304 | tf_op jit(solution)/shard_map/ppermute | solution.py:336
  55.7 22.7 %collective-permute-start.11 = (bf16[4,384,256]{2,1,0:T(8,128)(2,1)S(1)}, bf16[4,384,256]{2,1,0:T(8,128)(2,1)S(1)}, u32[]{:S(2)}, u32[]{:S(2)}) collective-permute-start(bf16[4,384,256]{2,1,0:T(8,128)(2,1)S(1)} %pad_maximum_fusion.here), channel_id=1, source_target_pairs={{0,32},{8,40},{16,48},{24,56},{32,64},{40,72},{48,80},{56,88},{64,... | collective-permute-start | bytes 2359304 | tf_op jit(solution)/shard_map/ppermute | solution.py:336
  57.7 23.4 %collective-permute-start.13 = (f32[12,1024]{1,0:T(8,128)S(1)}, f32[12,1024]{1,0:T(8,128)S(1)}, u32[]{:S(2)}, u32[]{:S(2)}) collective-permute-start(f32[12,1024]{1,0:T(8,128)S(1)} %get-tuple-element.59), channel_id=1, source_target_pairs={{0,120},{1,121},{2,122},{3,123},{4,124},{5,125},{6,126},{7,127},{8... | collective-permute-start | bytes 147464 | tf_op jit(solution)/shard_map/ppermute | solution.py:344
  61.6 19.6 %collective-permute-start.14 = (f32[12,1024]{1,0:T(8,128)S(1)}, f32[12,1024]{1,0:T(8,128)S(1)}, u32[]{:S(2)}, u32[]{:S(2)}) collective-permute-start(f32[12,1024]{1,0:T(8,128)S(1)} %get-tuple-element.60), channel_id=1, source_target_pairs={{0,64},{1,65},{2,66},{3,67},{4,68},{5,69},{6,70},{7,71},{8,72},{9,... | collective-permute-start | bytes 147464 | tf_op jit(solution)/shard_map/ppermute | solution.py:344
  78.5 10.7 %collective-permute-start.16 = (bf16[2,384,256]{2,1,0:T(8,128)(2,1)S(1)}, bf16[2,384,256]{2,1,0:T(8,128)(2,1)S(1)}, u32[]{:S(2)}, u32[]{:S(2)}) collective-permute-start(bf16[2,384,256]{2,1,0:T(8,128)(2,1)S(1)} %slice.59), channel_id=1, source_target_pairs={{0,96},{8,104},{16,112},{24,120},{32,0},{40,8},{48,16},{56,24},{64... | collective-permute-start | bytes 1179656 | tf_op jit(solution)/shard_map/ppermute | solution.py:336
  81.1 9.0 %collective-permute-start.15 = (bf16[2,384,256]{2,1,0:T(8,128)(2,1)S(1)}, bf16[2,384,256]{2,1,0:T(8,128)(2,1)S(1)}, u32[]{:S(2)}, u32[]{:S(2)}) collective-permute-start(bf16[2,384,256]{2,1,0:T(8,128)(2,1)S(1)} %slice.58), channel_id=1, source_target_pairs={{0,32},{8,40},{16,48},{24,56},{32,64},{40,72},{48,80},{56,88},{64,... | collective-permute-start | bytes 1179656 | tf_op jit(solution)/shard_map/ppermute | solution.py:336

commit v3 on v2

v3 whole, which is shorter than its diff:
```python
import functools

import jax
import jax.numpy as jnp
from jax import lax
from jax.experimental import pallas as pl
from jax.experimental.pallas import tpu as pltpu
from jax.sharding import PartitionSpec as P

F32 = jnp.float32
BF16 = jnp.bfloat16
W = 384
WINDOW = 768
PARTS = ((0, 512), (512, 256))
RANK = 256
SLOTS = 12
TILE = 512
CHUNK = 256
ACROSS = (0, 1, 3, 2)
BINS = {0: 0, 8: 12, 64: 24, 1: 40, 9: 52, 65: 64, 2: 80, 3: 96}
BIN_ROWS = 112


def split3(x):
    a = x.astype(BF16); r = x - a.astype(F32)
    b = r.astype(BF16); c = (r - b.astype(F32)).astype(BF16)
    return a, b, c


def dot_nn(a, b): return lax.dot_general(a, b, (((1,), (0,)), ((), ())), preferred_element_type=F32)
def dot_nt(a, b): return lax.dot_general(a, b, (((1,), (1,)), ((), ())), preferred_element_type=F32)


def product_tn(x, y):
    x1, x2, x3 = split3(x)
    y1, y2, y3 = split3(y)
    left = jnp.concatenate([x1, x1, x2, x1, x2, x3], axis=0)
    right = jnp.concatenate([y1, y2, y1, y3, y2, y1], axis=0)
    return lax.dot_general(left, right, (((0,), (0,)), ((), ())), preferred_element_type=F32)


def eliminate(rows, first):
    sub = lax.broadcasted_iota(jnp.int32, (8, 128), 0)
    n = len(rows)
    spread = lambda x, at: jnp.broadcast_to(x[at:at + 1, :], (8, 128))
    cols = {}
    for k in range(8 * n):
        for q in range(k // 8, n):
            cols[q, k] = jnp.broadcast_to(rows[q][0][:, first + k:first + k + 1], (8, 128))
    for k in range(8 * n):
        t, u = k // 8, k % 8
        rs = lax.rsqrt(spread(cols[t, k], u))
        f = {q: cols[q, k] * rs for q in range(t, n)}
        for m in range(k + 1, 8 * n):
            sm = spread(f[m // 8], m % 8)
            for q in range(m // 8, n):
                cols[q, m] = cols[q, m] - f[q] * sm
        fm = jnp.where(sub > u, f[t], 0.0)
        for h in range(len(rows[t])):
            r = spread(rows[t][h], u) * rs
            rows[t][h] = jnp.where(sub == u, r, rows[t][h] - fm * r)
            for q in range(t + 1, n):
                rows[q][h] = rows[q][h] - f[q] * r
    return rows


def unpack_tiles(packed, out_ref):
    n = packed.shape[0]
    lane = lax.broadcasted_iota(jnp.int32, (n, 128), 1)
    tile = lax.broadcasted_iota(jnp.int32, (n, 128), 0) % 4
    here = lane // 32 == tile
    entry = lane % 32
    for g in range(4):
        x = packed[:, 128 * g:128 * g + 128]
        turned = [x] + [pltpu.roll(x, 32 * r, 1) for r in range(1, 4)]
        for u in range(4):
            slot = turned[(0 - u) % 4]
            for v in range(1, 4):
                slot = jnp.where(tile == v, turned[(v - u) % 4], slot)
            p = 4 * g + u
            rows = ((30, 30), (31, 30)) if p == 15 else ((p, p), (29 - p, -1))
            for i, shift in rows:
                keep = here & (entry >= i) & (entry < (30 if i < 30 else i + 1))
                moved = pltpu.roll(slot, shift % 128, 1) if shift % 128 else slot
                out_ref[pl.ds(i, n, stride=32), :] = jnp.where(keep, moved, 0.0)


def stiffness_kernel(begin, strain, small, code, *refs):
    outs = refs[:-7] if begin == 0 else refs[1:-7]
    plain, weighted, sums, total, bins, data, sems = refs[-7:]
    steps = data.shape[0]
    copies = [
        pltpu.make_async_copy(strain.at[:, :, :, pl.ds((begin + n) * CHUNK, CHUNK)], data.at[n], sems.at[n])
        for n in range(steps)
    ]
    for copy in copies:
        copy.start()
    sums[...] = jnp.zeros_like(sums)
    if begin:
        total[...] = refs[0][...]
    else:
        total[...] = jnp.zeros_like(total)
        entry = lax.broadcasted_iota(jnp.int32, (W, TILE), 1)
        slot, at = entry // 32, entry % 32
        diagonal = jnp.where(slot == 15, 30 + at, jnp.where(at == 0, slot, jnp.where(at == 30 - slot, 29 - slot, -1)))
        spread = (diagonal == lax.broadcasted_iota(jnp.int32, (W, TILE), 0) % 32).astype(F32).astype(BF16)
        own = lax.broadcasted_iota(jnp.int32, (16, W), 1) // 32 == lax.broadcasted_iota(jnp.int32, (16, W), 0)
        mass = small[6:7, :W]
        total[:16, :] = sum(dot_nn(part, spread) for part in split3(jnp.where(own, mass, 0.0)))
    device = lax.axis_index("cand") * lax.axis_size("dom") + lax.axis_index("dom")
    offset = (device - code[...] // 16) & 127
    start = jnp.zeros_like(offset)
    for o, first in BINS.items():
        start = jnp.where(offset == o, first, start)
    bins[...] = start + code[...] % 16
    sub = lax.broadcasted_iota(jnp.int32, (8, 128), 0)

    def both(x):
        return jnp.concatenate([x[:, :128], x[:, 128:]], axis=0)

    def fold(a, b, bit):
        even = (sub & bit) == 0
        return jnp.where(even, a, pltpu.roll(b, bit, 0)) + jnp.where(even, pltpu.roll(a, 8 - bit, 0), b)

    def one_step(step, carry):
        for n, copy in enumerate(copies):
            @pl.when(step == n)
            def _():
                copy.wait()

        lanes = pl.ds(pl.multiple_of((begin + step) * CHUNK, CHUNK), CHUNK)
        weight = small[0:4, lanes]
        shear = both(weight * small[4:5, lanes])
        bulk = both(weight * small[5:6, lanes])
        for s in range(6):
            b = data[step, s].astype(F32)
            plain[s, :, 0:4, :] = b[:, :, :128]
            plain[s, :, 4:8, :] = b[:, :, 128:]
        for i in range(30):
            b = [plain[s, i] for s in range(6)]
            diverge = b[0] + b[1] + b[2]
            plain[6, i] = diverge
            weighted[6, i] = diverge * bulk
            for s in range(6):
                weighted[s, i] = b[s] * shear

        for first in range(0, 15, 2):
            slots = [p for p in (first, first + 1) if p < 15]
            owners = sorted({i for p in slots for i in (p, 29 - p)})
            rows = {i: [plain[s, i] for s in range(7)] for i in owners}
            ready = {(p, 31): None for p in slots}
            for col in range(first, 30):
                right = [weighted[s, col] for s in range(7)]
                for p in slots:
                    for i, l in ((p, col - p), (29 - p, col + 1)):
                        if col < i:
                            continue
                        products = [rows[i][s] * right[s] for s in range(7)]
                        value = products[0]
                        for product in products[1:]:
                            value = value + product
                        ready[p, l] = value
                        group = [(p, 8 * (l // 8) + m) for m in range(8)]
                        if not all(key in ready for key in group):
                            continue
                        eight = [ready.pop(key) for key in group]
                        eight = [jnp.zeros((8, 128), F32) if e is None else e for e in eight]
                        fours = []
                        for h in range(2):
                            a, b, c, d = eight[4 * h:4 * h + 4]
                            fours.append(fold(fold(a, b, 1), fold(c, d, 1), 2))
                        low, high = fours
                        r = 32 * p + 8 * (l // 8)
                        sums[r:r + 8, :128] = jnp.where(sub < 4, low, pltpu.roll(high, 4, 0))
                        sums[r:r + 8, 128:] = jnp.where(sub < 4, pltpu.roll(low, 4, 0), high)
        values = sums[...]
        high = values.astype(BF16)
        low = (values - high.astype(F32)).astype(BF16)
        chosen = lax.broadcasted_iota(jnp.int32, (BIN_ROWS, CHUNK), 0) == bins[:, lanes]
        chosen = chosen.astype(F32).astype(BF16)
        total[...] += dot_nt(chosen, high) + dot_nt(chosen, low)
        return carry

    lax.fori_loop(0, steps, one_step, 0)
    at = 0
    for out in outs:
        out[...] = total[at:at + out.shape[0], :]
        at += out.shape[0]


def stiffness_tiles(begin, steps, strain, small, code, total, outs):
    vmem = pl.BlockSpec(memory_space=pltpu.VMEM)
    return pl.pallas_call(
        functools.partial(stiffness_kernel, begin),
        in_specs=[pl.BlockSpec(memory_space=pltpu.HBM)] + [vmem] * (2 + len(total)),
        out_specs=[vmem] * len(outs),
        out_shape=[jax.ShapeDtypeStruct((r, TILE), F32) for r in outs],
        scratch_shapes=[
            pltpu.VMEM((7, 30, 8, 128), F32),
            pltpu.VMEM((7, 30, 8, 128), F32),
            pltpu.VMEM((TILE, CHUNK), F32),
            pltpu.VMEM((BIN_ROWS, TILE), F32),
            pltpu.VMEM(code.shape, jnp.int32),
            pltpu.VMEM((steps, 6, 30, 4, CHUNK), BF16),
            pltpu.SemaphoreType.DMA((steps,)),
        ],
        cost_estimate=pl.CostEstimate(flops=5 * 10**9, bytes_accessed=15 * 10**6, transcendentals=0),
        compiler_params=pltpu.CompilerParams(vmem_limit_bytes=32 * 2**20),
        name="stiffness_tiles",
    )(strain, small, code, *total)


def mirror(block):
    row = lax.broadcasted_iota(jnp.int32, block.shape, 0)
    col = lax.broadcasted_iota(jnp.int32, block.shape, 1)
    return jnp.where(row <= col, block, block.T)


def factor_window(diag, v_ref, h_ref, m_ref, work):
    square = lambda n, dim: lax.broadcasted_iota(jnp.int32, (n, n), dim)
    upper = square(128, 0) <= square(128, 1)

    def block(j, carry):
        at = pl.ds(pl.multiple_of(j * 128, 128), 128)
        v = v_ref[at, :]
        m1, m2, m3 = split3(m_ref[...])
        p = dot_nn(v, m1) + (dot_nn(v, m2) + dot_nn(v, m3))
        p1, p2, p3 = split3(p)
        work[:, :128] = mirror(diag[at, :]) + (dot_nt(p1, v) + (dot_nt(p2, v) + dot_nt(p3, v)))
        work[:, 128:] = p
        for s in range(4):
            at_row = lambda q: slice(32 * s + 8 * q, 32 * s + 8 * q + 8)
            rows = [[work[at_row(q), 128 * h:128 * h + 128] for h in range(3)] for q in range(4)]
            rows = eliminate(rows, 32 * s)
            for q in range(4):
                for h in range(3):
                    work[at_row(q), 128 * h:128 * h + 128] = rows[q][h]
            if s < 3:
                done = work[32 * s:32 * s + 32, :]
                change = product_tn(done[:, :128], done)
                work[32 * s + 32:, :] = work[32 * s + 32:, :] - change[32 * s + 32:, :]
        h = work[:, 128:]
        h_ref[at, :] = h
        diag[at, :] = jnp.where(upper, work[:, :128], 0.0).T
        m_ref[...] = m_ref[...] - product_tn(h, h)
        return carry

    lax.fori_loop(0, diag.shape[0] // 128, block, 0)


def window_kernel(part, lead, mine, beside, across, *refs):
    high_ref, low_ref, m_ref, diag, v_ref, h_ref, work = refs[-7:]
    first, size = PARTS[part]
    y = lax.rem(lax.axis_index("cand"), 4)
    for b, (own, other) in enumerate(((mine, beside), (beside, mine))):
        begin, end = max(first, W * b), min(first + size, W * b + W)
        if begin >= end:
            continue
        to = slice(begin - first, end - first)
        for n, holder in enumerate((own, other)):
            @pl.when(y == n)
            def _():
                v_ref[to, :] = holder[begin - W * b:end - W * b, :] * 0.0625

        @pl.when(y >= 2)
        def _():
            v_ref[to, :] = across[begin:end, :] * 0.0625

    if part:
        m_ref[...] = refs[0][...]
    else:
        square = lambda dim: lax.broadcasted_iota(jnp.int32, (RANK, RANK), dim)
        m_ref[...] = (square(0) == square(1)).astype(F32)
    unpack_tiles(lead[first // 32:(first + size) // 32, :], diag)
    factor_window(diag, v_ref, h_ref, m_ref, work)
    h = h_ref[...]
    high = h.astype(BF16)
    high_ref[...] = high
    low_ref[...] = (h - high.astype(F32)).astype(BF16)


def window_factor(part, lead, v, m):
    vmem = pl.BlockSpec(memory_space=pltpu.VMEM)
    size = PARTS[part][1]
    return pl.pallas_call(
        functools.partial(window_kernel, part),
        in_specs=[vmem] * (4 + len(m)),
        out_specs=[vmem] * 4,
        out_shape=[
            jax.ShapeDtypeStruct((size, RANK), BF16),
            jax.ShapeDtypeStruct((size, RANK), BF16),
            jax.ShapeDtypeStruct((RANK, RANK), F32),
            jax.ShapeDtypeStruct((size, 128), F32),
        ],
        scratch_shapes=[
            pltpu.VMEM((size, RANK), BF16),
            pltpu.VMEM((size, RANK), F32),
            pltpu.VMEM((128, 128 + RANK), F32),
        ],
        cost_estimate=pl.CostEstimate(flops=size * 10**7, bytes_accessed=size * 10**5, transcendentals=0),
        compiler_params=pltpu.CompilerParams(vmem_limit_bytes=32 * 2**20),
        name="window_factor",
    )(lead, *v, *m)


def rows_kernel(high0, low0, diag0, high1, low1, m_ref, diag1, kept, near, half, own, here, before, after, low, high, out, *scratch):
    own_diag, panel, blocks, sems = scratch
    cand = lax.axis_index("cand")
    x, y = cand // 4, lax.rem(cand, 4)
    v_own = own[...] * 0.0625
    split = PARTS[1][0]
    panel[:, :split] = dot_nt(v_own, high0[...]) + dot_nt(v_own, low0[...])
    panel[:, split:] = dot_nt(v_own, high1[...]) + dot_nt(v_own, low1[...])
    for n in range(2):
        @pl.when(cand == n)
        def _():
            row = lax.broadcasted_iota(jnp.int32, (W, WINDOW), 0) // 128 + 3 * n
            col = lax.broadcasted_iota(jnp.int32, (W, WINDOW), 1) // 128
            panel[...] = jnp.where(row > col, panel[...], 0.0)
            for a in range(3):
                at = W * n + 128 * a
                diag = diag0[at:at + 128, :] if at < split else diag1[at - split:at - split + 128, :]
                panel[128 * a:128 * a + 128, at:at + 128] = diag

    panel_copy = pltpu.make_async_copy(panel, out.at[0, :, pl.ds(0, WINDOW)], sems.at[16])
    panel_copy.start()
    unpack_tiles(kept[...] + near[...] + half[...], own_diag)
    m1, m2, m3 = split3(m_ref[...])
    q = (dot_nn(v_own, m1) + (dot_nn(v_own, m2) + dot_nn(v_own, m3))) * 0.0625
    q = jnp.where(cand < 2, 0.0, q)
    q1 = q.astype(BF16)
    q2 = (q - q1.astype(F32)).astype(BF16)
    stores = []
    for n, pieces in enumerate((here, before, after, (low, high))):
        column_y = lax.rem(y + (0, 3, 1, 2)[n], 4)
        for pair in range(2):
            v = pieces[pair][...] if n == 3 else pieces[2 * pair:2 * pair + 2]
            v = v.reshape(2 * W, RANK)
            slot = 2 * n + pair
            blocks[slot] = dot_nt(q1, v) + dot_nt(q2, v)
            if slot == 0:
                @pl.when(cand >= 2)
                def _():
                    for a in range(3):
                        at = slice(128 * a, 128 * a + 128)
                        blocks[0, at, at] += mirror(own_diag[at, :])

            for m in range(2):
                column = 4 * (x ^ ACROSS[2 * pair + m]) + column_y
                copy = pltpu.make_async_copy(
                    blocks.at[slot, :, pl.ds(W * m, W)],
                    out.at[0, :, pl.ds(pl.multiple_of(column * W, 128), W)],
                    sems.at[2 * slot + m],
                )
                stores.append((column, copy))

                @pl.when(column >= 2)
                def _():
                    copy.start()
    panel_copy.wait()
    for column, copy in stores:
        @pl.when(column >= 2)
        def _():
            copy.wait()


def factor_rows(*operands):
    vmem = pl.BlockSpec(memory_space=pltpu.VMEM)
    return pl.pallas_call(
        rows_kernel,
        in_specs=[vmem] * len(operands),
        out_specs=pl.BlockSpec(memory_space=pltpu.HBM),
        out_shape=jax.ShapeDtypeStruct((1, W, 16 * W), F32),
        scratch_shapes=[
            pltpu.VMEM((W, 128), F32),
            pltpu.VMEM((W, WINDOW), F32),
            pltpu.VMEM((8, W, 2 * W), F32),
            pltpu.SemaphoreType.DMA((17,)),
        ],
        compiler_params=pltpu.CompilerParams(vmem_limit_bytes=40 * 2**20),
        name="factor_rows",
    )(*operands)


def move_y(value, shift):
    return lax.ppermute(value, "cand", [(4 * x + y, 4 * x + (y + shift) % 4) for x in range(4) for y in range(4)])


def swap(value, bits):
    return lax.ppermute(value, "cand", [(i, i ^ bits) for i in range(16)])


def move_back(value, offset):
    return lax.ppermute(value, ("cand", "dom"), [(i, (i - offset) % 128) for i in range(128)])


def local(strain_ops, elem_scale, moduli, elem_block, elem_slot, mass, updates):
    cand = lax.axis_index("cand")
    x, y = cand // 4, cand % 4
    own = updates[0]

    small, row = 0.0, 0
    for part in (elem_scale, moduli, mass):
        rows, width = part.shape
        small = small + lax.pad(part, F32(0), ((row, 8 - row - rows, 0), (0, elem_scale.shape[1] - width, 0)))
        row += rows
    code = (elem_block[:, 0] * 16 + elem_slot)[None, :]
    strain = jnp.transpose(strain_ops, (1, 2, 0, 3))
    steps = strain.shape[3] // CHUNK

    beside = swap(own, 4)
    total = stiffness_tiles(0, steps // 2, strain, small, code, (), (BIN_ROWS,))
    total, beside = lax.optimization_barrier((total, beside))
    here = jnp.stack([own, beside])
    here = jnp.concatenate([here, swap(here, 12)])
    keep, far, two, three = stiffness_tiles(steps // 2, steps // 2, strain, small, code, total, (40, 40, 16, 16))

    far = move_back(far, 1)
    two = move_back(two, 2)
    three = move_back(three, 3)
    far, two, three, here = lax.optimization_barrier((far, two, three, here))
    kept = keep[:12] + far[:12] + two[:12] + three[:12]
    near = keep[12:24] + far[12:24]
    half = keep[24:36] + far[24:36]
    zero = jnp.zeros_like(kept)
    pick = lambda c: jnp.where(cand == c, kept, jnp.where(cand == c + 1, near, jnp.where(cand == c + 8, half, zero)))
    lead = jnp.concatenate([pick(0), pick(1)], axis=0)
    mine = functools.reduce(lambda u, n: jnp.where(x == ACROSS[n], here[n], u), range(1, 4), here[0])
    paired = swap(mine, 1)
    lead = lead + swap(lead, 4)
    lead = lead + swap(lead, 12)
    lead, paired, near, half = lax.optimization_barrier((lead, paired, near, half))
    near, half = move_back(near, 8), move_back(half, 64)
    across = swap(jnp.where(y == 0, jnp.concatenate([mine, paired]), jnp.concatenate([paired, mine])), 3)
    lead = lead + swap(lead, 1)
    lead = lead + swap(lead, 3)
    lead, across, here, near, half = lax.optimization_barrier((lead, across, here, near, half))

    before, after = move_y(here, 1), move_y(here, 3)
    window = (mine, paired, across)
    high0, low0, m, diag0 = window_factor(0, lead, window, ())
    m, before, after = lax.optimization_barrier((m, before, after))
    low, high = move_y(before[:2], 1), move_y(after[2:], 3)
    high1, low1, m, diag1 = window_factor(1, lead, window, (m,))
    return factor_rows(high0, low0, diag0, high1, low1, m, diag1, kept, near, half, own, here, before, after, low, high)


def solution(mesh):
    placed = (
        P(None, None, None, ("cand", "dom")),
        P(None, ("cand", "dom")),
        P(None, ("cand", "dom")),
        P(("cand", "dom"), None),
        P(("cand", "dom")),
        P("dom", "cand"),
        P("dom", "cand", None),
    )
    return jax.shard_map(
        local, mesh=mesh, in_specs=placed, out_specs=P("dom", "cand", None), check_vma=False
    )
```

time: 96.1 us -> 86 us (0.89)
  starting transfers between devices: 28.4 us -> 22.5 us
  waiting for transfers between devices: 27 us -> 21.3 us
  other arithmetic: 1.17 us -> 2.54 us
    ppermute x6 -> x4, starting transfers between devices: 11.7 us -> 4.12 us  [move_y(): lax.ppermute(value, 'cand', [(4 * x + y, 4 * x + (y + shift) % 4) for x i...]
    ppermute x6 -> x8, waiting for transfers between devices: 21.8 us -> 16.1 us  [swap(): return lax.ppermute(value, 'cand', [(i, i ^ bits) for i in range(16)])]
    ppermute x5, waiting for transfers between devices: 2.99 us -> 5.14 us  [move_back(): lax.ppermute(value, ('cand', 'dom'), [(i, (i - offset) % 128) for i in ra...]
    ppermute x6 -> x4, waiting for transfers between devices: 2.2 us -> 0.12 us  [move_y(): lax.ppermute(value, 'cand', [(4 * x + y, 4 * x + (y + shift) % 4) for x i...]
    add x2, other arithmetic: 0.02 us -> 1.45 us  [the longest x1 0.76 us: local(): small + lax.pad(part, F32(0), ((row, 8 - row - rows, 0), (0, elem_scale.s...]
    ppermute x6 -> x8, starting transfers between devices: 11.6 us -> 13 us  [swap(): return lax.ppermute(value, 'cand', [(i, i ^ bits) for i in range(16)])]
    pallas_call x4 -> x5, Pallas kernels: 37 us -> 36.9 us  [the longest x2 24.2 us: window_factor(): pl.pallas_call(functools.partial(window_kernel, part), in_specs=[vmem] *...]
  transfers between devices with their start and end apart: 17 -> 17, of which waited for: 9 -> 8; matrix products, arithmetic and copies ran while one was open for 3% -> 3% of each run, Pallas kernels for 33% -> 37%
where the time goes in v3:
time: 86 us; the launch traced here: 85.1 us
  Pallas kernels  36.9 us (43%)
  starting transfers between devices  22.5 us (26%)
  waiting for transfers between devices  21.3 us (25%)
  other arithmetic  2.54 us (3%)
  local copies, waits for them, and re-layouts  1.43 us (2%)
    pallas_call x2, Pallas kernels, window_factor(): pl.pallas_call(functools.partial(window_kernel, part), in_specs=[vmem] *...  24.2 us
    ppermute x8, waiting for transfers between devices, swap(): return lax.ppermute(value, 'cand', [(i, i ^ bits) for i in range(16)])  16.1 us
    ppermute x8, starting transfers between devices, swap(): return lax.ppermute(value, 'cand', [(i, i ^ bits) for i in range(16)])  13 us
    pallas_call x2, Pallas kernels, stiffness_tiles(): pl.pallas_call(functools.partial(stiffness_kernel, begin), in_specs=[pl.B...  7.24 us
    pallas_call x1, Pallas kernels, factor_rows(): pl.pallas_call(rows_kernel, in_specs=[vmem] * len(operands), out_specs=pl...  5.45 us
    ppermute x5, starting transfers between devices, move_back(): lax.ppermute(value, ('cand', 'dom'), [(i, (i - offset) % 128) for i in ra...  5.41 us
    ppermute x5, waiting for transfers between devices, move_back(): lax.ppermute(value, ('cand', 'dom'), [(i, (i - offset) % 128) for i in ra...  5.14 us
    ppermute x4, starting transfers between devices, move_y(): lax.ppermute(value, 'cand', [(4 * x + y, 4 * x + (y + shift) % 4) for x i...  4.12 us
  transfers between devices with their start and end apart: 17, of which 8 were waited for; matrix products, arithmetic and copies ran while one was open for 3% of the time, Pallas kernels for 37%

profile of v3, /device:TPU:96, one launch (start us, length us, event | category | flops | bytes accessed | tf_op | source)
XLA Modules:
  0.0 85.1 jit_solution(8059738766777488119)
XLA Ops:
  0.0 1.5 %collective-permute-start = (bf16[384,256]{1,0:T(8,128)(2,1)}, bf16[384,256]{1,0:T(8,128)(2,1)S(1)}, u32[]{:S(2)}, u32[]{:S(2)}) collective-permute-start(bf16[384,256]{1,0:T(8,128)(2,1)} %bitcast.7), channel_id=1, source_target_pairs={{0,32},{8,40},{16,48},{24,56},{32,0},{40,8},{48,16},{56,24},{64,96... | collective-permute-start | bytes 589832 | tf_op jit(solution)/shard_map/ppermute | solution.py:390
  1.5 0.7 broadcast_multiply_fusion
  2.2 0.7 add.49
  2.9 0.8 pad_add_fusion.small
  3.6 0.0 copy-start.1
  3.7 1.4 %copy-done.1 = bf16[4,6,30,1024]{3,0,2,1:T(4,128)(2,1)S(1)} copy-done((bf16[4,6,30,1024]{3,0,2,1:T(4,128)(2,1)S(1)}, bf16[4,6,30,1024]{3,0,2,1:T(4,128)(2,1)}, u32[]{:S(2)}) %copy-start.1) | copy-done | bytes 1474584
  5.0 3.8 %stiffness_tiles.2.refs_0_ = f32[112,512]{1,0:T(8,128)S(1)} custom-call(bf16[6,30,4,1024]{3,2,1,0:T(4,128)(2,1)S(1)} %bitcast.11, f32[8,1024]{1,0:T(8,128)S(1)} %pad_add_fusion.small, s32[1,1024]{1,0:T(1,128)S(1)} %bitcast.9), custom_call_target="tpu_custom_call" | custom-call | flops 5000000000 | bytes 15000000 | tf_op jit(solution)/shard_map/stiffness_tiles/pallas_call | solution.py:193
  8.9 2.2 %collective-permute-start.4 = (bf16[2,384,256]{2,1,0:T(8,128)(2,1)S(1)}, bf16[2,384,256]{2,1,0:T(8,128)(2,1)S(1)}, u32[]{:S(2)}, u32[]{:S(2)}) collective-permute-start(bf16[2,384,256]{2,1,0:T(8,128)(2,1)S(1)} %pad_maximum_fusion.1), channel_id=1, source_target_pairs={{0,96},{8,104},{16,112},{24,120},{32,64},{40,72},{48,80},{56,88},{... | collective-permute-start | bytes 1179656 | tf_op jit(solution)/shard_map/ppermute | solution.py:390
  11.1 3.5 %stiffness_tiles.3 = (f32[40,512]{1,0:T(8,128)S(1)}, f32[40,512]{1,0:T(8,128)S(1)}, f32[16,512]{1,0:T(8,128)S(1)}, f32[16,512]{1,0:T(8,128)S(1)}) custom-call(bf16[6,30,4,1024]{3,2,1,0:T(4,128)(2,1)S(1)} %bitcast.12, f32[8,1024]{1,0:T(8,128)S(1)} %pad_add_fusion.small, s32[1,1024]{1,0:T(1,128)S(1)} %bitcast.10, f32[112,512]{1,0:T(8,128)S(1)} %stiffness_tiles.2.refs_0_), custom_call_target="tpu_custom_call" | custom-call | flops 5000000000 | bytes 15000000 | tf_op jit(solution)/shard_map/stiffness_tiles/pallas_call | solution.py:193
  14.6 0.5 collective-permute-start.2
  15.0 5.7 %collective-permute-done.4 = bf16[2,384,256]{2,1,0:T(8,128)(2,1)S(1)} collective-permute-done((bf16[2,384,256]{2,1,0:T(8,128)(2,1)S(1)}, bf16[2,384,256]{2,1,0:T(8,128)(2,1)S(1)}, u32[]{:S(2)}, u32[]{:S(2)}) %collective-permute-start.4) | collective-permute-done | bytes 393248 | tf_op jit(solution)/shard_map/ppermute | solution.py:390
  20.7 0.1 pad_maximum_fusion.here
  20.9 0.6 collective-permute-start.5
  21.6 1.6 %collective-permute-start.7 = (bf16[384,256]{1,0:T(8,128)(2,1)S(1)}, bf16[384,256]{1,0:T(8,128)(2,1)S(1)}, u32[]{:S(2)}, u32[]{:S(2)}) collective-permute-start(bf16[384,256]{1,0:T(8,128)(2,1)S(1)} %select_bitcast_fusion.mine), channel_id=1, source_target_pairs={{0,8},{8,0},{16,24},{24,16},{32,40},{40,32},{48,56},{56,48},{64,72... | collective-permute-start | bytes 589832 | tf_op jit(solution)/shard_map/ppermute | solution.py:390
  23.3 2.3 %collective-permute-done.5 = f32[24,512]{1,0:T(8,128)S(1)} collective-permute-done((f32[24,512]{1,0:T(8,128)S(1)}, f32[24,512]{1,0:T(8,128)S(1)}, u32[]{:S(2)}, u32[]{:S(2)}) %collective-permute-start.5) | collective-permute-done | bytes 49184 | tf_op jit(solution)/shard_map/ppermute | solution.py:390
  25.6 1.7 %collective-permute-start.6 = (f32[24,512]{1,0:T(8,128)S(1)}, f32[24,512]{1,0:T(8,128)S(1)}, u32[]{:S(2)}, u32[]{:S(2)}) collective-permute-start(f32[24,512]{1,0:T(8,128)S(1)} %fusion), channel_id=1, source_target_pairs={{0,96},{8,104},{16,112},{24,120},{32,64},{40,72},{48,80},{56,88},{... | collective-permute-start | bytes 147464 | tf_op jit(solution)/shard_map/ppermute | solution.py:390
  27.3 3.7 %collective-permute-done.6 = f32[24,512]{1,0:T(8,128)S(1)} collective-permute-done((f32[24,512]{1,0:T(8,128)S(1)}, f32[24,512]{1,0:T(8,128)S(1)}, u32[]{:S(2)}, u32[]{:S(2)}) %collective-permute-start.6) | collective-permute-done | bytes 49184 | tf_op jit(solution)/shard_map/ppermute | solution.py:390
  31.0 0.2 maximum_select_fusion
  31.2 5.1 %collective-permute-start.10 = (bf16[768,256]{1,0:T(8,128)(2,1)S(1)}, bf16[768,256]{1,0:T(8,128)(2,1)S(1)}, u32[]{:S(2)}, u32[]{:S(2)}) collective-permute-start(bf16[768,256]{1,0:T(8,128)(2,1)S(1)} %maximum_select_fusion), channel_id=1, source_target_pairs={{0,24},{8,16},{16,8},{24,0},{32,56},{40,48},{48,40},{56,32},{64,88... | collective-permute-start | bytes 1179656 | tf_op jit(solution)/shard_map/ppermute | solution.py:390
  36.3 4.1 %collective-permute-done.8 = f32[24,512]{1,0:T(8,128)S(1)} collective-permute-done((f32[24,512]{1,0:T(8,128)S(1)}, f32[24,512]{1,0:T(8,128)S(1)}, u32[]{:S(2)}, u32[]{:S(2)}) %collective-permute-start.8) | collective-permute-done | bytes 49184 | tf_op jit(solution)/shard_map/ppermute | solution.py:390
  40.4 0.2 collective-permute-start.9
  40.6 4.9 %collective-permute-start.11 = (f32[12,512]{1,0:T(8,128)S(1)}, f32[12,512]{1,0:T(8,128)S(1)}, u32[]{:S(2)}, u32[]{:S(2)}) collective-permute-start(f32[12,512]{1,0:T(8,128)S(1)} %get-tuple-element.47), channel_id=1, source_target_pairs={{0,120},{1,121},{2,122},{3,123},{4,124},{5,125},{6,126},{7,127},{8... | collective-permute-start | bytes 73736 | tf_op jit(solution)/shard_map/ppermute | solution.py:394
  45.5 0.3 collective-permute-done.9
  45.8 1.5 %collective-permute-done.11.near = f32[12,512]{1,0:T(8,128)S(1)} collective-permute-done((f32[12,512]{1,0:T(8,128)S(1)}, f32[12,512]{1,0:T(8,128)S(1)}, u32[]{:S(2)}, u32[]{:S(2)}) %collective-permute-start.11) | collective-permute-done | bytes 24608 | tf_op jit(solution)/shard_map/ppermute | solution.py:394
  47.3 3.6 %collective-permute-done.12.half = f32[12,512]{1,0:T(8,128)S(1)} collective-permute-done((f32[12,512]{1,0:T(8,128)S(1)}, f32[12,512]{1,0:T(8,128)S(1)}, u32[]{:S(2)}, u32[]{:S(2)}) %collective-permute-start.12) | collective-permute-done | bytes 24608 | tf_op jit(solution)/shard_map/ppermute | solution.py:394
  50.9 2.0 %collective-permute-start.13 = (bf16[4,384,256]{2,1,0:T(8,128)(2,1)S(1)}, bf16[4,384,256]{2,1,0:T(8,128)(2,1)S(1)}, u32[]{:S(2)}, u32[]{:S(2)}) collective-permute-start(bf16[4,384,256]{2,1,0:T(8,128)(2,1)S(1)} %pad_maximum_fusion.here), channel_id=1, source_target_pairs={{0,8},{8,16},{16,24},{24,0},{32,40},{40,48},{48,56},{56,32},{64,72... | collective-permute-start | bytes 2359304 | tf_op jit(solution)/shard_map/ppermute | solution.py:386
  53.0 16.2 %window_factor.2 = (bf16[512,256]{1,0:T(8,128)(2,1)S(1)}, bf16[512,256]{1,0:T(8,128)(2,1)S(1)}, f32[256,256]{1,0:T(8,128)S(1)}, f32[512,128]{1,0:T(8,128)S(1)}) custom-call(f32[24,512]{1,0:T(8,128)S(1)} %add.58.lead, bf16[384,256]{1,0:T(8,128)(2,1)S(1)} %select_bitcast_fusion.mine, bf16[384,256]{1,0:T(8,128)(2,1)S(1)} %collective-permute-done.7.beside, ...), custom_call_target="tpu_custom_call" | custom-call | flops 5120000000 | bytes 51200000 | tf_op jit(solution)/shard_map/window_factor/pallas_call | solution.py:285
  69.3 1.3 %collective-permute-start.16 = (bf16[2,384,256]{2,1,0:T(8,128)(2,1)S(1)}, bf16[2,384,256]{2,1,0:T(8,128)(2,1)S(1)}, u32[]{:S(2)}, u32[]{:S(2)}) collective-permute-start(bf16[2,384,256]{2,1,0:T(8,128)(2,1)S(1)} %slice.55), channel_id=1, source_target_pairs={{0,24},{8,0},{16,8},{24,16},{32,56},{40,32},{48,40},{56,48},{64,88... | collective-permute-start | bytes 1179656 | tf_op jit(solution)/shard_map/ppermute | solution.py:386
  70.5 0.8 collective-permute-start.15
  71.3 8.0 %window_factor.3 = (bf16[256,256]{1,0:T(8,128)(2,1)S(1)}, bf16[256,256]{1,0:T(8,128)(2,1)S(1)}, f32[256,256]{1,0:T(8,128)S(1)}, f32[256,128]{1,0:T(8,128)S(1)}) custom-call(f32[24,512]{1,0:T(8,128)S(1)} %add.58.lead, bf16[384,256]{1,0:T(8,128)(2,1)S(1)} %select_bitcast_fusion.mine, bf16[384,256]{1,0:T(8,128)(2,1)S(1)} %collective-permute-done.7.beside, ...), custom_call_target="tpu_custom_call" | custom-call | flops 2560000000 | bytes 25600000 | tf_op jit(solution)/shard_map/window_factor/pallas_call | solution.py:285
  79.4 0.1 collective-permute-done.15.low
  79.5 5.4 %factor_rows.1 = f32[1,384,6144]{2,1,0:T(8,128)} custom-call(bf16[512,256]{1,0:T(8,128)(2,1)S(1)} %get-tuple-element.51.high0, bf16[512,256]{1,0:T(8,128)(2,1)S(1)} %get-tuple-element.52.low0, f32[512,128]{1,0:T(8,128)S(1)} %get-tuple-element.53.diag0, bf16[256,256]{1,0:T(8,128)(2,1)S(1)} %get-tuple-element.57.high1, ...), custom_call_target="tpu_custom_call" | custom-call | tf_op jit(solution)/shard_map/factor_rows/pallas_call | solution.py:369
  (29 shorter events, 0.3 us)
Async XLA Ops:
  0.0 8.8 %copy-start = (bf16[1,384,256]{2,1,0:T(8,128)(2,1)S(1)}, bf16[1,384,256]{2,1,0:T(8,128)(2,1)}, u32[]{:S(2)}) copy-start(bf16[1,384,256]{2,1,0:T(8,128)(2,1)} %param.13) | copy-start | bytes 589828
  0.0 8.8 %collective-permute-start = (bf16[384,256]{1,0:T(8,128)(2,1)}, bf16[384,256]{1,0:T(8,128)(2,1)S(1)}, u32[]{:S(2)}, u32[]{:S(2)}) collective-permute-start(bf16[384,256]{1,0:T(8,128)(2,1)} %bitcast.7), channel_id=1, source_target_pairs={{0,32},{8,40},{16,48},{24,56},{32,0},{40,8},{48,16},{56,24},{64,96... | collective-permute-start | bytes 589832 | tf_op jit(solution)/shard_map/ppermute | solution.py:390
  3.6 1.4 %copy-start.1 = (bf16[4,6,30,1024]{3,0,2,1:T(4,128)(2,1)S(1)}, bf16[4,6,30,1024]{3,0,2,1:T(4,128)(2,1)}, u32[]{:S(2)}) copy-start(bf16[4,6,30,1024]{3,0,2,1:T(4,128)(2,1)} %param.7) | copy-start | bytes 4423684
  5.0 6.0 %copy-start.2 = (bf16[4,6,30,1024]{3,0,2,1:T(4,128)(2,1)S(1)}, bf16[4,6,30,1024]{3,0,2,1:T(4,128)(2,1)}, u32[]{:S(2)}) copy-start(bf16[4,6,30,1024]{3,0,2,1:T(4,128)(2,1)} %param.7) | copy-start | bytes 4423684
  8.9 11.9 %collective-permute-start.4 = (bf16[2,384,256]{2,1,0:T(8,128)(2,1)S(1)}, bf16[2,384,256]{2,1,0:T(8,128)(2,1)S(1)}, u32[]{:S(2)}, u32[]{:S(2)}) collective-permute-start(bf16[2,384,256]{2,1,0:T(8,128)(2,1)S(1)} %pad_maximum_fusion.1), channel_id=1, source_target_pairs={{0,96},{8,104},{16,112},{24,120},{32,64},{40,72},{48,80},{56,88},{... | collective-permute-start | bytes 1179656 | tf_op jit(solution)/shard_map/ppermute | solution.py:390
  14.6 6.3 %collective-permute-start.2 = (f32[16,512]{1,0:T(8,128)S(1)}, f32[16,512]{1,0:T(8,128)S(1)}, u32[]{:S(2)}, u32[]{:S(2)}) collective-permute-start(f32[16,512]{1,0:T(8,128)S(1)} %get-tuple-element.38), channel_id=1, source_target_pairs={{0,126},{1,127},{2,0},{3,1},{4,2},{5,3},{6,4},{7,5},{8,6},{9,7},{1... | collective-permute-start | bytes 98312 | tf_op jit(solution)/shard_map/ppermute | solution.py:394
  15.0 5.8 %collective-permute-start.3 = (f32[16,512]{1,0:T(8,128)S(1)}, f32[16,512]{1,0:T(8,128)S(1)}, u32[]{:S(2)}, u32[]{:S(2)}) collective-permute-start(f32[16,512]{1,0:T(8,128)S(1)} %get-tuple-element.39), channel_id=1, source_target_pairs={{0,125},{1,126},{2,127},{3,0},{4,1},{5,2},{6,3},{7,4},{8,5},{9,6},... | collective-permute-start | bytes 98312 | tf_op jit(solution)/shard_map/ppermute | solution.py:394
  15.0 5.8 %collective-permute-start.1 = (f32[40,512]{1,0:T(8,128)S(1)}, f32[40,512]{1,0:T(8,128)S(1)}, u32[]{:S(2)}, u32[]{:S(2)}) collective-permute-start(f32[40,512]{1,0:T(8,128)S(1)} %get-tuple-element.37), channel_id=1, source_target_pairs={{0,127},{1,0},{2,1},{3,2},{4,3},{5,4},{6,5},{7,6},{8,7},{9,8},{10,... | collective-permute-start | bytes 245768 | tf_op jit(solution)/shard_map/ppermute | solution.py:394
  20.9 4.7 %collective-permute-start.5 = (f32[24,512]{1,0:T(8,128)S(1)}, f32[24,512]{1,0:T(8,128)S(1)}, u32[]{:S(2)}, u32[]{:S(2)}) collective-permute-start(f32[24,512]{1,0:T(8,128)S(1)} %pad_maximum_fusion.2), channel_id=1, source_target_pairs={{0,32},{8,40},{16,48},{24,56},{32,0},{40,8},{48,16},{56,24},{64,96... | collective-permute-start | bytes 147464 | tf_op jit(solution)/shard_map/ppermute | solution.py:390
  21.6 9.4 %collective-permute-start.7 = (bf16[384,256]{1,0:T(8,128)(2,1)S(1)}, bf16[384,256]{1,0:T(8,128)(2,1)S(1)}, u32[]{:S(2)}, u32[]{:S(2)}) collective-permute-start(bf16[384,256]{1,0:T(8,128)(2,1)S(1)} %select_bitcast_fusion.mine), channel_id=1, source_target_pairs={{0,8},{8,0},{16,24},{24,16},{32,40},{40,32},{48,56},{56,48},{64,72... | collective-permute-start | bytes 589832 | tf_op jit(solution)/shard_map/ppermute | solution.py:390
  25.6 5.4 %collective-permute-start.6 = (f32[24,512]{1,0:T(8,128)S(1)}, f32[24,512]{1,0:T(8,128)S(1)}, u32[]{:S(2)}, u32[]{:S(2)}) collective-permute-start(f32[24,512]{1,0:T(8,128)S(1)} %fusion), channel_id=1, source_target_pairs={{0,96},{8,104},{16,112},{24,120},{32,64},{40,72},{48,80},{56,88},{... | collective-permute-start | bytes 147464 | tf_op jit(solution)/shard_map/ppermute | solution.py:390
  31.2 19.8 %collective-permute-start.10 = (bf16[768,256]{1,0:T(8,128)(2,1)S(1)}, bf16[768,256]{1,0:T(8,128)(2,1)S(1)}, u32[]{:S(2)}, u32[]{:S(2)}) collective-permute-start(bf16[768,256]{1,0:T(8,128)(2,1)S(1)} %maximum_select_fusion), channel_id=1, source_target_pairs={{0,24},{8,16},{16,8},{24,0},{32,56},{40,48},{48,40},{56,32},{64,88... | collective-permute-start | bytes 1179656 | tf_op jit(solution)/shard_map/ppermute | solution.py:390
  36.3 4.1 %collective-permute-start.8 = (f32[24,512]{1,0:T(8,128)S(1)}, f32[24,512]{1,0:T(8,128)S(1)}, u32[]{:S(2)}, u32[]{:S(2)}) collective-permute-start(f32[24,512]{1,0:T(8,128)S(1)} %add.56), channel_id=1, source_target_pairs={{0,8},{8,0},{16,24},{24,16},{32,40},{40,32},{48,56},{56,48},{64,72... | collective-permute-start | bytes 147464 | tf_op jit(solution)/shard_map/ppermute | solution.py:390
  40.4 5.4 %collective-permute-start.9 = (f32[24,512]{1,0:T(8,128)S(1)}, f32[24,512]{1,0:T(8,128)S(1)}, u32[]{:S(2)}, u32[]{:S(2)}) collective-permute-start(f32[24,512]{1,0:T(8,128)S(1)} %add.57), channel_id=1, source_target_pairs={{0,24},{8,16},{16,8},{24,0},{32,56},{40,48},{48,40},{56,32},{64,88... | collective-permute-start | bytes 147464 | tf_op jit(solution)/shard_map/ppermute | solution.py:390
  40.6 6.8 %collective-permute-start.11 = (f32[12,512]{1,0:T(8,128)S(1)}, f32[12,512]{1,0:T(8,128)S(1)}, u32[]{:S(2)}, u32[]{:S(2)}) collective-permute-start(f32[12,512]{1,0:T(8,128)S(1)} %get-tuple-element.47), channel_id=1, source_target_pairs={{0,120},{1,121},{2,122},{3,123},{4,124},{5,125},{6,126},{7,127},{8... | collective-permute-start | bytes 73736 | tf_op jit(solution)/shard_map/ppermute | solution.py:394
  45.5 5.4 %collective-permute-start.12 = (f32[12,512]{1,0:T(8,128)S(1)}, f32[12,512]{1,0:T(8,128)S(1)}, u32[]{:S(2)}, u32[]{:S(2)}) collective-permute-start(f32[12,512]{1,0:T(8,128)S(1)} %get-tuple-element.48), channel_id=1, source_target_pairs={{0,64},{1,65},{2,66},{3,67},{4,68},{5,69},{6,70},{7,71},{8,72},{9,... | collective-permute-start | bytes 73736 | tf_op jit(solution)/shard_map/ppermute | solution.py:394
  50.9 18.2 %collective-permute-start.14 = (bf16[4,384,256]{2,1,0:T(8,128)(2,1)S(1)}, bf16[4,384,256]{2,1,0:T(8,128)(2,1)S(1)}, u32[]{:S(2)}, u32[]{:S(2)}) collective-permute-start(bf16[4,384,256]{2,1,0:T(8,128)(2,1)S(1)} %pad_maximum_fusion.here), channel_id=1, source_target_pairs={{0,24},{8,0},{16,8},{24,16},{32,56},{40,32},{48,40},{56,48},{64,88... | collective-permute-start | bytes 2359304 | tf_op jit(solution)/shard_map/ppermute | solution.py:386
  50.9 18.2 %collective-permute-start.13 = (bf16[4,384,256]{2,1,0:T(8,128)(2,1)S(1)}, bf16[4,384,256]{2,1,0:T(8,128)(2,1)S(1)}, u32[]{:S(2)}, u32[]{:S(2)}) collective-permute-start(bf16[4,384,256]{2,1,0:T(8,128)(2,1)S(1)} %pad_maximum_fusion.here), channel_id=1, source_target_pairs={{0,8},{8,16},{16,24},{24,0},{32,40},{40,48},{48,56},{56,32},{64,72... | collective-permute-start | bytes 2359304 | tf_op jit(solution)/shard_map/ppermute | solution.py:386
  69.3 10.1 %collective-permute-start.16 = (bf16[2,384,256]{2,1,0:T(8,128)(2,1)S(1)}, bf16[2,384,256]{2,1,0:T(8,128)(2,1)S(1)}, u32[]{:S(2)}, u32[]{:S(2)}) collective-permute-start(bf16[2,384,256]{2,1,0:T(8,128)(2,1)S(1)} %slice.55), channel_id=1, source_target_pairs={{0,24},{8,0},{16,8},{24,16},{32,56},{40,32},{48,40},{56,48},{64,88... | collective-permute-start | bytes 1179656 | tf_op jit(solution)/shard_map/ppermute | solution.py:386
  70.5 9.0 %collective-permute-start.15 = (bf16[2,384,256]{2,1,0:T(8,128)(2,1)S(1)}, bf16[2,384,256]{2,1,0:T(8,128)(2,1)S(1)}, u32[]{:S(2)}, u32[]{:S(2)}) collective-permute-start(bf16[2,384,256]{2,1,0:T(8,128)(2,1)S(1)} %slice.54), channel_id=1, source_target_pairs={{0,8},{8,16},{16,24},{24,0},{32,40},{40,48},{48,56},{56,32},{64,72... | collective-permute-start | bytes 1179656 | tf_op jit(solution)/shard_map/ppermute | solution.py:386

commit v4 on v3

--- a/solution.py
+++ b/solution.py
@@ -31,11 +31,16 @@
 def dot_nt(a, b): return lax.dot_general(a, b, (((1,), (1,)), ((), ())), preferred_element_type=F32)
 
 
+def six_terms(x1, x2, x3, axis):
+    return jnp.concatenate([x1, x1, x2, x1, x2, x3], axis=axis)
+
+
+def six_terms_across(y1, y2, y3, axis):
+    return jnp.concatenate([y1, y2, y1, y3, y2, y1], axis=axis)
+
+
 def product_tn(x, y):
-    x1, x2, x3 = split3(x)
-    y1, y2, y3 = split3(y)
-    left = jnp.concatenate([x1, x1, x2, x1, x2, x3], axis=0)
-    right = jnp.concatenate([y1, y2, y1, y3, y2, y1], axis=0)
+    left, right = six_terms(*split3(x), 0), six_terms_across(*split3(y), 0)
     return lax.dot_general(left, right, (((0,), (0,)), ((), ())), preferred_element_type=F32)
 
 
@@ -43,24 +48,27 @@
     sub = lax.broadcasted_iota(jnp.int32, (8, 128), 0)
     n = len(rows)
     spread = lambda x, at: jnp.broadcast_to(x[at:at + 1, :], (8, 128))
-    cols = {}
-    for k in range(8 * n):
-        for q in range(k // 8, n):
-            cols[q, k] = jnp.broadcast_to(rows[q][0][:, first + k:first + k + 1], (8, 128))
-    for k in range(8 * n):
-        t, u = k // 8, k % 8
-        rs = lax.rsqrt(spread(cols[t, k], u))
-        f = {q: cols[q, k] * rs for q in range(t, n)}
-        for m in range(k + 1, 8 * n):
-            sm = spread(f[m // 8], m % 8)
-            for q in range(m // 8, n):
-                cols[q, m] = cols[q, m] - f[q] * sm
-        fm = jnp.where(sub > u, f[t], 0.0)
-        for h in range(len(rows[t])):
-            r = spread(rows[t][h], u) * rs
-            rows[t][h] = jnp.where(sub == u, r, rows[t][h] - fm * r)
-            for q in range(t + 1, n):
-                rows[q][h] = rows[q][h] - f[q] * r
+    fetch = lambda k, q: jnp.broadcast_to(rows[q][0][:, first + k:first + k + 1], (8, 128))
+    cols = {(q, k): fetch(k, q) for k in range(16) for q in range(k // 8, n)}
+    for t in range(n):
+        if 0 < t < n - 1:
+            for k in range(8 * t + 8, 8 * t + 16):
+                for q in range(t + 1, n):
+                    cols[q, k] = fetch(k, q)
+        for k in range(8 * t, 8 * t + 8):
+            u = k % 8
+            rs = lax.rsqrt(spread(cols[t, k], u))
+            f = {q: cols[q, k] * rs for q in range(t, n)}
+            for m in range(k + 1, min(8 * t + 16, 8 * n)):
+                sm = spread(f[m // 8], m % 8)
+                for q in range(m // 8, n):
+                    cols[q, m] = cols[q, m] - f[q] * sm
+            fm = jnp.where(sub > u, f[t], 0.0)
+            for h in range(len(rows[t])):
+                r = spread(rows[t][h], u) * rs
+                rows[t][h] = jnp.where(sub == u, r, rows[t][h] - fm * r)
+                for q in range(t + 1, n):
+                    rows[q][h] = rows[q][h] - f[q] * r
     return rows
 
 
@@ -216,18 +224,26 @@
     return jnp.where(row <= col, block, block.T)
 
 
-def factor_window(diag, v_ref, h_ref, m_ref, work):
+def factor_window(diag, v_ref, h_ref, m_ref, work, ahead, last):
     square = lambda n, dim: lax.broadcasted_iota(jnp.int32, (n, n), dim)
     upper = square(128, 0) <= square(128, 1)
-
-    def block(j, carry):
-        at = pl.ds(pl.multiple_of(j * 128, 128), 128)
+    blocks = diag.shape[0] // 128
+    rows_of = lambda j: pl.ds(pl.multiple_of(j * 128, 128), 128)
+
+    def start_block(at, m, to):
         v = v_ref[at, :]
-        m1, m2, m3 = split3(m_ref[...])
+        m1, m2, m3 = split3(m)
         p = dot_nn(v, m1) + (dot_nn(v, m2) + dot_nn(v, m3))
         p1, p2, p3 = split3(p)
-        work[:, :128] = mirror(diag[at, :]) + (dot_nt(p1, v) + (dot_nt(p2, v) + dot_nt(p3, v)))
-        work[:, 128:] = p
+        to[:, :128] = mirror(diag[at, :]) + (dot_nt(p1, v) + (dot_nt(p2, v) + dot_nt(p3, v)))
+        to[:, 128:] = p
+
+    def block(j, carry):
+        at, following = rows_of(j), rows_of(jnp.minimum(j + 1, blocks - 1))
+        done = last[...]
+        m = m_ref[...] - product_tn(done, done)
+        m_ref[...] = m
+        start_block(following, m, ahead)
         for s in range(4):
             at_row = lambda q: slice(32 * s + 8 * q, 32 * s + 8 * q + 8)
             rows = [[work[at_row(q), 128 * h:128 * h + 128] for h in range(3)] for q in range(4)]
@@ -236,35 +252,46 @@
                 for h in range(3):
                     work[at_row(q), 128 * h:128 * h + 128] = rows[q][h]
             if s < 3:
-                done = work[32 * s:32 * s + 32, :]
-                change = product_tn(done[:, :128], done)
-                work[32 * s + 32:, :] = work[32 * s + 32:, :] - change[32 * s + 32:, :]
+                later = 32 * s + 32
+                done = work[32 * s:later, :]
+                left = six_terms(*split3(done[:, :128]), 0).T[later:, :]
+                work[later:, :] = work[later:, :] - dot_nn(left, six_terms_across(*split3(done), 0))
         h = work[:, 128:]
         h_ref[at, :] = h
+        last[...] = h
         diag[at, :] = jnp.where(upper, work[:, :128], 0.0).T
-        m_ref[...] = m_ref[...] - product_tn(h, h)
+
+        @pl.when(j < blocks - 1)
+        def _():
+            v = v_ref[following, :]
+            h1, h2, h3 = split3(h)
+            c = dot_nt(v, h1) + (dot_nt(v, h2) + dot_nt(v, h3))
+            c = split3(c)
+            left = six_terms(*c, 1)
+            work[:, 128:] = ahead[:, 128:] - dot_nn(left, six_terms_across(h1, h2, h3, 0))
+            work[:, :128] = ahead[:, :128] - dot_nt(left, six_terms_across(*c, 1))
+
         return carry
 
-    lax.fori_loop(0, diag.shape[0] // 128, block, 0)
-
-
-def window_kernel(part, lead, mine, beside, across, *refs):
-    high_ref, low_ref, m_ref, diag, v_ref, h_ref, work = refs[-7:]
+    last[...] = jnp.zeros_like(last)
+    start_block(pl.ds(0, 128), m_ref[...], work)
+    lax.fori_loop(0, blocks, block, 0)
+    done = last[...]
+    m_ref[...] = m_ref[...] - product_tn(done, done)
+
+
+def window_kernel(part, lead, mine, beside, across, last_piece, *refs):
+    high_ref, low_ref, m_ref, diag, v_ref, h_ref, work, ahead, last = refs[-9:]
     first, size = PARTS[part]
     y = lax.rem(lax.axis_index("cand"), 4)
-    for b, (own, other) in enumerate(((mine, beside), (beside, mine))):
+    for b, holders in enumerate(((mine, beside, last_piece, across), (beside, mine, across, last_piece))):
         begin, end = max(first, W * b), min(first + size, W * b + W)
         if begin >= end:
             continue
-        to = slice(begin - first, end - first)
-        for n, holder in enumerate((own, other)):
+        for n, holder in enumerate(holders):
             @pl.when(y == n)
             def _():
-                v_ref[to, :] = holder[begin - W * b:end - W * b, :] * 0.0625
-
-        @pl.when(y >= 2)
-        def _():
-            v_ref[to, :] = across[begin:end, :] * 0.0625
+                v_ref[begin - first:end - first, :] = holder[begin - W * b:end - W * b, :] * 0.0625
 
     if part:
         m_ref[...] = refs[0][...]
@@ -272,7 +299,7 @@
         square = lambda dim: lax.broadcasted_iota(jnp.int32, (RANK, RANK), dim)
         m_ref[...] = (square(0) == square(1)).astype(F32)
     unpack_tiles(lead[first // 32:(first + size) // 32, :], diag)
-    factor_window(diag, v_ref, h_ref, m_ref, work)
+    factor_window(diag, v_ref, h_ref, m_ref, work, ahead, last)
     h = h_ref[...]
     high = h.astype(BF16)
     high_ref[...] = high
@@ -284,7 +311,7 @@
     size = PARTS[part][1]
     return pl.pallas_call(
         functools.partial(window_kernel, part),
-        in_specs=[vmem] * (4 + len(m)),
+        in_specs=[vmem] * (5 + len(m)),
         out_specs=[vmem] * 4,
         out_shape=[
             jax.ShapeDtypeStruct((size, RANK), BF16),
@@ -296,6 +323,8 @@
             pltpu.VMEM((size, RANK), BF16),
             pltpu.VMEM((size, RANK), F32),
             pltpu.VMEM((128, 128 + RANK), F32),
+            pltpu.VMEM((128, 128 + RANK), F32),
+            pltpu.VMEM((128, RANK), F32),
         ],
         cost_estimate=pl.CostEstimate(flops=size * 10**7, bytes_accessed=size * 10**5, transcendentals=0),
         compiler_params=pltpu.CompilerParams(vmem_limit_bytes=32 * 2**20),
@@ -404,7 +433,7 @@
         rows, width = part.shape
         small = small + lax.pad(part, F32(0), ((row, 8 - row - rows, 0), (0, elem_scale.shape[1] - width, 0)))
         row += rows
-    code = (elem_block[:, 0] * 16 + elem_slot)[None, :]
+    code = elem_block.T * 16 + elem_slot[None, :]
     strain = jnp.transpose(strain_ops, (1, 2, 0, 3))
     steps = strain.shape[3] // CHUNK
 
@@ -426,20 +455,20 @@
     pick = lambda c: jnp.where(cand == c, kept, jnp.where(cand == c + 1, near, jnp.where(cand == c + 8, half, zero)))
     lead = jnp.concatenate([pick(0), pick(1)], axis=0)
     mine = functools.reduce(lambda u, n: jnp.where(x == ACROSS[n], here[n], u), range(1, 4), here[0])
-    paired = swap(mine, 1)
+    paired, crossed = swap(mine, 1), swap(mine, 3)
     lead = lead + swap(lead, 4)
     lead = lead + swap(lead, 12)
-    lead, paired, near, half = lax.optimization_barrier((lead, paired, near, half))
+    lead, paired, crossed, near, half = lax.optimization_barrier((lead, paired, crossed, near, half))
     near, half = move_back(near, 8), move_back(half, 64)
-    across = swap(jnp.where(y == 0, jnp.concatenate([mine, paired]), jnp.concatenate([paired, mine])), 3)
+    last_piece = swap(crossed, 1)
     lead = lead + swap(lead, 1)
     lead = lead + swap(lead, 3)
-    lead, across, here, near, half = lax.optimization_barrier((lead, across, here, near, half))
+    lead, last_piece, here = lax.optimization_barrier((lead, last_piece, here))
 
     before, after = move_y(here, 1), move_y(here, 3)
-    window = (mine, paired, across)
+    window = (mine, paired, crossed, last_piece)
     high0, low0, m, diag0 = window_factor(0, lead, window, ())
-    m, before, after = lax.optimization_barrier((m, before, after))
+    m, before, after, near, half = lax.optimization_barrier((m, before, after, near, half))
     low, high = move_y(before[:2], 1), move_y(after[2:], 3)
     high1, low1, m, diag1 = window_factor(1, lead, window, (m,))
     return factor_rows(high0, low0, diag0, high1, low1, m, diag1, kept, near, half, own, here, before, after, low, high)

time: 86 us -> 84.5 us (0.983)
  Pallas kernels: 36.9 us -> 33.2 us
  starting transfers between devices: 22.5 us -> 25.7 us
    ppermute x5, waiting for transfers between devices: 5.14 us -> 0.03 us  [move_back(): lax.ppermute(value, ('cand', 'dom'), [(i, (i - offset) % 128) for i in ra...]
    ppermute x8 -> x9, waiting for transfers between devices: 16.1 us -> 20.2 us  [swap(): return lax.ppermute(value, 'cand', [(i, i ^ bits) for i in range(16)])]
    pallas_call x2, Pallas kernels: 24.2 us -> 20.5 us  [window_factor(): pl.pallas_call(functools.partial(window_kernel, part), in_specs=[vmem] *...]
    ppermute x8 -> x9, starting transfers between devices: 13 us -> 15.2 us  [swap(): return lax.ppermute(value, 'cand', [(i, i ^ bits) for i in range(16)])]
    ppermute x5, starting transfers between devices: 5.41 us -> 6.33 us  [move_back(): lax.ppermute(value, ('cand', 'dom'), [(i, (i - offset) % 128) for i in ra...]
  transfers between devices with their start and end apart: 17 -> 18, of which waited for: 8 -> 7; matrix products, arithmetic and copies ran while one was open for 3% -> 3% of each run, Pallas kernels for 37% -> 33%
where the time goes in v4:
time: 84.5 us; the launch traced here: 83.7 us
  Pallas kernels  33.2 us (39%)
  starting transfers between devices  25.7 us (30%)
  waiting for transfers between devices  20.6 us (24%)
  other arithmetic  2.38 us (3%)
  local copies, waits for them, and re-layouts  1.43 us (2%)
    pallas_call x2, Pallas kernels, window_factor(): pl.pallas_call(functools.partial(window_kernel, part), in_specs=[vmem] *...  20.5 us
    ppermute x9, waiting for transfers between devices, swap(): return lax.ppermute(value, 'cand', [(i, i ^ bits) for i in range(16)])  20.2 us
    ppermute x9, starting transfers between devices, swap(): return lax.ppermute(value, 'cand', [(i, i ^ bits) for i in range(16)])  15.2 us
    pallas_call x2, Pallas kernels, stiffness_tiles(): pl.pallas_call(functools.partial(stiffness_kernel, begin), in_specs=[pl.B...  7.25 us
    ppermute x5, starting transfers between devices, move_back(): lax.ppermute(value, ('cand', 'dom'), [(i, (i - offset) % 128) for i in ra...  6.33 us
    pallas_call x1, Pallas kernels, factor_rows(): pl.pallas_call(rows_kernel, in_specs=[vmem] * len(operands), out_specs=pl...  5.45 us
    ppermute x4, starting transfers between devices, move_y(): lax.ppermute(value, 'cand', [(4 * x + y, 4 * x + (y + shift) % 4) for x i...  4.19 us
  transfers between devices with their start and end apart: 18, of which 7 were waited for; matrix products, arithmetic and copies ran while one was open for 3% of the time, Pallas kernels for 33%

profile of v4, /device:TPU:96, one launch (start us, length us, event | category | flops | bytes accessed | tf_op | source)
XLA Modules:
  0.0 83.7 jit_solution(18043458101883854398)
XLA Ops:
  0.0 1.5 %collective-permute-start = (bf16[384,256]{1,0:T(8,128)(2,1)}, bf16[384,256]{1,0:T(8,128)(2,1)S(1)}, u32[]{:S(2)}, u32[]{:S(2)}) collective-permute-start(bf16[384,256]{1,0:T(8,128)(2,1)} %bitcast.7), channel_id=1, source_target_pairs={{0,32},{8,40},{16,48},{24,56},{32,0},{40,8},{48,16},{56,24},{64,96... | collective-permute-start | bytes 589832 | tf_op jit(solution)/shard_map/ppermute | solution.py:419
  1.5 0.7 broadcast_multiply_fusion
  2.2 0.7 add.47
  2.9 0.8 pad_add_fusion.small
  3.7 1.4 %copy-done.1 = bf16[4,6,30,1024]{3,0,2,1:T(4,128)(2,1)S(1)} copy-done((bf16[4,6,30,1024]{3,0,2,1:T(4,128)(2,1)S(1)}, bf16[4,6,30,1024]{3,0,2,1:T(4,128)(2,1)}, u32[]{:S(2)}) %copy-start.1) | copy-done | bytes 1474584
  5.0 3.8 %stiffness_tiles.2.refs_0_ = f32[112,512]{1,0:T(8,128)S(1)} custom-call(bf16[6,30,4,1024]{3,2,1,0:T(4,128)(2,1)S(1)} %bitcast.11, f32[8,1024]{1,0:T(8,128)S(1)} %pad_add_fusion.small, s32[1,1024]{1,0:T(1,128)S(1)} %bitcast.9), custom_call_target="tpu_custom_call" | custom-call | flops 5000000000 | bytes 15000000 | tf_op jit(solution)/shard_map/stiffness_tiles/pallas_call | solution.py:201
  8.9 2.2 %collective-permute-start.4 = (bf16[2,384,256]{2,1,0:T(8,128)(2,1)S(1)}, bf16[2,384,256]{2,1,0:T(8,128)(2,1)S(1)}, u32[]{:S(2)}, u32[]{:S(2)}) collective-permute-start(bf16[2,384,256]{2,1,0:T(8,128)(2,1)S(1)} %pad_maximum_fusion.1), channel_id=1, source_target_pairs={{0,96},{8,104},{16,112},{24,120},{32,64},{40,72},{48,80},{56,88},{... | collective-permute-start | bytes 1179656 | tf_op jit(solution)/shard_map/ppermute | solution.py:419
  11.1 3.5 %stiffness_tiles.3 = (f32[40,512]{1,0:T(8,128)S(1)}, f32[40,512]{1,0:T(8,128)S(1)}, f32[16,512]{1,0:T(8,128)S(1)}, f32[16,512]{1,0:T(8,128)S(1)}) custom-call(bf16[6,30,4,1024]{3,2,1,0:T(4,128)(2,1)S(1)} %bitcast.12, f32[8,1024]{1,0:T(8,128)S(1)} %pad_add_fusion.small, s32[1,1024]{1,0:T(1,128)S(1)} %bitcast.10, f32[112,512]{1,0:T(8,128)S(1)} %stiffness_tiles.2.refs_0_), custom_call_target="tpu_custom_call" | custom-call | flops 5000000000 | bytes 15000000 | tf_op jit(solution)/shard_map/stiffness_tiles/pallas_call | solution.py:201
  14.6 0.5 collective-permute-start.2
  15.1 5.7 %collective-permute-done.4 = bf16[2,384,256]{2,1,0:T(8,128)(2,1)S(1)} collective-permute-done((bf16[2,384,256]{2,1,0:T(8,128)(2,1)S(1)}, bf16[2,384,256]{2,1,0:T(8,128)(2,1)S(1)}, u32[]{:S(2)}, u32[]{:S(2)}) %collective-permute-start.4) | collective-permute-done | bytes 393248 | tf_op jit(solution)/shard_map/ppermute | solution.py:419
  20.7 0.1 pad_maximum_fusion.here
  20.9 0.7 collective-permute-start.5
  21.6 5.2 %collective-permute-start.8 = (bf16[384,256]{1,0:T(8,128)(2,1)S(1)}, bf16[384,256]{1,0:T(8,128)(2,1)S(1)}, u32[]{:S(2)}, u32[]{:S(2)}) collective-permute-start(bf16[384,256]{1,0:T(8,128)(2,1)S(1)} %select_bitcast_fusion.mine), channel_id=1, source_target_pairs={{0,24},{8,16},{16,8},{24,0},{32,56},{40,48},{48,40},{56,32},{64,88... | collective-permute-start | bytes 589832 | tf_op jit(solution)/shard_map/ppermute | solution.py:419
  26.9 1.9 %collective-permute-start.6 = (f32[24,512]{1,0:T(8,128)S(1)}, f32[24,512]{1,0:T(8,128)S(1)}, u32[]{:S(2)}, u32[]{:S(2)}) collective-permute-start(f32[24,512]{1,0:T(8,128)S(1)} %fusion), channel_id=1, source_target_pairs={{0,96},{8,104},{16,112},{24,120},{32,64},{40,72},{48,80},{56,88},{... | collective-permute-start | bytes 147464 | tf_op jit(solution)/shard_map/ppermute | solution.py:419
  28.7 3.6 %collective-permute-done.6 = f32[24,512]{1,0:T(8,128)S(1)} collective-permute-done((f32[24,512]{1,0:T(8,128)S(1)}, f32[24,512]{1,0:T(8,128)S(1)}, u32[]{:S(2)}, u32[]{:S(2)}) %collective-permute-start.6) | collective-permute-done | bytes 49184 | tf_op jit(solution)/shard_map/ppermute | solution.py:419
  32.3 0.2 collective-permute-done.8.across
  32.5 1.6 %collective-permute-done.7.beside = bf16[384,256]{1,0:T(8,128)(2,1)S(1)} collective-permute-done((bf16[384,256]{1,0:T(8,128)(2,1)S(1)}, bf16[384,256]{1,0:T(8,128)(2,1)S(1)}, u32[]{:S(2)}, u32[]{:S(2)}) %collective-permute-start.7) | collective-permute-done | bytes 196640 | tf_op jit(solution)/shard_map/ppermute | solution.py:419
  34.1 0.3 collective-permute-start.11
  34.4 1.7 %collective-permute-start.9 = (f32[24,512]{1,0:T(8,128)S(1)}, f32[24,512]{1,0:T(8,128)S(1)}, u32[]{:S(2)}, u32[]{:S(2)}) collective-permute-start(f32[24,512]{1,0:T(8,128)S(1)} %add.55), channel_id=1, source_target_pairs={{0,8},{8,0},{16,24},{24,16},{32,40},{40,32},{48,56},{56,48},{64,72... | collective-permute-start | bytes 147464 | tf_op jit(solution)/shard_map/ppermute | solution.py:419
  36.1 5.5 %collective-permute-done.9 = f32[24,512]{1,0:T(8,128)S(1)} collective-permute-done((f32[24,512]{1,0:T(8,128)S(1)}, f32[24,512]{1,0:T(8,128)S(1)}, u32[]{:S(2)}, u32[]{:S(2)}) %collective-permute-start.9) | collective-permute-done | bytes 49184 | tf_op jit(solution)/shard_map/ppermute | solution.py:419
  41.7 1.8 %collective-permute-start.10 = (f32[24,512]{1,0:T(8,128)S(1)}, f32[24,512]{1,0:T(8,128)S(1)}, u32[]{:S(2)}, u32[]{:S(2)}) collective-permute-start(f32[24,512]{1,0:T(8,128)S(1)} %add.56), channel_id=1, source_target_pairs={{0,24},{8,16},{16,8},{24,0},{32,56},{40,48},{48,40},{56,32},{64,88... | collective-permute-start | bytes 147464 | tf_op jit(solution)/shard_map/ppermute | solution.py:419
  43.5 3.6 %collective-permute-done.10 = f32[24,512]{1,0:T(8,128)S(1)} collective-permute-done((f32[24,512]{1,0:T(8,128)S(1)}, f32[24,512]{1,0:T(8,128)S(1)}, u32[]{:S(2)}, u32[]{:S(2)}) %collective-permute-start.10) | collective-permute-done | bytes 49184 | tf_op jit(solution)/shard_map/ppermute | solution.py:419
  47.1 1.8 %collective-permute-start.13 = (bf16[4,384,256]{2,1,0:T(8,128)(2,1)S(1)}, bf16[4,384,256]{2,1,0:T(8,128)(2,1)S(1)}, u32[]{:S(2)}, u32[]{:S(2)}) collective-permute-start(bf16[4,384,256]{2,1,0:T(8,128)(2,1)S(1)} %pad_maximum_fusion.here), channel_id=1, source_target_pairs={{0,24},{8,0},{16,8},{24,16},{32,56},{40,32},{48,40},{56,48},{64,88... | collective-permute-start | bytes 2359304 | tf_op jit(solution)/shard_map/ppermute | solution.py:415
  48.9 0.3 collective-permute-start.12
  49.2 4.6 %collective-permute-start.14 = (f32[12,512]{1,0:T(8,128)S(1)}, f32[12,512]{1,0:T(8,128)S(1)}, u32[]{:S(2)}, u32[]{:S(2)}) collective-permute-start(f32[12,512]{1,0:T(8,128)S(1)} %get-tuple-element.56), channel_id=1, source_target_pairs={{0,120},{1,121},{2,122},{3,123},{4,124},{5,125},{6,126},{7,127},{8... | collective-permute-start | bytes 73736 | tf_op jit(solution)/shard_map/ppermute | solution.py:423
  53.8 1.3 %collective-permute-start.15 = (f32[12,512]{1,0:T(8,128)S(1)}, f32[12,512]{1,0:T(8,128)S(1)}, u32[]{:S(2)}, u32[]{:S(2)}) collective-permute-start(f32[12,512]{1,0:T(8,128)S(1)} %get-tuple-element.57), channel_id=1, source_target_pairs={{0,64},{1,65},{2,66},{3,67},{4,68},{5,69},{6,70},{7,71},{8,72},{9,... | collective-permute-start | bytes 73736 | tf_op jit(solution)/shard_map/ppermute | solution.py:423
  55.0 13.6 %window_factor.2 = (bf16[512,256]{1,0:T(8,128)(2,1)S(1)}, bf16[512,256]{1,0:T(8,128)(2,1)S(1)}, f32[256,256]{1,0:T(8,128)S(1)}, f32[512,128]{1,0:T(8,128)S(1)}) custom-call(f32[24,512]{1,0:T(8,128)S(1)} %add.57.lead, bf16[384,256]{1,0:T(8,128)(2,1)S(1)} %select_bitcast_fusion.mine, bf16[384,256]{1,0:T(8,128)(2,1)S(1)} %collective-permute-done.7.beside, ...), custom_call_target="tpu_custom_call" | custom-call | flops 5120000000 | bytes 51200000 | tf_op jit(solution)/shard_map/window_factor/pallas_call | solution.py:312
  68.8 0.3 collective-permute-start.17
  69.1 1.7 %collective-permute-start.16 = (bf16[2,384,256]{2,1,0:T(8,128)(2,1)S(1)}, bf16[2,384,256]{2,1,0:T(8,128)(2,1)S(1)}, u32[]{:S(2)}, u32[]{:S(2)}) collective-permute-start(bf16[2,384,256]{2,1,0:T(8,128)(2,1)S(1)} %slice.54), channel_id=1, source_target_pairs={{0,8},{8,16},{16,24},{24,0},{32,40},{40,48},{48,56},{56,32},{64,72... | collective-permute-start | bytes 1179656 | tf_op jit(solution)/shard_map/ppermute | solution.py:415
  70.9 6.9 %window_factor.3 = (bf16[256,256]{1,0:T(8,128)(2,1)S(1)}, bf16[256,256]{1,0:T(8,128)(2,1)S(1)}, f32[256,256]{1,0:T(8,128)S(1)}, f32[256,128]{1,0:T(8,128)S(1)}) custom-call(f32[24,512]{1,0:T(8,128)S(1)} %add.57.lead, bf16[384,256]{1,0:T(8,128)(2,1)S(1)} %select_bitcast_fusion.mine, bf16[384,256]{1,0:T(8,128)(2,1)S(1)} %collective-permute-done.7.beside, ...), custom_call_target="tpu_custom_call" | custom-call | flops 2560000000 | bytes 25600000 | tf_op jit(solution)/shard_map/window_factor/pallas_call | solution.py:312
  77.8 0.4 collective-permute-done.16.low
  78.1 5.4 %factor_rows.1 = f32[1,384,6144]{2,1,0:T(8,128)} custom-call(bf16[512,256]{1,0:T(8,128)(2,1)S(1)} %get-tuple-element.51.high0, bf16[512,256]{1,0:T(8,128)(2,1)S(1)} %get-tuple-element.52.low0, f32[512,128]{1,0:T(8,128)S(1)} %get-tuple-element.53.diag0, bf16[256,256]{1,0:T(8,128)(2,1)S(1)} %get-tuple-element.59.high1, ...), custom_call_target="tpu_custom_call" | custom-call | tf_op jit(solution)/shard_map/factor_rows/pallas_call | solution.py:398
  (30 shorter events, 0.3 us)
Async XLA Ops:
  0.0 8.8 %copy-start = (bf16[1,384,256]{2,1,0:T(8,128)(2,1)S(1)}, bf16[1,384,256]{2,1,0:T(8,128)(2,1)}, u32[]{:S(2)}) copy-start(bf16[1,384,256]{2,1,0:T(8,128)(2,1)} %param.13) | copy-start | bytes 589828
  0.0 8.8 %collective-permute-start = (bf16[384,256]{1,0:T(8,128)(2,1)}, bf16[384,256]{1,0:T(8,128)(2,1)S(1)}, u32[]{:S(2)}, u32[]{:S(2)}) collective-permute-start(bf16[384,256]{1,0:T(8,128)(2,1)} %bitcast.7), channel_id=1, source_target_pairs={{0,32},{8,40},{16,48},{24,56},{32,0},{40,8},{48,16},{56,24},{64,96... | collective-permute-start | bytes 589832 | tf_op jit(solution)/shard_map/ppermute | solution.py:419
  3.6 1.4 %copy-start.1 = (bf16[4,6,30,1024]{3,0,2,1:T(4,128)(2,1)S(1)}, bf16[4,6,30,1024]{3,0,2,1:T(4,128)(2,1)}, u32[]{:S(2)}) copy-start(bf16[4,6,30,1024]{3,0,2,1:T(4,128)(2,1)} %param.7) | copy-start | bytes 4423684
  5.0 6.0 %copy-start.2 = (bf16[4,6,30,1024]{3,0,2,1:T(4,128)(2,1)S(1)}, bf16[4,6,30,1024]{3,0,2,1:T(4,128)(2,1)}, u32[]{:S(2)}) copy-start(bf16[4,6,30,1024]{3,0,2,1:T(4,128)(2,1)} %param.7) | copy-start | bytes 4423684
  8.9 11.9 %collective-permute-start.4 = (bf16[2,384,256]{2,1,0:T(8,128)(2,1)S(1)}, bf16[2,384,256]{2,1,0:T(8,128)(2,1)S(1)}, u32[]{:S(2)}, u32[]{:S(2)}) collective-permute-start(bf16[2,384,256]{2,1,0:T(8,128)(2,1)S(1)} %pad_maximum_fusion.1), channel_id=1, source_target_pairs={{0,96},{8,104},{16,112},{24,120},{32,64},{40,72},{48,80},{56,88},{... | collective-permute-start | bytes 1179656 | tf_op jit(solution)/shard_map/ppermute | solution.py:419
  14.6 6.3 %collective-permute-start.2 = (f32[16,512]{1,0:T(8,128)S(1)}, f32[16,512]{1,0:T(8,128)S(1)}, u32[]{:S(2)}, u32[]{:S(2)}) collective-permute-start(f32[16,512]{1,0:T(8,128)S(1)} %get-tuple-element.39), channel_id=1, source_target_pairs={{0,126},{1,127},{2,0},{3,1},{4,2},{5,3},{6,4},{7,5},{8,6},{9,7},{1... | collective-permute-start | bytes 98312 | tf_op jit(solution)/shard_map/ppermute | solution.py:423
  15.0 5.8 %collective-permute-start.3 = (f32[16,512]{1,0:T(8,128)S(1)}, f32[16,512]{1,0:T(8,128)S(1)}, u32[]{:S(2)}, u32[]{:S(2)}) collective-permute-start(f32[16,512]{1,0:T(8,128)S(1)} %get-tuple-element.40), channel_id=1, source_target_pairs={{0,125},{1,126},{2,127},{3,0},{4,1},{5,2},{6,3},{7,4},{8,5},{9,6},... | collective-permute-start | bytes 98312 | tf_op jit(solution)/shard_map/ppermute | solution.py:423
  15.1 5.8 %collective-permute-start.1 = (f32[40,512]{1,0:T(8,128)S(1)}, f32[40,512]{1,0:T(8,128)S(1)}, u32[]{:S(2)}, u32[]{:S(2)}) collective-permute-start(f32[40,512]{1,0:T(8,128)S(1)} %get-tuple-element.38), channel_id=1, source_target_pairs={{0,127},{1,0},{2,1},{3,2},{4,3},{5,4},{6,5},{7,6},{8,7},{9,8},{10,... | collective-permute-start | bytes 245768 | tf_op jit(solution)/shard_map/ppermute | solution.py:423
  20.9 5.9 %collective-permute-start.5 = (f32[24,512]{1,0:T(8,128)S(1)}, f32[24,512]{1,0:T(8,128)S(1)}, u32[]{:S(2)}, u32[]{:S(2)}) collective-permute-start(f32[24,512]{1,0:T(8,128)S(1)} %pad_maximum_fusion.2), channel_id=1, source_target_pairs={{0,32},{8,40},{16,48},{24,56},{32,0},{40,8},{48,16},{56,24},{64,96... | collective-permute-start | bytes 147464 | tf_op jit(solution)/shard_map/ppermute | solution.py:419
  21.6 10.9 %collective-permute-start.8 = (bf16[384,256]{1,0:T(8,128)(2,1)S(1)}, bf16[384,256]{1,0:T(8,128)(2,1)S(1)}, u32[]{:S(2)}, u32[]{:S(2)}) collective-permute-start(bf16[384,256]{1,0:T(8,128)(2,1)S(1)} %select_bitcast_fusion.mine), channel_id=1, source_target_pairs={{0,24},{8,16},{16,8},{24,0},{32,56},{40,48},{48,40},{56,32},{64,88... | collective-permute-start | bytes 589832 | tf_op jit(solution)/shard_map/ppermute | solution.py:419
  26.8 7.3 %collective-permute-start.7 = (bf16[384,256]{1,0:T(8,128)(2,1)S(1)}, bf16[384,256]{1,0:T(8,128)(2,1)S(1)}, u32[]{:S(2)}, u32[]{:S(2)}) collective-permute-start(bf16[384,256]{1,0:T(8,128)(2,1)S(1)} %select_bitcast_fusion.mine), channel_id=1, source_target_pairs={{0,8},{8,0},{16,24},{24,16},{32,40},{40,32},{48,56},{56,48},{64,72... | collective-permute-start | bytes 589832 | tf_op jit(solution)/shard_map/ppermute | solution.py:419
  26.9 5.4 %collective-permute-start.6 = (f32[24,512]{1,0:T(8,128)S(1)}, f32[24,512]{1,0:T(8,128)S(1)}, u32[]{:S(2)}, u32[]{:S(2)}) collective-permute-start(f32[24,512]{1,0:T(8,128)S(1)} %fusion), channel_id=1, source_target_pairs={{0,96},{8,104},{16,112},{24,120},{32,64},{40,72},{48,80},{56,88},{... | collective-permute-start | bytes 147464 | tf_op jit(solution)/shard_map/ppermute | solution.py:419
  34.1 13.0 %collective-permute-start.11 = (bf16[384,256]{1,0:T(8,128)(2,1)S(1)}, bf16[384,256]{1,0:T(8,128)(2,1)S(1)}, u32[]{:S(2)}, u32[]{:S(2)}) collective-permute-start(bf16[384,256]{1,0:T(8,128)(2,1)S(1)} %collective-permute-done.8.across), channel_id=1, source_target_pairs={{0,8},{8,0},{16,24},{24,16},{32,40},{40,32},{48,56},{56,48},{64,72... | collective-permute-start | bytes 589832 | tf_op jit(solution)/shard_map/ppermute | solution.py:419
  34.4 7.3 %collective-permute-start.9 = (f32[24,512]{1,0:T(8,128)S(1)}, f32[24,512]{1,0:T(8,128)S(1)}, u32[]{:S(2)}, u32[]{:S(2)}) collective-permute-start(f32[24,512]{1,0:T(8,128)S(1)} %add.55), channel_id=1, source_target_pairs={{0,8},{8,0},{16,24},{24,16},{32,40},{40,32},{48,56},{56,48},{64,72... | collective-permute-start | bytes 147464 | tf_op jit(solution)/shard_map/ppermute | solution.py:419
  41.7 5.4 %collective-permute-start.10 = (f32[24,512]{1,0:T(8,128)S(1)}, f32[24,512]{1,0:T(8,128)S(1)}, u32[]{:S(2)}, u32[]{:S(2)}) collective-permute-start(f32[24,512]{1,0:T(8,128)S(1)} %add.56), channel_id=1, source_target_pairs={{0,24},{8,16},{16,8},{24,0},{32,56},{40,48},{48,40},{56,32},{64,88... | collective-permute-start | bytes 147464 | tf_op jit(solution)/shard_map/ppermute | solution.py:419
  47.1 21.6 %collective-permute-start.13 = (bf16[4,384,256]{2,1,0:T(8,128)(2,1)S(1)}, bf16[4,384,256]{2,1,0:T(8,128)(2,1)S(1)}, u32[]{:S(2)}, u32[]{:S(2)}) collective-permute-start(bf16[4,384,256]{2,1,0:T(8,128)(2,1)S(1)} %pad_maximum_fusion.here), channel_id=1, source_target_pairs={{0,24},{8,0},{16,8},{24,16},{32,56},{40,32},{48,40},{56,48},{64,88... | collective-permute-start | bytes 2359304 | tf_op jit(solution)/shard_map/ppermute | solution.py:415
  48.9 19.8 %collective-permute-start.12 = (bf16[4,384,256]{2,1,0:T(8,128)(2,1)S(1)}, bf16[4,384,256]{2,1,0:T(8,128)(2,1)S(1)}, u32[]{:S(2)}, u32[]{:S(2)}) collective-permute-start(bf16[4,384,256]{2,1,0:T(8,128)(2,1)S(1)} %pad_maximum_fusion.here), channel_id=1, source_target_pairs={{0,8},{8,16},{16,24},{24,0},{32,40},{40,48},{48,56},{56,32},{64,72... | collective-permute-start | bytes 2359304 | tf_op jit(solution)/shard_map/ppermute | solution.py:415
  49.2 19.5 %collective-permute-start.14 = (f32[12,512]{1,0:T(8,128)S(1)}, f32[12,512]{1,0:T(8,128)S(1)}, u32[]{:S(2)}, u32[]{:S(2)}) collective-permute-start(f32[12,512]{1,0:T(8,128)S(1)} %get-tuple-element.56), channel_id=1, source_target_pairs={{0,120},{1,121},{2,122},{3,123},{4,124},{5,125},{6,126},{7,127},{8... | collective-permute-start | bytes 73736 | tf_op jit(solution)/shard_map/ppermute | solution.py:423
  53.8 14.9 %collective-permute-start.15 = (f32[12,512]{1,0:T(8,128)S(1)}, f32[12,512]{1,0:T(8,128)S(1)}, u32[]{:S(2)}, u32[]{:S(2)}) collective-permute-start(f32[12,512]{1,0:T(8,128)S(1)} %get-tuple-element.57), channel_id=1, source_target_pairs={{0,64},{1,65},{2,66},{3,67},{4,68},{5,69},{6,70},{7,71},{8,72},{9,... | collective-permute-start | bytes 73736 | tf_op jit(solution)/shard_map/ppermute | solution.py:423
  68.8 9.0 %collective-permute-start.17 = (bf16[2,384,256]{2,1,0:T(8,128)(2,1)S(1)}, bf16[2,384,256]{2,1,0:T(8,128)(2,1)S(1)}, u32[]{:S(2)}, u32[]{:S(2)}) collective-permute-start(bf16[2,384,256]{2,1,0:T(8,128)(2,1)S(1)} %slice.55), channel_id=1, source_target_pairs={{0,24},{8,0},{16,8},{24,16},{32,56},{40,32},{48,40},{56,48},{64,88... | collective-permute-start | bytes 1179656 | tf_op jit(solution)/shard_map/ppermute | solution.py:415
  69.1 9.0 %collective-permute-start.16 = (bf16[2,384,256]{2,1,0:T(8,128)(2,1)S(1)}, bf16[2,384,256]{2,1,0:T(8,128)(2,1)S(1)}, u32[]{:S(2)}, u32[]{:S(2)}) collective-permute-start(bf16[2,384,256]{2,1,0:T(8,128)(2,1)S(1)} %slice.54), channel_id=1, source_target_pairs={{0,8},{8,16},{16,24},{24,0},{32,40},{40,48},{48,56},{56,32},{64,72... | collective-permute-start | bytes 1179656 | tf_op jit(solution)/shard_map/ppermute | solution.py:415

commit v5 on v4

--- a/solution.py
+++ b/solution.py
@@ -461,8 +461,8 @@
     lead, paired, crossed, near, half = lax.optimization_barrier((lead, paired, crossed, near, half))
     near, half = move_back(near, 8), move_back(half, 64)
     last_piece = swap(crossed, 1)
+    lead = lead + swap(lead, 3)
     lead = lead + swap(lead, 1)
-    lead = lead + swap(lead, 3)
     lead, last_piece, here = lax.optimization_barrier((lead, last_piece, here))
 
     before, after = move_y(here, 1), move_y(here, 3)

time: 84.5 us -> 81.3 us (0.962)
  waiting for transfers between devices: 20.6 us -> 18.5 us
  starting transfers between devices: 25.7 us -> 24.2 us
    ppermute x9, waiting for transfers between devices: 20.2 us -> 18.1 us  [swap(): return lax.ppermute(value, 'cand', [(i, i ^ bits) for i in range(16)])]
    ppermute x9, starting transfers between devices: 15.2 us -> 14.1 us  [swap(): return lax.ppermute(value, 'cand', [(i, i ^ bits) for i in range(16)])]
  transfers between devices with their start and end apart: 18 -> 18, of which waited for: 7 -> 7; matrix products, arithmetic and copies ran while one was open for 3% -> 3% of each run, Pallas kernels for 33% -> 35%
where the time goes in v5:
time: 81.3 us; the launch traced here: 80 us
  Pallas kernels  33.2 us (41%)
  starting transfers between devices  24.2 us (30%)
  waiting for transfers between devices  18.5 us (23%)
  other arithmetic  2.38 us (3%)
  local copies, waits for them, and re-layouts  1.43 us (2%)
    pallas_call x2, Pallas kernels, window_factor(): pl.pallas_call(functools.partial(window_kernel, part), in_specs=[vmem] *...  20.5 us
    ppermute x9, waiting for transfers between devices, swap(): return lax.ppermute(value, 'cand', [(i, i ^ bits) for i in range(16)])  18.1 us
    ppermute x9, starting transfers between devices, swap(): return lax.ppermute(value, 'cand', [(i, i ^ bits) for i in range(16)])  14.1 us
    pallas_call x2, Pallas kernels, stiffness_tiles(): pl.pallas_call(functools.partial(stiffness_kernel, begin), in_specs=[pl.B...  7.25 us
    ppermute x5, starting transfers between devices, move_back(): lax.ppermute(value, ('cand', 'dom'), [(i, (i - offset) % 128) for i in ra...  5.84 us
    pallas_call x1, Pallas kernels, factor_rows(): pl.pallas_call(rows_kernel, in_specs=[vmem] * len(operands), out_specs=pl...  5.44 us
    ppermute x4, starting transfers between devices, move_y(): lax.ppermute(value, 'cand', [(4 * x + y, 4 * x + (y + shift) % 4) for x i...  4.19 us
  transfers between devices with their start and end apart: 18, of which 7 were waited for; matrix products, arithmetic and copies ran while one was open for 3% of the time, Pallas kernels for 35%

profile of v5, /device:TPU:96, one launch (start us, length us, event | category | flops | bytes accessed | tf_op | source)
XLA Modules:
  0.0 80.0 jit_solution(3876619965631444531)
XLA Ops:
  0.0 1.5 %collective-permute-start = (bf16[384,256]{1,0:T(8,128)(2,1)}, bf16[384,256]{1,0:T(8,128)(2,1)S(1)}, u32[]{:S(2)}, u32[]{:S(2)}) collective-permute-start(bf16[384,256]{1,0:T(8,128)(2,1)} %bitcast.7), channel_id=1, source_target_pairs={{0,32},{8,40},{16,48},{24,56},{32,0},{40,8},{48,16},{56,24},{64,96... | collective-permute-start | bytes 589832 | tf_op jit(solution)/shard_map/ppermute | solution.py:419
  1.5 0.7 broadcast_multiply_fusion
  2.2 0.7 add.47
  2.9 0.8 pad_add_fusion.small
  3.7 1.4 %copy-done.1 = bf16[4,6,30,1024]{3,0,2,1:T(4,128)(2,1)S(1)} copy-done((bf16[4,6,30,1024]{3,0,2,1:T(4,128)(2,1)S(1)}, bf16[4,6,30,1024]{3,0,2,1:T(4,128)(2,1)}, u32[]{:S(2)}) %copy-start.1) | copy-done | bytes 1474584
  5.0 3.8 %stiffness_tiles.2.refs_0_ = f32[112,512]{1,0:T(8,128)S(1)} custom-call(bf16[6,30,4,1024]{3,2,1,0:T(4,128)(2,1)S(1)} %bitcast.11, f32[8,1024]{1,0:T(8,128)S(1)} %pad_add_fusion.small, s32[1,1024]{1,0:T(1,128)S(1)} %bitcast.9), custom_call_target="tpu_custom_call" | custom-call | flops 5000000000 | bytes 15000000 | tf_op jit(solution)/shard_map/stiffness_tiles/pallas_call | solution.py:201
  8.9 2.2 %collective-permute-start.4 = (bf16[2,384,256]{2,1,0:T(8,128)(2,1)S(1)}, bf16[2,384,256]{2,1,0:T(8,128)(2,1)S(1)}, u32[]{:S(2)}, u32[]{:S(2)}) collective-permute-start(bf16[2,384,256]{2,1,0:T(8,128)(2,1)S(1)} %pad_maximum_fusion.1), channel_id=1, source_target_pairs={{0,96},{8,104},{16,112},{24,120},{32,64},{40,72},{48,80},{56,88},{... | collective-permute-start | bytes 1179656 | tf_op jit(solution)/shard_map/ppermute | solution.py:419
  11.1 3.5 %stiffness_tiles.3 = (f32[40,512]{1,0:T(8,128)S(1)}, f32[40,512]{1,0:T(8,128)S(1)}, f32[16,512]{1,0:T(8,128)S(1)}, f32[16,512]{1,0:T(8,128)S(1)}) custom-call(bf16[6,30,4,1024]{3,2,1,0:T(4,128)(2,1)S(1)} %bitcast.12, f32[8,1024]{1,0:T(8,128)S(1)} %pad_add_fusion.small, s32[1,1024]{1,0:T(1,128)S(1)} %bitcast.10, f32[112,512]{1,0:T(8,128)S(1)} %stiffness_tiles.2.refs_0_), custom_call_target="tpu_custom_call" | custom-call | flops 5000000000 | bytes 15000000 | tf_op jit(solution)/shard_map/stiffness_tiles/pallas_call | solution.py:201
  14.6 0.5 collective-permute-start.2
  15.1 5.7 %collective-permute-done.4 = bf16[2,384,256]{2,1,0:T(8,128)(2,1)S(1)} collective-permute-done((bf16[2,384,256]{2,1,0:T(8,128)(2,1)S(1)}, bf16[2,384,256]{2,1,0:T(8,128)(2,1)S(1)}, u32[]{:S(2)}, u32[]{:S(2)}) %collective-permute-start.4) | collective-permute-done | bytes 393248 | tf_op jit(solution)/shard_map/ppermute | solution.py:419
  20.7 0.1 pad_maximum_fusion.here
  20.9 0.7 collective-permute-start.5
  21.6 5.2 %collective-permute-start.8 = (bf16[384,256]{1,0:T(8,128)(2,1)S(1)}, bf16[384,256]{1,0:T(8,128)(2,1)S(1)}, u32[]{:S(2)}, u32[]{:S(2)}) collective-permute-start(bf16[384,256]{1,0:T(8,128)(2,1)S(1)} %select_bitcast_fusion.mine), channel_id=1, source_target_pairs={{0,24},{8,16},{16,8},{24,0},{32,56},{40,48},{48,40},{56,32},{64,88... | collective-permute-start | bytes 589832 | tf_op jit(solution)/shard_map/ppermute | solution.py:419
  26.9 1.9 %collective-permute-start.6 = (f32[24,512]{1,0:T(8,128)S(1)}, f32[24,512]{1,0:T(8,128)S(1)}, u32[]{:S(2)}, u32[]{:S(2)}) collective-permute-start(f32[24,512]{1,0:T(8,128)S(1)} %fusion), channel_id=1, source_target_pairs={{0,96},{8,104},{16,112},{24,120},{32,64},{40,72},{48,80},{56,88},{... | collective-permute-start | bytes 147464 | tf_op jit(solution)/shard_map/ppermute | solution.py:419
  28.7 3.6 %collective-permute-done.6 = f32[24,512]{1,0:T(8,128)S(1)} collective-permute-done((f32[24,512]{1,0:T(8,128)S(1)}, f32[24,512]{1,0:T(8,128)S(1)}, u32[]{:S(2)}, u32[]{:S(2)}) %collective-permute-start.6) | collective-permute-done | bytes 49184 | tf_op jit(solution)/shard_map/ppermute | solution.py:419
  32.3 0.2 collective-permute-done.8.across
  32.5 1.6 %collective-permute-done.7.beside = bf16[384,256]{1,0:T(8,128)(2,1)S(1)} collective-permute-done((bf16[384,256]{1,0:T(8,128)(2,1)S(1)}, bf16[384,256]{1,0:T(8,128)(2,1)S(1)}, u32[]{:S(2)}, u32[]{:S(2)}) %collective-permute-start.7) | collective-permute-done | bytes 196640 | tf_op jit(solution)/shard_map/ppermute | solution.py:419
  34.1 0.3 collective-permute-start.11
  34.4 1.9 %collective-permute-start.9 = (f32[24,512]{1,0:T(8,128)S(1)}, f32[24,512]{1,0:T(8,128)S(1)}, u32[]{:S(2)}, u32[]{:S(2)}) collective-permute-start(f32[24,512]{1,0:T(8,128)S(1)} %add.55), channel_id=1, source_target_pairs={{0,24},{8,16},{16,8},{24,0},{32,56},{40,48},{48,40},{56,32},{64,88... | collective-permute-start | bytes 147464 | tf_op jit(solution)/shard_map/ppermute | solution.py:419
  36.3 3.4 %collective-permute-done.9 = f32[24,512]{1,0:T(8,128)S(1)} collective-permute-done((f32[24,512]{1,0:T(8,128)S(1)}, f32[24,512]{1,0:T(8,128)S(1)}, u32[]{:S(2)}, u32[]{:S(2)}) %collective-permute-start.9) | collective-permute-done | bytes 49184 | tf_op jit(solution)/shard_map/ppermute | solution.py:419
  39.7 0.6 collective-permute-start.10
  40.3 3.6 %collective-permute-done.10 = f32[24,512]{1,0:T(8,128)S(1)} collective-permute-done((f32[24,512]{1,0:T(8,128)S(1)}, f32[24,512]{1,0:T(8,128)S(1)}, u32[]{:S(2)}, u32[]{:S(2)}) %collective-permute-start.10) | collective-permute-done | bytes 49184 | tf_op jit(solution)/shard_map/ppermute | solution.py:419
  43.9 1.9 %collective-permute-start.13 = (bf16[4,384,256]{2,1,0:T(8,128)(2,1)S(1)}, bf16[4,384,256]{2,1,0:T(8,128)(2,1)S(1)}, u32[]{:S(2)}, u32[]{:S(2)}) collective-permute-start(bf16[4,384,256]{2,1,0:T(8,128)(2,1)S(1)} %pad_maximum_fusion.here), channel_id=1, source_target_pairs={{0,24},{8,0},{16,8},{24,16},{32,56},{40,32},{48,40},{56,48},{64,88... | collective-permute-start | bytes 2359304 | tf_op jit(solution)/shard_map/ppermute | solution.py:415
  45.8 0.2 collective-permute-start.12
  46.0 4.9 %collective-permute-start.14 = (f32[12,512]{1,0:T(8,128)S(1)}, f32[12,512]{1,0:T(8,128)S(1)}, u32[]{:S(2)}, u32[]{:S(2)}) collective-permute-start(f32[12,512]{1,0:T(8,128)S(1)} %get-tuple-element.56), channel_id=1, source_target_pairs={{0,120},{1,121},{2,122},{3,123},{4,124},{5,125},{6,126},{7,127},{8... | collective-permute-start | bytes 73736 | tf_op jit(solution)/shard_map/ppermute | solution.py:423
  50.9 0.5 collective-permute-start.15
  51.4 13.6 %window_factor.2 = (bf16[512,256]{1,0:T(8,128)(2,1)S(1)}, bf16[512,256]{1,0:T(8,128)(2,1)S(1)}, f32[256,256]{1,0:T(8,128)S(1)}, f32[512,128]{1,0:T(8,128)S(1)}) custom-call(f32[24,512]{1,0:T(8,128)S(1)} %add.57.lead, bf16[384,256]{1,0:T(8,128)(2,1)S(1)} %select_bitcast_fusion.mine, bf16[384,256]{1,0:T(8,128)(2,1)S(1)} %collective-permute-done.7.beside, ...), custom_call_target="tpu_custom_call" | custom-call | flops 5120000000 | bytes 51200000 | tf_op jit(solution)/shard_map/window_factor/pallas_call | solution.py:312
  65.1 0.3 collective-permute-start.17
  65.5 1.8 %collective-permute-start.16 = (bf16[2,384,256]{2,1,0:T(8,128)(2,1)S(1)}, bf16[2,384,256]{2,1,0:T(8,128)(2,1)S(1)}, u32[]{:S(2)}, u32[]{:S(2)}) collective-permute-start(bf16[2,384,256]{2,1,0:T(8,128)(2,1)S(1)} %slice.54), channel_id=1, source_target_pairs={{0,8},{8,16},{16,24},{24,0},{32,40},{40,48},{48,56},{56,32},{64,72... | collective-permute-start | bytes 1179656 | tf_op jit(solution)/shard_map/ppermute | solution.py:415
  67.2 6.9 %window_factor.3 = (bf16[256,256]{1,0:T(8,128)(2,1)S(1)}, bf16[256,256]{1,0:T(8,128)(2,1)S(1)}, f32[256,256]{1,0:T(8,128)S(1)}, f32[256,128]{1,0:T(8,128)S(1)}) custom-call(f32[24,512]{1,0:T(8,128)S(1)} %add.57.lead, bf16[384,256]{1,0:T(8,128)(2,1)S(1)} %select_bitcast_fusion.mine, bf16[384,256]{1,0:T(8,128)(2,1)S(1)} %collective-permute-done.7.beside, ...), custom_call_target="tpu_custom_call" | custom-call | flops 2560000000 | bytes 25600000 | tf_op jit(solution)/shard_map/window_factor/pallas_call | solution.py:312
  74.1 0.3 collective-permute-done.16.low
  74.4 5.4 %factor_rows.1 = f32[1,384,6144]{2,1,0:T(8,128)} custom-call(bf16[512,256]{1,0:T(8,128)(2,1)S(1)} %get-tuple-element.51.high0, bf16[512,256]{1,0:T(8,128)(2,1)S(1)} %get-tuple-element.52.low0, f32[512,128]{1,0:T(8,128)S(1)} %get-tuple-element.53.diag0, bf16[256,256]{1,0:T(8,128)(2,1)S(1)} %get-tuple-element.59.high1, ...), custom_call_target="tpu_custom_call" | custom-call | tf_op jit(solution)/shard_map/factor_rows/pallas_call | solution.py:398
  (30 shorter events, 0.3 us)
Async XLA Ops:
  0.0 8.8 %copy-start = (bf16[1,384,256]{2,1,0:T(8,128)(2,1)S(1)}, bf16[1,384,256]{2,1,0:T(8,128)(2,1)}, u32[]{:S(2)}) copy-start(bf16[1,384,256]{2,1,0:T(8,128)(2,1)} %param.13) | copy-start | bytes 589828
  0.0 8.8 %collective-permute-start = (bf16[384,256]{1,0:T(8,128)(2,1)}, bf16[384,256]{1,0:T(8,128)(2,1)S(1)}, u32[]{:S(2)}, u32[]{:S(2)}) collective-permute-start(bf16[384,256]{1,0:T(8,128)(2,1)} %bitcast.7), channel_id=1, source_target_pairs={{0,32},{8,40},{16,48},{24,56},{32,0},{40,8},{48,16},{56,24},{64,96... | collective-permute-start | bytes 589832 | tf_op jit(solution)/shard_map/ppermute | solution.py:419
  3.6 1.4 %copy-start.1 = (bf16[4,6,30,1024]{3,0,2,1:T(4,128)(2,1)S(1)}, bf16[4,6,30,1024]{3,0,2,1:T(4,128)(2,1)}, u32[]{:S(2)}) copy-start(bf16[4,6,30,1024]{3,0,2,1:T(4,128)(2,1)} %param.7) | copy-start | bytes 4423684
  5.0 6.0 %copy-start.2 = (bf16[4,6,30,1024]{3,0,2,1:T(4,128)(2,1)S(1)}, bf16[4,6,30,1024]{3,0,2,1:T(4,128)(2,1)}, u32[]{:S(2)}) copy-start(bf16[4,6,30,1024]{3,0,2,1:T(4,128)(2,1)} %param.7) | copy-start | bytes 4423684
  8.9 11.9 %collective-permute-start.4 = (bf16[2,384,256]{2,1,0:T(8,128)(2,1)S(1)}, bf16[2,384,256]{2,1,0:T(8,128)(2,1)S(1)}, u32[]{:S(2)}, u32[]{:S(2)}) collective-permute-start(bf16[2,384,256]{2,1,0:T(8,128)(2,1)S(1)} %pad_maximum_fusion.1), channel_id=1, source_target_pairs={{0,96},{8,104},{16,112},{24,120},{32,64},{40,72},{48,80},{56,88},{... | collective-permute-start | bytes 1179656 | tf_op jit(solution)/shard_map/ppermute | solution.py:419
  14.6 6.3 %collective-permute-start.2 = (f32[16,512]{1,0:T(8,128)S(1)}, f32[16,512]{1,0:T(8,128)S(1)}, u32[]{:S(2)}, u32[]{:S(2)}) collective-permute-start(f32[16,512]{1,0:T(8,128)S(1)} %get-tuple-element.39), channel_id=1, source_target_pairs={{0,126},{1,127},{2,0},{3,1},{4,2},{5,3},{6,4},{7,5},{8,6},{9,7},{1... | collective-permute-start | bytes 98312 | tf_op jit(solution)/shard_map/ppermute | solution.py:423
  15.0 5.8 %collective-permute-start.3 = (f32[16,512]{1,0:T(8,128)S(1)}, f32[16,512]{1,0:T(8,128)S(1)}, u32[]{:S(2)}, u32[]{:S(2)}) collective-permute-start(f32[16,512]{1,0:T(8,128)S(1)} %get-tuple-element.40), channel_id=1, source_target_pairs={{0,125},{1,126},{2,127},{3,0},{4,1},{5,2},{6,3},{7,4},{8,5},{9,6},... | collective-permute-start | bytes 98312 | tf_op jit(solution)/shard_map/ppermute | solution.py:423
  15.1 5.8 %collective-permute-start.1 = (f32[40,512]{1,0:T(8,128)S(1)}, f32[40,512]{1,0:T(8,128)S(1)}, u32[]{:S(2)}, u32[]{:S(2)}) collective-permute-start(f32[40,512]{1,0:T(8,128)S(1)} %get-tuple-element.38), channel_id=1, source_target_pairs={{0,127},{1,0},{2,1},{3,2},{4,3},{5,4},{6,5},{7,6},{8,7},{9,8},{10,... | collective-permute-start | bytes 245768 | tf_op jit(solution)/shard_map/ppermute | solution.py:423
  20.9 5.9 %collective-permute-start.5 = (f32[24,512]{1,0:T(8,128)S(1)}, f32[24,512]{1,0:T(8,128)S(1)}, u32[]{:S(2)}, u32[]{:S(2)}) collective-permute-start(f32[24,512]{1,0:T(8,128)S(1)} %pad_maximum_fusion.2), channel_id=1, source_target_pairs={{0,32},{8,40},{16,48},{24,56},{32,0},{40,8},{48,16},{56,24},{64,96... | collective-permute-start | bytes 147464 | tf_op jit(solution)/shard_map/ppermute | solution.py:419
  21.6 10.9 %collective-permute-start.8 = (bf16[384,256]{1,0:T(8,128)(2,1)S(1)}, bf16[384,256]{1,0:T(8,128)(2,1)S(1)}, u32[]{:S(2)}, u32[]{:S(2)}) collective-permute-start(bf16[384,256]{1,0:T(8,128)(2,1)S(1)} %select_bitcast_fusion.mine), channel_id=1, source_target_pairs={{0,24},{8,16},{16,8},{24,0},{32,56},{40,48},{48,40},{56,32},{64,88... | collective-permute-start | bytes 589832 | tf_op jit(solution)/shard_map/ppermute | solution.py:419
  26.8 7.3 %collective-permute-start.7 = (bf16[384,256]{1,0:T(8,128)(2,1)S(1)}, bf16[384,256]{1,0:T(8,128)(2,1)S(1)}, u32[]{:S(2)}, u32[]{:S(2)}) collective-permute-start(bf16[384,256]{1,0:T(8,128)(2,1)S(1)} %select_bitcast_fusion.mine), channel_id=1, source_target_pairs={{0,8},{8,0},{16,24},{24,16},{32,40},{40,32},{48,56},{56,48},{64,72... | collective-permute-start | bytes 589832 | tf_op jit(solution)/shard_map/ppermute | solution.py:419
  26.9 5.4 %collective-permute-start.6 = (f32[24,512]{1,0:T(8,128)S(1)}, f32[24,512]{1,0:T(8,128)S(1)}, u32[]{:S(2)}, u32[]{:S(2)}) collective-permute-start(f32[24,512]{1,0:T(8,128)S(1)} %fusion), channel_id=1, source_target_pairs={{0,96},{8,104},{16,112},{24,120},{32,64},{40,72},{48,80},{56,88},{... | collective-permute-start | bytes 147464 | tf_op jit(solution)/shard_map/ppermute | solution.py:419
  34.1 9.8 %collective-permute-start.11 = (bf16[384,256]{1,0:T(8,128)(2,1)S(1)}, bf16[384,256]{1,0:T(8,128)(2,1)S(1)}, u32[]{:S(2)}, u32[]{:S(2)}) collective-permute-start(bf16[384,256]{1,0:T(8,128)(2,1)S(1)} %collective-permute-done.8.across), channel_id=1, source_target_pairs={{0,8},{8,0},{16,24},{24,16},{32,40},{40,32},{48,56},{56,48},{64,72... | collective-permute-start | bytes 589832 | tf_op jit(solution)/shard_map/ppermute | solution.py:419
  34.4 5.3 %collective-permute-start.9 = (f32[24,512]{1,0:T(8,128)S(1)}, f32[24,512]{1,0:T(8,128)S(1)}, u32[]{:S(2)}, u32[]{:S(2)}) collective-permute-start(f32[24,512]{1,0:T(8,128)S(1)} %add.55), channel_id=1, source_target_pairs={{0,24},{8,16},{16,8},{24,0},{32,56},{40,48},{48,40},{56,32},{64,88... | collective-permute-start | bytes 147464 | tf_op jit(solution)/shard_map/ppermute | solution.py:419
  39.7 4.2 %collective-permute-start.10 = (f32[24,512]{1,0:T(8,128)S(1)}, f32[24,512]{1,0:T(8,128)S(1)}, u32[]{:S(2)}, u32[]{:S(2)}) collective-permute-start(f32[24,512]{1,0:T(8,128)S(1)} %add.56), channel_id=1, source_target_pairs={{0,8},{8,0},{16,24},{24,16},{32,40},{40,32},{48,56},{56,48},{64,72... | collective-permute-start | bytes 147464 | tf_op jit(solution)/shard_map/ppermute | solution.py:419
  43.9 21.1 %collective-permute-start.13 = (bf16[4,384,256]{2,1,0:T(8,128)(2,1)S(1)}, bf16[4,384,256]{2,1,0:T(8,128)(2,1)S(1)}, u32[]{:S(2)}, u32[]{:S(2)}) collective-permute-start(bf16[4,384,256]{2,1,0:T(8,128)(2,1)S(1)} %pad_maximum_fusion.here), channel_id=1, source_target_pairs={{0,24},{8,0},{16,8},{24,16},{32,56},{40,32},{48,40},{56,48},{64,88... | collective-permute-start | bytes 2359304 | tf_op jit(solution)/shard_map/ppermute | solution.py:415
  45.8 19.2 %collective-permute-start.12 = (bf16[4,384,256]{2,1,0:T(8,128)(2,1)S(1)}, bf16[4,384,256]{2,1,0:T(8,128)(2,1)S(1)}, u32[]{:S(2)}, u32[]{:S(2)}) collective-permute-start(bf16[4,384,256]{2,1,0:T(8,128)(2,1)S(1)} %pad_maximum_fusion.here), channel_id=1, source_target_pairs={{0,8},{8,16},{16,24},{24,0},{32,40},{40,48},{48,56},{56,32},{64,72... | collective-permute-start | bytes 2359304 | tf_op jit(solution)/shard_map/ppermute | solution.py:415
  46.0 19.0 %collective-permute-start.14 = (f32[12,512]{1,0:T(8,128)S(1)}, f32[12,512]{1,0:T(8,128)S(1)}, u32[]{:S(2)}, u32[]{:S(2)}) collective-permute-start(f32[12,512]{1,0:T(8,128)S(1)} %get-tuple-element.56), channel_id=1, source_target_pairs={{0,120},{1,121},{2,122},{3,123},{4,124},{5,125},{6,126},{7,127},{8... | collective-permute-start | bytes 73736 | tf_op jit(solution)/shard_map/ppermute | solution.py:423
  50.9 14.2 %collective-permute-start.15 = (f32[12,512]{1,0:T(8,128)S(1)}, f32[12,512]{1,0:T(8,128)S(1)}, u32[]{:S(2)}, u32[]{:S(2)}) collective-permute-start(f32[12,512]{1,0:T(8,128)S(1)} %get-tuple-element.57), channel_id=1, source_target_pairs={{0,64},{1,65},{2,66},{3,67},{4,68},{5,69},{6,70},{7,71},{8,72},{9,... | collective-permute-start | bytes 73736 | tf_op jit(solution)/shard_map/ppermute | solution.py:423
  65.1 9.0 %collective-permute-start.17 = (bf16[2,384,256]{2,1,0:T(8,128)(2,1)S(1)}, bf16[2,384,256]{2,1,0:T(8,128)(2,1)S(1)}, u32[]{:S(2)}, u32[]{:S(2)}) collective-permute-start(bf16[2,384,256]{2,1,0:T(8,128)(2,1)S(1)} %slice.55), channel_id=1, source_target_pairs={{0,24},{8,0},{16,8},{24,16},{32,56},{40,32},{48,40},{56,48},{64,88... | collective-permute-start | bytes 1179656 | tf_op jit(solution)/shard_map/ppermute | solution.py:415
  65.5 9.0 %collective-permute-start.16 = (bf16[2,384,256]{2,1,0:T(8,128)(2,1)S(1)}, bf16[2,384,256]{2,1,0:T(8,128)(2,1)S(1)}, u32[]{:S(2)}, u32[]{:S(2)}) collective-permute-start(bf16[2,384,256]{2,1,0:T(8,128)(2,1)S(1)} %slice.54), channel_id=1, source_target_pairs={{0,8},{8,16},{16,24},{24,0},{32,40},{40,48},{48,56},{56,32},{64,72... | collective-permute-start | bytes 1179656 | tf_op jit(solution)/shard_map/ppermute | solution.py:415

commit v6 on v5

--- a/solution.py
+++ b/solution.py
@@ -359,6 +359,7 @@
     q = jnp.where(cand < 2, 0.0, q)
     q1 = q.astype(BF16)
     q2 = (q - q1.astype(F32)).astype(BF16)
+    q12 = jnp.concatenate([q1, q2], axis=1)
     stores = []
     for n, pieces in enumerate((here, before, after, (low, high))):
         column_y = lax.rem(y + (0, 3, 1, 2)[n], 4)
@@ -366,7 +367,7 @@
             v = pieces[pair][...] if n == 3 else pieces[2 * pair:2 * pair + 2]
             v = v.reshape(2 * W, RANK)
             slot = 2 * n + pair
-            blocks[slot] = dot_nt(q1, v) + dot_nt(q2, v)
+            blocks[slot] = dot_nt(q12, jnp.concatenate([v, v], axis=1))
             if slot == 0:
                 @pl.when(cand >= 2)
                 def _():

time: 81.3 us -> 81.3 us (level)
  no operation moved by 1% of the time
where the time goes in v6:
time: 81.3 us; the launch traced here: 80 us
  Pallas kernels  33.2 us (41%)
  starting transfers between devices  24.2 us (30%)
  waiting for transfers between devices  18.5 us (23%)
  other arithmetic  2.38 us (3%)
  local copies, waits for them, and re-layouts  1.43 us (2%)
    pallas_call x2, Pallas kernels, window_factor(): pl.pallas_call(functools.partial(window_kernel, part), in_specs=[vmem] *...  20.5 us
    ppermute x9, waiting for transfers between devices, swap(): return lax.ppermute(value, 'cand', [(i, i ^ bits) for i in range(16)])  18.1 us
    ppermute x9, starting transfers between devices, swap(): return lax.ppermute(value, 'cand', [(i, i ^ bits) for i in range(16)])  14.1 us
    pallas_call x2, Pallas kernels, stiffness_tiles(): pl.pallas_call(functools.partial(stiffness_kernel, begin), in_specs=[pl.B...  7.25 us
    ppermute x5, starting transfers between devices, move_back(): lax.ppermute(value, ('cand', 'dom'), [(i, (i - offset) % 128) for i in ra...  5.84 us
    pallas_call x1, Pallas kernels, factor_rows(): pl.pallas_call(rows_kernel, in_specs=[vmem] * len(operands), out_specs=pl...  5.43 us
    ppermute x4, starting transfers between devices, move_y(): lax.ppermute(value, 'cand', [(4 * x + y, 4 * x + (y + shift) % 4) for x i...  4.19 us
  transfers between devices with their start and end apart: 18, of which 7 were waited for; matrix products, arithmetic and copies ran while one was open for 3% of the time, Pallas kernels for 35%

profile of v6, /device:TPU:96, one launch (start us, length us, event | category | flops | bytes accessed | tf_op | source)
XLA Modules:
  0.0 80.0 jit_solution(5340040309061068915)
XLA Ops:
  0.0 1.5 %collective-permute-start = (bf16[384,256]{1,0:T(8,128)(2,1)}, bf16[384,256]{1,0:T(8,128)(2,1)S(1)}, u32[]{:S(2)}, u32[]{:S(2)}) collective-permute-start(bf16[384,256]{1,0:T(8,128)(2,1)} %bitcast.7), channel_id=1, source_target_pairs={{0,32},{8,40},{16,48},{24,56},{32,0},{40,8},{48,16},{56,24},{64,96... | collective-permute-start | bytes 589832 | tf_op jit(solution)/shard_map/ppermute | solution.py:420
  1.5 0.7 broadcast_multiply_fusion
  2.2 0.7 add.47
  2.9 0.8 pad_add_fusion.small
  3.7 1.4 %copy-done.1 = bf16[4,6,30,1024]{3,0,2,1:T(4,128)(2,1)S(1)} copy-done((bf16[4,6,30,1024]{3,0,2,1:T(4,128)(2,1)S(1)}, bf16[4,6,30,1024]{3,0,2,1:T(4,128)(2,1)}, u32[]{:S(2)}) %copy-start.1) | copy-done | bytes 1474584
  5.0 3.8 %stiffness_tiles.2.refs_0_ = f32[112,512]{1,0:T(8,128)S(1)} custom-call(bf16[6,30,4,1024]{3,2,1,0:T(4,128)(2,1)S(1)} %bitcast.11, f32[8,1024]{1,0:T(8,128)S(1)} %pad_add_fusion.small, s32[1,1024]{1,0:T(1,128)S(1)} %bitcast.9), custom_call_target="tpu_custom_call" | custom-call | flops 5000000000 | bytes 15000000 | tf_op jit(solution)/shard_map/stiffness_tiles/pallas_call | solution.py:201
  8.9 2.2 %collective-permute-start.4 = (bf16[2,384,256]{2,1,0:T(8,128)(2,1)S(1)}, bf16[2,384,256]{2,1,0:T(8,128)(2,1)S(1)}, u32[]{:S(2)}, u32[]{:S(2)}) collective-permute-start(bf16[2,384,256]{2,1,0:T(8,128)(2,1)S(1)} %pad_maximum_fusion.1), channel_id=1, source_target_pairs={{0,96},{8,104},{16,112},{24,120},{32,64},{40,72},{48,80},{56,88},{... | collective-permute-start | bytes 1179656 | tf_op jit(solution)/shard_map/ppermute | solution.py:420
  11.1 3.5 %stiffness_tiles.3 = (f32[40,512]{1,0:T(8,128)S(1)}, f32[40,512]{1,0:T(8,128)S(1)}, f32[16,512]{1,0:T(8,128)S(1)}, f32[16,512]{1,0:T(8,128)S(1)}) custom-call(bf16[6,30,4,1024]{3,2,1,0:T(4,128)(2,1)S(1)} %bitcast.12, f32[8,1024]{1,0:T(8,128)S(1)} %pad_add_fusion.small, s32[1,1024]{1,0:T(1,128)S(1)} %bitcast.10, f32[112,512]{1,0:T(8,128)S(1)} %stiffness_tiles.2.refs_0_), custom_call_target="tpu_custom_call" | custom-call | flops 5000000000 | bytes 15000000 | tf_op jit(solution)/shard_map/stiffness_tiles/pallas_call | solution.py:201
  14.6 0.5 collective-permute-start.2
  15.1 5.7 %collective-permute-done.4 = bf16[2,384,256]{2,1,0:T(8,128)(2,1)S(1)} collective-permute-done((bf16[2,384,256]{2,1,0:T(8,128)(2,1)S(1)}, bf16[2,384,256]{2,1,0:T(8,128)(2,1)S(1)}, u32[]{:S(2)}, u32[]{:S(2)}) %collective-permute-start.4) | collective-permute-done | bytes 393248 | tf_op jit(solution)/shard_map/ppermute | solution.py:420
  20.7 0.1 pad_maximum_fusion.here
  20.9 0.7 collective-permute-start.5
  21.6 5.2 %collective-permute-start.8 = (bf16[384,256]{1,0:T(8,128)(2,1)S(1)}, bf16[384,256]{1,0:T(8,128)(2,1)S(1)}, u32[]{:S(2)}, u32[]{:S(2)}) collective-permute-start(bf16[384,256]{1,0:T(8,128)(2,1)S(1)} %select_bitcast_fusion.mine), channel_id=1, source_target_pairs={{0,24},{8,16},{16,8},{24,0},{32,56},{40,48},{48,40},{56,32},{64,88... | collective-permute-start | bytes 589832 | tf_op jit(solution)/shard_map/ppermute | solution.py:420
  26.9 1.9 %collective-permute-start.6 = (f32[24,512]{1,0:T(8,128)S(1)}, f32[24,512]{1,0:T(8,128)S(1)}, u32[]{:S(2)}, u32[]{:S(2)}) collective-permute-start(f32[24,512]{1,0:T(8,128)S(1)} %fusion), channel_id=1, source_target_pairs={{0,96},{8,104},{16,112},{24,120},{32,64},{40,72},{48,80},{56,88},{... | collective-permute-start | bytes 147464 | tf_op jit(solution)/shard_map/ppermute | solution.py:420
  28.7 3.6 %collective-permute-done.6 = f32[24,512]{1,0:T(8,128)S(1)} collective-permute-done((f32[24,512]{1,0:T(8,128)S(1)}, f32[24,512]{1,0:T(8,128)S(1)}, u32[]{:S(2)}, u32[]{:S(2)}) %collective-permute-start.6) | collective-permute-done | bytes 49184 | tf_op jit(solution)/shard_map/ppermute | solution.py:420
  32.3 0.2 collective-permute-done.8.across
  32.5 1.6 %collective-permute-done.7.beside = bf16[384,256]{1,0:T(8,128)(2,1)S(1)} collective-permute-done((bf16[384,256]{1,0:T(8,128)(2,1)S(1)}, bf16[384,256]{1,0:T(8,128)(2,1)S(1)}, u32[]{:S(2)}, u32[]{:S(2)}) %collective-permute-start.7) | collective-permute-done | bytes 196640 | tf_op jit(solution)/shard_map/ppermute | solution.py:420
  34.1 0.3 collective-permute-start.11
  34.4 1.9 %collective-permute-start.9 = (f32[24,512]{1,0:T(8,128)S(1)}, f32[24,512]{1,0:T(8,128)S(1)}, u32[]{:S(2)}, u32[]{:S(2)}) collective-permute-start(f32[24,512]{1,0:T(8,128)S(1)} %add.55), channel_id=1, source_target_pairs={{0,24},{8,16},{16,8},{24,0},{32,56},{40,48},{48,40},{56,32},{64,88... | collective-permute-start | bytes 147464 | tf_op jit(solution)/shard_map/ppermute | solution.py:420
  36.3 3.4 %collective-permute-done.9 = f32[24,512]{1,0:T(8,128)S(1)} collective-permute-done((f32[24,512]{1,0:T(8,128)S(1)}, f32[24,512]{1,0:T(8,128)S(1)}, u32[]{:S(2)}, u32[]{:S(2)}) %collective-permute-start.9) | collective-permute-done | bytes 49184 | tf_op jit(solution)/shard_map/ppermute | solution.py:420
  39.7 0.6 collective-permute-start.10
  40.3 3.6 %collective-permute-done.10 = f32[24,512]{1,0:T(8,128)S(1)} collective-permute-done((f32[24,512]{1,0:T(8,128)S(1)}, f32[24,512]{1,0:T(8,128)S(1)}, u32[]{:S(2)}, u32[]{:S(2)}) %collective-permute-start.10) | collective-permute-done | bytes 49184 | tf_op jit(solution)/shard_map/ppermute | solution.py:420
  43.9 1.9 %collective-permute-start.13 = (bf16[4,384,256]{2,1,0:T(8,128)(2,1)S(1)}, bf16[4,384,256]{2,1,0:T(8,128)(2,1)S(1)}, u32[]{:S(2)}, u32[]{:S(2)}) collective-permute-start(bf16[4,384,256]{2,1,0:T(8,128)(2,1)S(1)} %pad_maximum_fusion.here), channel_id=1, source_target_pairs={{0,24},{8,0},{16,8},{24,16},{32,56},{40,32},{48,40},{56,48},{64,88... | collective-permute-start | bytes 2359304 | tf_op jit(solution)/shard_map/ppermute | solution.py:416
  45.8 0.2 collective-permute-start.12
  46.0 4.9 %collective-permute-start.14 = (f32[12,512]{1,0:T(8,128)S(1)}, f32[12,512]{1,0:T(8,128)S(1)}, u32[]{:S(2)}, u32[]{:S(2)}) collective-permute-start(f32[12,512]{1,0:T(8,128)S(1)} %get-tuple-element.56), channel_id=1, source_target_pairs={{0,120},{1,121},{2,122},{3,123},{4,124},{5,125},{6,126},{7,127},{8... | collective-permute-start | bytes 73736 | tf_op jit(solution)/shard_map/ppermute | solution.py:424
  50.9 0.5 collective-permute-start.15
  51.4 13.6 %window_factor.2 = (bf16[512,256]{1,0:T(8,128)(2,1)S(1)}, bf16[512,256]{1,0:T(8,128)(2,1)S(1)}, f32[256,256]{1,0:T(8,128)S(1)}, f32[512,128]{1,0:T(8,128)S(1)}) custom-call(f32[24,512]{1,0:T(8,128)S(1)} %add.57.lead, bf16[384,256]{1,0:T(8,128)(2,1)S(1)} %select_bitcast_fusion.mine, bf16[384,256]{1,0:T(8,128)(2,1)S(1)} %collective-permute-done.7.beside, ...), custom_call_target="tpu_custom_call" | custom-call | flops 5120000000 | bytes 51200000 | tf_op jit(solution)/shard_map/window_factor/pallas_call | solution.py:312
  65.1 0.3 collective-permute-start.17
  65.5 1.8 %collective-permute-start.16 = (bf16[2,384,256]{2,1,0:T(8,128)(2,1)S(1)}, bf16[2,384,256]{2,1,0:T(8,128)(2,1)S(1)}, u32[]{:S(2)}, u32[]{:S(2)}) collective-permute-start(bf16[2,384,256]{2,1,0:T(8,128)(2,1)S(1)} %slice.54), channel_id=1, source_target_pairs={{0,8},{8,16},{16,24},{24,0},{32,40},{40,48},{48,56},{56,32},{64,72... | collective-permute-start | bytes 1179656 | tf_op jit(solution)/shard_map/ppermute | solution.py:416
  67.2 6.9 %window_factor.3 = (bf16[256,256]{1,0:T(8,128)(2,1)S(1)}, bf16[256,256]{1,0:T(8,128)(2,1)S(1)}, f32[256,256]{1,0:T(8,128)S(1)}, f32[256,128]{1,0:T(8,128)S(1)}) custom-call(f32[24,512]{1,0:T(8,128)S(1)} %add.57.lead, bf16[384,256]{1,0:T(8,128)(2,1)S(1)} %select_bitcast_fusion.mine, bf16[384,256]{1,0:T(8,128)(2,1)S(1)} %collective-permute-done.7.beside, ...), custom_call_target="tpu_custom_call" | custom-call | flops 2560000000 | bytes 25600000 | tf_op jit(solution)/shard_map/window_factor/pallas_call | solution.py:312
  74.1 0.3 collective-permute-done.16.low
  74.4 5.4 %factor_rows.1 = f32[1,384,6144]{2,1,0:T(8,128)} custom-call(bf16[512,256]{1,0:T(8,128)(2,1)S(1)} %get-tuple-element.51.high0, bf16[512,256]{1,0:T(8,128)(2,1)S(1)} %get-tuple-element.52.low0, f32[512,128]{1,0:T(8,128)S(1)} %get-tuple-element.53.diag0, bf16[256,256]{1,0:T(8,128)(2,1)S(1)} %get-tuple-element.59.high1, ...), custom_call_target="tpu_custom_call" | custom-call | tf_op jit(solution)/shard_map/factor_rows/pallas_call | solution.py:399
  (30 shorter events, 0.3 us)
Async XLA Ops:
  0.0 8.8 %copy-start = (bf16[1,384,256]{2,1,0:T(8,128)(2,1)S(1)}, bf16[1,384,256]{2,1,0:T(8,128)(2,1)}, u32[]{:S(2)}) copy-start(bf16[1,384,256]{2,1,0:T(8,128)(2,1)} %param.13) | copy-start | bytes 589828
  0.0 8.8 %collective-permute-start = (bf16[384,256]{1,0:T(8,128)(2,1)}, bf16[384,256]{1,0:T(8,128)(2,1)S(1)}, u32[]{:S(2)}, u32[]{:S(2)}) collective-permute-start(bf16[384,256]{1,0:T(8,128)(2,1)} %bitcast.7), channel_id=1, source_target_pairs={{0,32},{8,40},{16,48},{24,56},{32,0},{40,8},{48,16},{56,24},{64,96... | collective-permute-start | bytes 589832 | tf_op jit(solution)/shard_map/ppermute | solution.py:420
  3.6 1.4 %copy-start.1 = (bf16[4,6,30,1024]{3,0,2,1:T(4,128)(2,1)S(1)}, bf16[4,6,30,1024]{3,0,2,1:T(4,128)(2,1)}, u32[]{:S(2)}) copy-start(bf16[4,6,30,1024]{3,0,2,1:T(4,128)(2,1)} %param.7) | copy-start | bytes 4423684
  5.0 6.0 %copy-start.2 = (bf16[4,6,30,1024]{3,0,2,1:T(4,128)(2,1)S(1)}, bf16[4,6,30,1024]{3,0,2,1:T(4,128)(2,1)}, u32[]{:S(2)}) copy-start(bf16[4,6,30,1024]{3,0,2,1:T(4,128)(2,1)} %param.7) | copy-start | bytes 4423684
  8.9 11.9 %collective-permute-start.4 = (bf16[2,384,256]{2,1,0:T(8,128)(2,1)S(1)}, bf16[2,384,256]{2,1,0:T(8,128)(2,1)S(1)}, u32[]{:S(2)}, u32[]{:S(2)}) collective-permute-start(bf16[2,384,256]{2,1,0:T(8,128)(2,1)S(1)} %pad_maximum_fusion.1), channel_id=1, source_target_pairs={{0,96},{8,104},{16,112},{24,120},{32,64},{40,72},{48,80},{56,88},{... | collective-permute-start | bytes 1179656 | tf_op jit(solution)/shard_map/ppermute | solution.py:420
  14.6 6.3 %collective-permute-start.2 = (f32[16,512]{1,0:T(8,128)S(1)}, f32[16,512]{1,0:T(8,128)S(1)}, u32[]{:S(2)}, u32[]{:S(2)}) collective-permute-start(f32[16,512]{1,0:T(8,128)S(1)} %get-tuple-element.39), channel_id=1, source_target_pairs={{0,126},{1,127},{2,0},{3,1},{4,2},{5,3},{6,4},{7,5},{8,6},{9,7},{1... | collective-permute-start | bytes 98312 | tf_op jit(solution)/shard_map/ppermute | solution.py:424
  15.0 5.8 %collective-permute-start.3 = (f32[16,512]{1,0:T(8,128)S(1)}, f32[16,512]{1,0:T(8,128)S(1)}, u32[]{:S(2)}, u32[]{:S(2)}) collective-permute-start(f32[16,512]{1,0:T(8,128)S(1)} %get-tuple-element.40), channel_id=1, source_target_pairs={{0,125},{1,126},{2,127},{3,0},{4,1},{5,2},{6,3},{7,4},{8,5},{9,6},... | collective-permute-start | bytes 98312 | tf_op jit(solution)/shard_map/ppermute | solution.py:424
  15.1 5.8 %collective-permute-start.1 = (f32[40,512]{1,0:T(8,128)S(1)}, f32[40,512]{1,0:T(8,128)S(1)}, u32[]{:S(2)}, u32[]{:S(2)}) collective-permute-start(f32[40,512]{1,0:T(8,128)S(1)} %get-tuple-element.38), channel_id=1, source_target_pairs={{0,127},{1,0},{2,1},{3,2},{4,3},{5,4},{6,5},{7,6},{8,7},{9,8},{10,... | collective-permute-start | bytes 245768 | tf_op jit(solution)/shard_map/ppermute | solution.py:424
  20.9 5.9 %collective-permute-start.5 = (f32[24,512]{1,0:T(8,128)S(1)}, f32[24,512]{1,0:T(8,128)S(1)}, u32[]{:S(2)}, u32[]{:S(2)}) collective-permute-start(f32[24,512]{1,0:T(8,128)S(1)} %pad_maximum_fusion.2), channel_id=1, source_target_pairs={{0,32},{8,40},{16,48},{24,56},{32,0},{40,8},{48,16},{56,24},{64,96... | collective-permute-start | bytes 147464 | tf_op jit(solution)/shard_map/ppermute | solution.py:420
  21.6 10.9 %collective-permute-start.8 = (bf16[384,256]{1,0:T(8,128)(2,1)S(1)}, bf16[384,256]{1,0:T(8,128)(2,1)S(1)}, u32[]{:S(2)}, u32[]{:S(2)}) collective-permute-start(bf16[384,256]{1,0:T(8,128)(2,1)S(1)} %select_bitcast_fusion.mine), channel_id=1, source_target_pairs={{0,24},{8,16},{16,8},{24,0},{32,56},{40,48},{48,40},{56,32},{64,88... | collective-permute-start | bytes 589832 | tf_op jit(solution)/shard_map/ppermute | solution.py:420
  26.8 7.3 %collective-permute-start.7 = (bf16[384,256]{1,0:T(8,128)(2,1)S(1)}, bf16[384,256]{1,0:T(8,128)(2,1)S(1)}, u32[]{:S(2)}, u32[]{:S(2)}) collective-permute-start(bf16[384,256]{1,0:T(8,128)(2,1)S(1)} %select_bitcast_fusion.mine), channel_id=1, source_target_pairs={{0,8},{8,0},{16,24},{24,16},{32,40},{40,32},{48,56},{56,48},{64,72... | collective-permute-start | bytes 589832 | tf_op jit(solution)/shard_map/ppermute | solution.py:420
  26.9 5.4 %collective-permute-start.6 = (f32[24,512]{1,0:T(8,128)S(1)}, f32[24,512]{1,0:T(8,128)S(1)}, u32[]{:S(2)}, u32[]{:S(2)}) collective-permute-start(f32[24,512]{1,0:T(8,128)S(1)} %fusion), channel_id=1, source_target_pairs={{0,96},{8,104},{16,112},{24,120},{32,64},{40,72},{48,80},{56,88},{... | collective-permute-start | bytes 147464 | tf_op jit(solution)/shard_map/ppermute | solution.py:420
  34.1 9.8 %collective-permute-start.11 = (bf16[384,256]{1,0:T(8,128)(2,1)S(1)}, bf16[384,256]{1,0:T(8,128)(2,1)S(1)}, u32[]{:S(2)}, u32[]{:S(2)}) collective-permute-start(bf16[384,256]{1,0:T(8,128)(2,1)S(1)} %collective-permute-done.8.across), channel_id=1, source_target_pairs={{0,8},{8,0},{16,24},{24,16},{32,40},{40,32},{48,56},{56,48},{64,72... | collective-permute-start | bytes 589832 | tf_op jit(solution)/shard_map/ppermute | solution.py:420
  34.4 5.3 %collective-permute-start.9 = (f32[24,512]{1,0:T(8,128)S(1)}, f32[24,512]{1,0:T(8,128)S(1)}, u32[]{:S(2)}, u32[]{:S(2)}) collective-permute-start(f32[24,512]{1,0:T(8,128)S(1)} %add.55), channel_id=1, source_target_pairs={{0,24},{8,16},{16,8},{24,0},{32,56},{40,48},{48,40},{56,32},{64,88... | collective-permute-start | bytes 147464 | tf_op jit(solution)/shard_map/ppermute | solution.py:420
  39.7 4.2 %collective-permute-start.10 = (f32[24,512]{1,0:T(8,128)S(1)}, f32[24,512]{1,0:T(8,128)S(1)}, u32[]{:S(2)}, u32[]{:S(2)}) collective-permute-start(f32[24,512]{1,0:T(8,128)S(1)} %add.56), channel_id=1, source_target_pairs={{0,8},{8,0},{16,24},{24,16},{32,40},{40,32},{48,56},{56,48},{64,72... | collective-permute-start | bytes 147464 | tf_op jit(solution)/shard_map/ppermute | solution.py:420
  43.9 21.1 %collective-permute-start.13 = (bf16[4,384,256]{2,1,0:T(8,128)(2,1)S(1)}, bf16[4,384,256]{2,1,0:T(8,128)(2,1)S(1)}, u32[]{:S(2)}, u32[]{:S(2)}) collective-permute-start(bf16[4,384,256]{2,1,0:T(8,128)(2,1)S(1)} %pad_maximum_fusion.here), channel_id=1, source_target_pairs={{0,24},{8,0},{16,8},{24,16},{32,56},{40,32},{48,40},{56,48},{64,88... | collective-permute-start | bytes 2359304 | tf_op jit(solution)/shard_map/ppermute | solution.py:416
  45.8 19.2 %collective-permute-start.12 = (bf16[4,384,256]{2,1,0:T(8,128)(2,1)S(1)}, bf16[4,384,256]{2,1,0:T(8,128)(2,1)S(1)}, u32[]{:S(2)}, u32[]{:S(2)}) collective-permute-start(bf16[4,384,256]{2,1,0:T(8,128)(2,1)S(1)} %pad_maximum_fusion.here), channel_id=1, source_target_pairs={{0,8},{8,16},{16,24},{24,0},{32,40},{40,48},{48,56},{56,32},{64,72... | collective-permute-start | bytes 2359304 | tf_op jit(solution)/shard_map/ppermute | solution.py:416
  46.0 19.0 %collective-permute-start.14 = (f32[12,512]{1,0:T(8,128)S(1)}, f32[12,512]{1,0:T(8,128)S(1)}, u32[]{:S(2)}, u32[]{:S(2)}) collective-permute-start(f32[12,512]{1,0:T(8,128)S(1)} %get-tuple-element.56), channel_id=1, source_target_pairs={{0,120},{1,121},{2,122},{3,123},{4,124},{5,125},{6,126},{7,127},{8... | collective-permute-start | bytes 73736 | tf_op jit(solution)/shard_map/ppermute | solution.py:424
  50.9 14.2 %collective-permute-start.15 = (f32[12,512]{1,0:T(8,128)S(1)}, f32[12,512]{1,0:T(8,128)S(1)}, u32[]{:S(2)}, u32[]{:S(2)}) collective-permute-start(f32[12,512]{1,0:T(8,128)S(1)} %get-tuple-element.57), channel_id=1, source_target_pairs={{0,64},{1,65},{2,66},{3,67},{4,68},{5,69},{6,70},{7,71},{8,72},{9,... | collective-permute-start | bytes 73736 | tf_op jit(solution)/shard_map/ppermute | solution.py:424
  65.1 9.0 %collective-permute-start.17 = (bf16[2,384,256]{2,1,0:T(8,128)(2,1)S(1)}, bf16[2,384,256]{2,1,0:T(8,128)(2,1)S(1)}, u32[]{:S(2)}, u32[]{:S(2)}) collective-permute-start(bf16[2,384,256]{2,1,0:T(8,128)(2,1)S(1)} %slice.55), channel_id=1, source_target_pairs={{0,24},{8,0},{16,8},{24,16},{32,56},{40,32},{48,40},{56,48},{64,88... | collective-permute-start | bytes 1179656 | tf_op jit(solution)/shard_map/ppermute | solution.py:416
  65.5 9.0 %collective-permute-start.16 = (bf16[2,384,256]{2,1,0:T(8,128)(2,1)S(1)}, bf16[2,384,256]{2,1,0:T(8,128)(2,1)S(1)}, u32[]{:S(2)}, u32[]{:S(2)}) collective-permute-start(bf16[2,384,256]{2,1,0:T(8,128)(2,1)S(1)} %slice.54), channel_id=1, source_target_pairs={{0,8},{8,16},{16,24},{24,0},{32,40},{40,48},{48,56},{56,32},{64,72... | collective-permute-start | bytes 1179656 | tf_op jit(solution)/shard_map/ppermute | solution.py:416
